TPU v7x, 32 devices: a whole 2x2x4 slice. The times are simulated.
32 devices in a mesh: leaf: 16 (over z, y, core), blk: 2 (over x).
Axes of the slice: x: 2, y: 2, z: 4, core: 2. Of those that a mesh axis runs over, the one named last changes fastest.
Arguments:
- leaf_rows: bfloat16 [32, 8, 512, 512], P('leaf', None, 'blk'), may hold values from -2 to 2
- leaf_weight: bfloat16 [32, 8, 512], P('leaf', None, 'blk'), may hold values from 0.25 to 4
- branching: int32 [32], P('leaf'), may hold values from 1 to 8, as said below
- sibling: int32 [16, 2], P('leaf'), may hold values from 0 to 1, each once within a row
- node_block: bfloat16 [512, 32, 512], P('blk', 'leaf'), may hold values from -6 to 6
- na_rows: bfloat16 [16384, 512], P(('leaf', 'blk')), may hold values from -3 to 3
- na_weight: bfloat16 [16384], P(('leaf', 'blk')), may hold values from 0.25 to 4
- na_route: int32 [16384, 1], P(('leaf', 'blk')), may hold values from 0 to 31; in each aligned block of 512 rows (0 to 511, 512 to 1023, ...) at most 24 rows name the same one
Outputs:
- node_schur: float32 [512, 32, 512], P('blk', 'leaf')
- merged: float32 [512, 32, 512], P('blk', 'leaf')
Inputs may be any that keep to these rules, and one draw needn't show every extreme that they name: `branching`: some node has exactly 8 children. `sibling`: each row is a permutation. `na_route`: within the rows of one device, no node is named by more than 24 rows, a bound that some block reaches.
All inputs are finite; a program needn't handle non-finite values.
Results may differ from a plain program's by a relative error of at most 0.0012.
Values may be sent and summed in bfloat16 or wider, within the bound.
No kernel may reach another device: no remote copies, remote signals or barrier semaphores. Data moves between devices by JAX's collectives and lax.ppermute only.
A program may use at most 64 MiB of HBM per device.

v0:
```python
import jax
import jax.numpy as jnp
from jax import lax
from jax.sharding import PartitionSpec as P


def from_partner(shard, axis, apart):
    return lax.ppermute(shard, axis, [(i, i ^ 1 << apart) for i in range(lax.axis_size(axis))])


def bucket_rows(route, rows, weight, total_nodes, capacity):
    count = route.shape[0]
    order = jnp.argsort(route, stable=True)
    sorted_route = route[order]
    first = jnp.searchsorted(sorted_route, sorted_route, side="left")
    position = jnp.arange(count, dtype=jnp.int32) - first
    slot = sorted_route * capacity + position
    width = rows.shape[1]
    filled = jnp.zeros((total_nodes * capacity, width), rows.dtype).at[slot].set(rows[order])
    weights = jnp.zeros((total_nodes * capacity,), weight.dtype).at[slot].set(weight[order])
    return (filled, weights)


def scale_rows(rows, weight, alive):
    factor = weight.astype(jnp.float32) * alive[:, :, None]
    return (rows.astype(jnp.float32) * factor[..., None]).astype(jnp.bfloat16)


def shards(leaf_rows, leaf_weight, branching, sibling, node_block, na_rows, na_weight, na_route):
    leaf_count = lax.axis_size("leaf")
    node_dev = leaf_rows.shape[0]
    most_children = leaf_rows.shape[1]
    state = leaf_rows.shape[3]
    na_dev = na_rows.shape[0]
    capacity = 3 * na_dev // (2 * leaf_count * node_dev)
    live = (jnp.arange(most_children, dtype=jnp.int32)[None, :] < branching[:, None]).astype(
        jnp.float32
    )
    filled, fill_weights = bucket_rows(
        na_route[:, 0], na_rows, na_weight, leaf_count * node_dev, capacity
    )
    got_rows, got_weights = (
        lax.all_to_all(
            filled.reshape(leaf_count, node_dev * capacity, state),
            "leaf",
            split_axis=0,
            concat_axis=0,
            tiled=True,
        ),
        lax.all_to_all(
            fill_weights.reshape(leaf_count, node_dev * capacity),
            "leaf",
            split_axis=0,
            concat_axis=0,
            tiled=True,
        ),
    )
    got_scaled = (got_rows.astype(jnp.float32) * got_weights.astype(jnp.float32)[..., None]).astype(
        jnp.bfloat16
    )
    got_scaled = got_scaled.reshape(leaf_count, node_dev, capacity, state)
    got_plain = got_rows.reshape(leaf_count, node_dev, capacity, state)
    scaled_leaf = scale_rows(leaf_rows, leaf_weight, live)
    sliced = scaled_leaf
    leaf_part = lax.psum_scatter(
        jnp.einsum("nbks,nbkt->snt", sliced, leaf_rows, preferred_element_type=jnp.float32),
        "blk",
        scatter_dimension=0,
        tiled=True,
    )
    sliced = got_scaled
    routed_part = lax.psum_scatter(
        jnp.einsum("incs,inct->snt", sliced, got_plain, preferred_element_type=jnp.float32),
        "blk",
        scatter_dimension=0,
        tiled=True,
    )
    total = leaf_part + routed_part
    node_schur = total + node_block.astype(jnp.float32)
    partner = from_partner(node_schur, "leaf", 0)
    matches = sibling[0][:, None] == jnp.arange(node_dev, dtype=jnp.int32)[None, :]
    picked = jnp.sum(jnp.where(matches[None, :, :, None], partner[:, None, :, :], 0.0), axis=2)
    merged = node_schur + picked
    return (node_schur, merged)


def solution(mesh):
    return jax.shard_map(
        shards,
        mesh=mesh,
        in_specs=(
            P("leaf", None, "blk", None),
            P("leaf", None, "blk"),
            P("leaf"),
            P("leaf", None),
            P("blk", "leaf", None),
            P(("leaf", "blk"), None),
            P(("leaf", "blk")),
            P(("leaf", "blk"), None),
        ),
        out_specs=(P("blk", "leaf", None), P("blk", "leaf", None)),
        check_vma=False,
    )
```

profile of v0, /device:TPU:9, one launch (start us, length us, event | category | flops | bytes accessed | tf_op | source)
XLA Modules:
  0.0 144.3 jit_solution(7570440120294963030)
XLA Ops:
  7.2 0.0 copy-start
  7.2 4.5 %sort.17 = (s32[512]{0:T(512)}, s32[512]{0:T(512)S(1)}) sort(s32[512]{0:T(512)} %bitcast.18, s32[512]{0:T(512)S(1)} %iota.22), dimensions={0}, to_apply=%region_1.2 | sort | flops 4608 | bytes 8192 | tf_op jit(solution)/shard_map/jit(argsort)/sort | solution.py:13
  11.7 3.6 %gather_fusion.1 = s32[512]{0:T(512)S(1)} fusion(s32[512]{0:T(512)} %bitcast.19, s32[1024]{0:T(1024)S(1)} %pad_clamp_fusion.1), kind=kCustom, calls=%fused_computation.1 | custom fusion | bytes 6144 | tf_op jit(solution)/shard_map/gather | solution.py:14
  15.3 0.0 copy-start.1
  15.3 36.1 %while.25 = (s32[]{:T(128)}, u32[512]{0:T(512)S(1)}, u32[512]{0:T(512)S(1)}, s32[512]{0:T(512)S(1)}, s32[]{:T(128)}, /*index=5*/s32[]{:T(128)}, s32[]{}) while((s32[]{:T(128)}, u32[512]{0:T(512)S(1)}, u32[512]{0:T(512)S(1)}, s32[512]{0:T(512)S(1)}, s32[]{:T(128)}, /*index=5*/s32[]{:T(128)}, s32[]{}) %tuple.45), condition=%wide.region_3.4_spmd.clone, body=%wide.region_2.3_spmd.clone.sunk | while | flops 10244 | bytes 40037 | solution.py:15
  15.4 3.5 %gather_fusion = s32[512]{0:T(512)S(1)} fusion(s32[512]{0:T(512)S(1)} %get-tuple-element.153, u32[1024]{0:T(1024)S(1)} %pad_clamp_fusion.3), kind=kCustom, calls=%fused_computation.clone.clone.1 | custom fusion | bytes 6144 | tf_op jit(solution)/shard_map/jit(searchsorted)/jit(_searchsorted_scan_impl)/vmap(jit(_searchsorted_scan_impl))/while/body/eval_jaxpr/gather | solution.py:15
  19.0 3.5 %gather_fusion = s32[512]{0:T(512)S(1)} fusion(s32[512]{0:T(512)S(1)} %get-tuple-element.153, u32[1024]{0:T(1024)S(1)} %pad_clamp_fusion.3), kind=kCustom, calls=%fused_computation.clone.clone.1 | custom fusion | bytes 6144 | tf_op jit(solution)/shard_map/jit(searchsorted)/jit(_searchsorted_scan_impl)/vmap(jit(_searchsorted_scan_impl))/while/body/eval_jaxpr/gather | solution.py:15
  22.6 3.5 %gather_fusion = s32[512]{0:T(512)S(1)} fusion(s32[512]{0:T(512)S(1)} %get-tuple-element.153, u32[1024]{0:T(1024)S(1)} %pad_clamp_fusion.3), kind=kCustom, calls=%fused_computation.clone.clone.1 | custom fusion | bytes 6144 | tf_op jit(solution)/shard_map/jit(searchsorted)/jit(_searchsorted_scan_impl)/vmap(jit(_searchsorted_scan_impl))/while/body/eval_jaxpr/gather | solution.py:15
  26.2 3.5 %gather_fusion = s32[512]{0:T(512)S(1)} fusion(s32[512]{0:T(512)S(1)} %get-tuple-element.153, u32[1024]{0:T(1024)S(1)} %pad_clamp_fusion.3), kind=kCustom, calls=%fused_computation.clone.clone.1 | custom fusion | bytes 6144 | tf_op jit(solution)/shard_map/jit(searchsorted)/jit(_searchsorted_scan_impl)/vmap(jit(_searchsorted_scan_impl))/while/body/eval_jaxpr/gather | solution.py:15
  29.8 3.5 %gather_fusion = s32[512]{0:T(512)S(1)} fusion(s32[512]{0:T(512)S(1)} %get-tuple-element.153, u32[1024]{0:T(1024)S(1)} %pad_clamp_fusion.3), kind=kCustom, calls=%fused_computation.clone.clone.1 | custom fusion | bytes 6144 | tf_op jit(solution)/shard_map/jit(searchsorted)/jit(_searchsorted_scan_impl)/vmap(jit(_searchsorted_scan_impl))/while/body/eval_jaxpr/gather | solution.py:15
  33.4 3.5 %gather_fusion = s32[512]{0:T(512)S(1)} fusion(s32[512]{0:T(512)S(1)} %get-tuple-element.153, u32[1024]{0:T(1024)S(1)} %pad_clamp_fusion.3), kind=kCustom, calls=%fused_computation.clone.clone.1 | custom fusion | bytes 6144 | tf_op jit(solution)/shard_map/jit(searchsorted)/jit(_searchsorted_scan_impl)/vmap(jit(_searchsorted_scan_impl))/while/body/eval_jaxpr/gather | solution.py:15
  37.0 3.5 %gather_fusion = s32[512]{0:T(512)S(1)} fusion(s32[512]{0:T(512)S(1)} %get-tuple-element.153, u32[1024]{0:T(1024)S(1)} %pad_clamp_fusion.3), kind=kCustom, calls=%fused_computation.clone.clone.1 | custom fusion | bytes 6144 | tf_op jit(solution)/shard_map/jit(searchsorted)/jit(_searchsorted_scan_impl)/vmap(jit(_searchsorted_scan_impl))/while/body/eval_jaxpr/gather | solution.py:15
  40.6 3.5 %gather_fusion = s32[512]{0:T(512)S(1)} fusion(s32[512]{0:T(512)S(1)} %get-tuple-element.153, u32[1024]{0:T(1024)S(1)} %pad_clamp_fusion.3), kind=kCustom, calls=%fused_computation.clone.clone.1 | custom fusion | bytes 6144 | tf_op jit(solution)/shard_map/jit(searchsorted)/jit(_searchsorted_scan_impl)/vmap(jit(_searchsorted_scan_impl))/while/body/eval_jaxpr/gather | solution.py:15
  44.3 3.5 %gather_fusion = s32[512]{0:T(512)S(1)} fusion(s32[512]{0:T(512)S(1)} %get-tuple-element.153, u32[1024]{0:T(1024)S(1)} %pad_clamp_fusion.3), kind=kCustom, calls=%fused_computation.clone.clone.1 | custom fusion | bytes 6144 | tf_op jit(solution)/shard_map/jit(searchsorted)/jit(_searchsorted_scan_impl)/vmap(jit(_searchsorted_scan_impl))/while/body/eval_jaxpr/gather | solution.py:15
  47.9 3.5 %gather_fusion = s32[512]{0:T(512)S(1)} fusion(s32[512]{0:T(512)S(1)} %get-tuple-element.153, u32[1024]{0:T(1024)S(1)} %pad_clamp_fusion.3), kind=kCustom, calls=%fused_computation.clone.clone.1 | custom fusion | bytes 6144 | tf_op jit(solution)/shard_map/jit(searchsorted)/jit(_searchsorted_scan_impl)/vmap(jit(_searchsorted_scan_impl))/while/body/eval_jaxpr/gather | solution.py:15
  51.4 0.0 copy-start.4
  51.5 0.0 copy-start.3
  51.5 0.0 copy-done.1
  51.5 3.5 %gather_fusion.2 = bf16[512]{0:T(512)(128)(2,1)S(1)} fusion(bf16[512]{0:T(512)(128)(2,1)S(1)} %copy-done.1, s32[1024]{0:T(1024)S(1)} %pad_clamp_fusion.1), kind=kCustom, calls=%fused_computation.3 | custom fusion | bytes 4096 | tf_op jit(solution)/shard_map/gather | solution.py:20
  55.0 3.8 %scatter_custom_fusion.1 = bf16[768]{0:T(1024)(128)(2,1)S(1)} fusion(s32[512]{0:T(512)S(1)} %compare_select_fusion, bf16[512]{0:T(512)(128)(2,1)S(1)} %gather_fusion.2, bf16[]{:T(256)} %constant.38.clone.1), kind=kCustom, calls=%fused_computation.26 | custom fusion | bytes 1538 | tf_op jit(solution)/shard_map/scatter | solution.py:20
  58.8 0.7 all_to_all.12
  59.5 6.6 %all-to-all-start.1 = ((bf16[16,1,48]{2,1,0:T(2,128)(2,1)}), bf16[16,1,48]{2,1,0:T(2,128)(2,1)S(1)}, u32[]{:S(2)}, u32[]{:S(2)}) async-start(bf16[16,1,48]{2,1,0:T(2,128)(2,1)} %all_to_all.12), calls=%async_computation.1 | async-start | bytes 16384 | tf_op jit(solution)/shard_map/all_to_all | solution.py:50
  66.1 0.0 copy-done
  66.1 5.6 %scatter_custom_fusion = bf16[768,512]{1,0:T(8,128)(2,1)} fusion(s32[512]{0:T(512)S(1)} %compare_select_fusion, bf16[512,512]{1,0:T(8,128)(2,1)S(1)} %copy-done, s32[1024]{0:T(1024)S(1)} %pad_clamp_fusion.1, bf16[]{:T(256)} %constant.38.clone.1), kind=kCustom, calls=%fused_computation.17 | custom fusion | bytes 786434 | tf_op jit(solution)/shard_map/scatter | solution.py:19
  71.7 0.0 all-to-all-done.1
  71.7 6.0 %all-to-all-start = ((bf16[16,48,512]{2,1,0:T(8,128)(2,1)}), bf16[16,48,512]{2,1,0:T(8,128)(2,1)S(1)}, u32[]{:S(2)}, u32[]{:S(2)}) async-start(bf16[16,48,512]{2,1,0:T(8,128)(2,1)} %bitcast.4), calls=%async_computation | async-start | bytes 1572864 | tf_op jit(solution)/shard_map/all_to_all | solution.py:43
  77.7 0.2 reduce-scatter.2.cloned.1.call-start
  78.0 0.0 copy-done.4
  78.0 0.1 compare_convert_fusion
  78.0 0.0 copy-done.3
  78.1 0.1 convert_multiply_fusion
  78.1 6.6 %fusion = f32[2,512,512,1]{2,1,3,0:T(8,128)S(1)} fusion(bf16[2,8,256,512]{3,2,1,0:T(8,128)(2,1)} %param.10, f32[2,8,256]{2,1,0:T(8,128)S(1)} %convert_multiply_fusion), kind=kOutput, calls=%fused_computation.11 | convolution fusion | flops 2153775104 | bytes 6307840 | tf_op jit(solution)/shard_map/nbks,nbkt->snt/dot_general | solution.py:66
  84.7 12.6 %all-to-all-done = bf16[16,48,512]{2,1,0:T(8,128)(2,1)S(1)} async-done(((bf16[16,48,512]{2,1,0:T(8,128)(2,1)}), bf16[16,48,512]{2,1,0:T(8,128)(2,1)S(1)}, u32[]{:S(2)}, u32[]{:S(2)}) %all-to-all-start) | async-done | bytes 786464 | tf_op jit(solution)/shard_map/all_to_all | solution.py:43
  97.3 0.2 multiply_convert_fusion.2
  97.5 2.1 %bitcast_add_fusion = f32[512,2,512]{2,0,1:T(8,128)} fusion(f32[2,512,512,1]{2,1,3,0:T(8,128)S(1)} %fusion, bf16[16,2,24,512]{3,2,1,0:T(8,128)(2,1)S(1)} %bitcast.20, bf16[16,2,24,512]{3,2,1,0:T(8,128)(2,1)S(1)} %bitcast.21), kind=kOutput, calls=%fused_computation.13 | convolution fusion | flops 403177472 | bytes 5767168 | tf_op jit(solution)/shard_map/incs,inct->snt/dot_general | solution.py:73
  99.7 0.0 copy-start.2
  99.7 0.0 reduce-scatter.2.cloned.1.call-update
  99.7 31.2 %reduce-scatter.2.cloned.1.call-done = f32[256,2,512]{2,0,1:T(8,128)} async-done(((f32[512,2,512]{2,0,1:T(8,128)}), f32[256,2,512]{2,0,1:T(8,128)}) %reduce-scatter.2.cloned.1.call-update) | async-done | bytes 1048592 | tf_op jit(solution)/shard_map/reduce_scatter | solution.py:65
  130.8 0.0 copy-done.2
  130.8 1.4 convert_add_fusion
  132.2 0.7 collective-permute-start
  133.0 0.0 copy-done.5
  133.0 0.1 iota_compare_fusion
  133.0 1.8 %copy.41 = f32[256,2,512]{2,1,0:T(2,128)} copy(f32[256,2,512]{2,0,1:T(8,128)S(1)} %convert_add_fusion) | data formatting | bytes 2097152
  134.8 0.4 collective-permute-done
  135.2 0.2 select_reduce_fusion
  135.5 0.2 add.44
  135.7 1.8 %copy.42 = f32[256,2,512]{2,1,0:T(2,128)} copy(f32[256,2,512]{2,0,1:T(8,128)S(1)} %add.44) | data formatting | bytes 2097152
  (58 shorter events, 0.5 us)
Async XLA Ops:
  7.2 58.9 %copy-start = (bf16[512,512]{1,0:T(8,128)(2,1)S(1)}, bf16[512,512]{1,0:T(8,128)(2,1)}, u32[]{:S(2)}) copy-start(bf16[512,512]{1,0:T(8,128)(2,1)} %param.15) | copy-start | bytes 1572868
  15.3 36.1 %copy-start.1 = (bf16[512]{0:T(512)(128)(2,1)S(1)}, bf16[512]{0:T(512)(128)(2,1)}, u32[]{:S(2)}) copy-start(bf16[512]{0:T(512)(128)(2,1)} %param.16) | copy-start | bytes 3076
  51.4 26.5 %copy-start.4 = (s32[2]{0:T(128)S(1)}, s32[2]{0:T(128)}, u32[]{:S(2)}) copy-start(s32[2]{0:T(128)} %param.12) | copy-start | bytes 28
  51.5 26.6 %copy-start.3 = (bf16[2,8,256]{2,1,0:T(8,128)(2,1)S(1)}, bf16[2,8,256]{2,1,0:T(8,128)(2,1)}, u32[]{:S(2)}) copy-start(bf16[2,8,256]{2,1,0:T(8,128)(2,1)} %param.11) | copy-start | bytes 24580
  59.5 12.2 %all-to-all-start.1 = ((bf16[16,1,48]{2,1,0:T(2,128)(2,1)}), bf16[16,1,48]{2,1,0:T(2,128)(2,1)S(1)}, u32[]{:S(2)}, u32[]{:S(2)}) async-start(bf16[16,1,48]{2,1,0:T(2,128)(2,1)} %all_to_all.12), calls=%async_computation.1 | async-start | bytes 16384 | tf_op jit(solution)/shard_map/all_to_all | solution.py:50
  71.7 25.6 %all-to-all-start = ((bf16[16,48,512]{2,1,0:T(8,128)(2,1)}), bf16[16,48,512]{2,1,0:T(8,128)(2,1)S(1)}, u32[]{:S(2)}, u32[]{:S(2)}) async-start(bf16[16,48,512]{2,1,0:T(8,128)(2,1)} %bitcast.4), calls=%async_computation | async-start | bytes 1572864 | tf_op jit(solution)/shard_map/all_to_all | solution.py:43
  77.7 53.1 %reduce-scatter.2.cloned.1.call-start = ((), (), s32[]{:S(2)}) async-start(), calls=%async_computation.3 | async-start | bytes 3145728 | tf_op jit(solution)/shard_map/reduce_scatter | solution.py:65
  99.7 31.2 %copy-start.2 = (bf16[256,2,512]{2,1,0:T(2,128)(2,1)S(1)}, bf16[256,2,512]{2,1,0:T(2,128)(2,1)}, u32[]{:S(2)}) copy-start(bf16[256,2,512]{2,1,0:T(2,128)(2,1)} %param.14) | copy-start | bytes 1572868
  99.7 33.3 %copy-start.5 = (s32[1,2]{1,0:T(1,128)S(1)}, s32[1,2]{1,0:T(1,128)}, u32[]{:S(2)}) copy-start(s32[1,2]{1,0:T(1,128)} %param.13) | copy-start | bytes 28
  132.2 3.0 %collective-permute-start = (f32[256,2,512]{2,0,1:T(8,128)S(1)}, f32[256,2,512]{2,0,1:T(8,128)S(1)}, u32[]{:S(2)}, u32[]{:S(2)}) collective-permute-start(f32[256,2,512]{2,0,1:T(8,128)S(1)} %convert_add_fusion), channel_id=1, source_target_pairs={{0,2},{2,0},{4,6},{6,4},{8,10},{10,8},{12,14},{14,12},{16,18},{18,... | collective-permute-start | bytes 3145736 | tf_op jit(solution)/shard_map/ppermute | solution.py:8
Sparse Core Ops, SparseCore 0:
  99.8 30.9 reduce-scatter.1
where the time goes:
time: 146 us; the launch traced here: 144 us
  local copies, waits for them, and re-layouts  56 us (38%)
  waiting for transfers between devices  44.2 us (30%)
  between operations  14.2 us (10%)
  starting transfers between devices  13.6 us (9%)
  matrix products  8.67 us (6%)
  other arithmetic  7.19 us (5%)
    gather x10, local copies, waits for them, and re-layouts, bucket_rows(): first = jnp.searchsorted(sorted_route, sorted_route, side='left')  35.1 us
    reduce_scatter x1, waiting for transfers between devices, shards(): lax.psum_scatter(jnp.einsum('nbks,nbkt->snt', sliced, leaf_rows, preferre...  31.2 us
    all_to_all x1, waiting for transfers between devices, shards(): lax.all_to_all(filled.reshape(leaf_count, node_dev * capacity, state), 'l...  12.6 us
    all_to_all x1, starting transfers between devices, shards(): lax.all_to_all(fill_weights.reshape(leaf_count, node_dev * capacity), 'le...  6.61 us
    dot_general x1, matrix products, shards(): jnp.einsum('nbks,nbkt->snt', sliced, leaf_rows, preferred_element_type=jn...  6.56 us
    all_to_all x1, starting transfers between devices, shards(): lax.all_to_all(filled.reshape(leaf_count, node_dev * capacity, state), 'l...  6.02 us
    scatter x1, local copies, waits for them, and re-layouts, bucket_rows(): jnp.zeros((total_nodes * capacity, width), rows.dtype).at[slot]  5.63 us
    sort x1, other arithmetic, bucket_rows(): order = jnp.argsort(route, stable=True)  4.5 us
  transfers between devices with their start and end apart: 4, of which 3 were waited for; matrix products, arithmetic and copies ran while one was open for 10% of the time, Pallas kernels for 0%

commit v1 on v0

v1 whole, which is shorter than its diff:
```python
import functools

import jax
import jax.numpy as jnp
from jax import lax
from jax.experimental import pallas as pl
from jax.experimental.pallas import tpu as pltpu
from jax.sharding import PartitionSpec as P

F32 = jnp.float32
BF16 = jnp.bfloat16
I32 = jnp.int32
LANES = 128
GROUP = 16
VMEM = pl.BlockSpec(memory_space=pltpu.VMEM)
SMEM = pl.BlockSpec(memory_space=pltpu.SMEM)
CODE = 32000.0


class Plan:
    def __init__(self, leaf_count, node_dev, capacity, state):
        self.leaf_count, self.node_dev, self.capacity, self.state = leaf_count, node_dev, capacity, state
        self.full = capacity // GROUP * GROUP
        self.rest = capacity - self.full
        self.rows = -(-node_dev * capacity // GROUP) * GROUP
        self.groups = self.rows // GROUP
        self.slabs = state // LANES
        self.block = self.slabs * self.rows + GROUP
        self.groups_of = [
            [g for g in range(self.groups) if q in {self.node_at(g * GROUP + i) for i in range(GROUP)}]
            for q in range(node_dev)
        ]
        self.depth = [leaf_count * GROUP * len(g) for g in self.groups_of]

    def node_at(self, row):
        if row < self.node_dev * self.full:
            return row // self.full
        return min((row - self.node_dev * self.full) // self.rest, self.node_dev - 1) if self.rest else 0


def dot_t(a, b):
    return lax.dot_general(a, b, (((0,), (0,)), ((), ())), preferred_element_type=F32)


def bucket_kernel(plan, route_ref, weight_ref, rows_ref, out_ref):
    count = rows_ref.shape[0]
    nodes = plan.leaf_count * plan.node_dev
    route = route_ref[...]
    member = lax.broadcasted_iota(I32, (nodes, count), 0) == route
    before = (
        lax.broadcasted_iota(I32, (count, count), 0) < lax.broadcasted_iota(I32, (count, count), 1)
    ).astype(BF16)
    seen = jnp.dot(member.astype(BF16), before, preferred_element_type=F32)
    position = jnp.sum(jnp.where(member, seen, 0.0), axis=0, keepdims=True).astype(I32)
    owner = route // plan.node_dev
    q = route - owner * plan.node_dev
    slot = owner * plan.rows + jnp.where(
        position < plan.full,
        q * plan.full + position,
        plan.node_dev * plan.full + q * plan.rest + position - plan.full,
    )
    total = plan.leaf_count * plan.rows
    hit = lax.broadcasted_iota(I32, (total, count), 0) == slot
    filled = jnp.dot(
        jnp.where(hit, 1.0, 0.0).astype(BF16), rows_ref[...], preferred_element_type=F32
    ).astype(BF16)
    weights = jnp.dot(
        jnp.where(hit, weight_ref[...].astype(F32), 0.0).astype(BF16),
        jnp.ones((count, LANES), BF16),
        preferred_element_type=F32,
    )
    lane = lax.broadcasted_iota(I32, (GROUP, LANES), 1)
    sub = lax.broadcasted_iota(I32, (GROUP, LANES), 0)
    want = []
    for g in range(plan.groups):
        q_of = jnp.zeros((GROUP, LANES), I32)
        for i in range(1, GROUP):
            step = plan.node_at(g * GROUP + i) - plan.node_at(g * GROUP + i - 1)
            if step:
                q_of = q_of + jnp.where(sub >= i, step, 0)
        want.append(lane == g * plan.node_dev + plan.node_at(g * GROUP) + q_of)
    for d in range(plan.leaf_count):
        at = d * plan.rows
        for c in range(plan.slabs):
            out_ref[d, c * plan.rows : (c + 1) * plan.rows, :] = filled[
                at : at + plan.rows, c * LANES : (c + 1) * LANES
            ]
        extra = jnp.zeros((GROUP, LANES), F32)
        for g in range(plan.groups):
            extra = jnp.where(want[g], weights[at + g * GROUP : at + (g + 1) * GROUP, :], extra)
        out_ref[d, plan.slabs * plan.rows :, :] = extra.astype(BF16)


def leaf_kernel(place_ref, branching_ref, weight_ref, rows_ref, block_ref, own_ref, send_ref, total):
    n = pl.program_id(0)
    share = own_ref.shape[1]
    peers = send_ref.shape[0]
    blk = place_ref[0]
    columns = jnp.transpose(weight_ref[0].astype(F32))
    total[...] = jnp.zeros_like(total)
    for b in range(rows_ref.shape[1]):

        @pl.when(b < branching_ref[n])
        def _():
            rows = rows_ref[0, b]
            scaled = (rows.astype(F32) * columns[:, b : b + 1]).astype(BF16)
            total[...] += dot_t(scaled, rows)

    own_ref[0] = total[pl.ds(pl.multiple_of(blk * share, share), share), :] + block_ref[0].astype(F32)
    for e in range(1, peers + 1):
        at = pl.multiple_of((blk ^ e) * share, share)
        send_ref[e - 1, 0] = total[pl.ds(at, share), :]


def send_kernel(plan, place_ref, got_ref, part_ref, code_ref, plain_ref, scaled_ref, total=None):
    blk = place_ref[0]
    peers, _, share, state = part_ref.shape
    for d in range(plan.leaf_count):
        extra = got_ref[d, plan.slabs * plan.rows :, :].astype(F32)
        for g in range(plan.groups):
            rows = jnp.concatenate(
                [
                    got_ref[d, c * plan.rows + g * GROUP : c * plan.rows + (g + 1) * GROUP, :]
                    for c in range(plan.slabs)
                ],
                axis=1,
            )
            wide = rows.astype(F32)
            for q in range(plan.node_dev):
                if g not in plan.groups_of[q]:
                    continue
                at = (plan.groups_of[q].index(g) * plan.leaf_count + d) * GROUP
                j = g * plan.node_dev + q
                plain_ref[q, at : at + GROUP, :] = rows
                scaled_ref[q, at : at + GROUP, :] = (wide * extra[:, j : j + 1]).astype(BF16)
    for q in range(plan.node_dev):
        product = Product(scaled_ref.at[q], plain_ref.at[q], total)
        for e in range(1, peers + 1):
            at = pl.multiple_of((blk ^ e) * share, share)
            encode(part_ref[e - 1, q] + product.rows(at, share), code_ref.at[e - 1], q, share)


class Product:
    def __init__(self, scaled_ref, plain_ref, total):
        self.scaled_ref, self.plain_ref, self.total = scaled_ref, plain_ref, total
        if total is not None:
            total[...] = dot_t(scaled_ref[...], plain_ref[...])

    def rows(self, at, share):
        if self.total is not None:
            return self.total[pl.ds(at, share), :]
        return dot_t(self.scaled_ref[:, pl.ds(at, share)], self.plain_ref[...])


def encode(value, code_ref, q, share):
    state = value.shape[1]
    most = jnp.max(jnp.abs(value), axis=1, keepdims=True)
    power = jnp.ceil(jnp.log2(jnp.maximum(most, 1e-30)))
    code_ref[q * share : (q + 1) * share, :] = (
        jnp.round(value * (CODE * jnp.exp2(-power))).astype(I32).astype(jnp.int16)
    )
    width = min(share, LANES)
    eye = lax.broadcasted_iota(I32, (width, LANES), 0) == lax.broadcasted_iota(I32, (width, LANES), 1)
    parts = []
    for k in range(0, share, width):
        parts.append(jnp.sum(jnp.where(eye, power[k : k + width], 0.0), axis=0, keepdims=True))
    line = jnp.concatenate(parts + [jnp.zeros((1, state - LANES * len(parts)), F32)], axis=1)
    line = jnp.broadcast_to(line, (GROUP, state)).astype(I32).astype(jnp.int16)
    base = code_ref.shape[0] - GROUP * (code_ref.shape[0] // share - q)
    code_ref[base : base + GROUP, :] = line


def decode(code_ref, q, share):
    base = code_ref.shape[0] - GROUP * (code_ref.shape[0] // share - q)
    line = code_ref[base : base + GROUP, :].astype(I32).astype(F32)[0:1, :]
    width = min(share, LANES)
    eye = lax.broadcasted_iota(I32, (width, LANES), 0) == lax.broadcasted_iota(I32, (width, LANES), 1)
    parts = []
    for k in range(share // width):
        one = line[:, k * LANES : (k + 1) * LANES]
        parts.append(jnp.sum(jnp.where(eye, one, 0.0), axis=1, keepdims=True))
    power = jnp.concatenate(parts, axis=0)
    value = code_ref[q * share : (q + 1) * share, :].astype(I32).astype(F32)
    return value * (jnp.exp2(power) * (1.0 / CODE))


def own_kernel(place_ref, part_ref, plain_ref, scaled_ref, own_ref, total=None):
    nodes, share, _ = part_ref.shape
    at = pl.multiple_of(place_ref[0] * share, share)
    for q in range(nodes):
        own_ref[q] = part_ref[q] + Product(scaled_ref.at[q], plain_ref.at[q], total).rows(at, share)


def node_kernel(own_ref, code_ref, out_ref, node_ref):
    nodes, share, _ = own_ref.shape
    for q in range(nodes):
        value = own_ref[q]
        for e in range(code_ref.shape[0]):
            value = value + decode(code_ref.at[e], q, share)
        node_ref[q] = value
        out_ref[:, q, :] = value


def merge_kernel(sibling_ref, node_ref, partner_ref, out_ref):
    for q in range(node_ref.shape[0]):
        out_ref[:, q, :] = node_ref[q] + partner_ref[sibling_ref[0, q]]


def call(kernel, out_shape, in_specs, flops=0, moved=1 << 20, **more):
    outs = jax.tree.map(lambda _: VMEM, out_shape)
    more.setdefault("out_specs", outs)
    return pl.pallas_call(
        kernel,
        out_shape=out_shape,
        in_specs=in_specs,
        compiler_params=pltpu.CompilerParams(vmem_limit_bytes=32 << 20),
        cost_estimate=pl.CostEstimate(flops=flops, bytes_accessed=moved, transcendentals=0),
        **more,
    )


def shards(leaf_rows, leaf_weight, branching, sibling, node_block, na_rows, na_weight, na_route):
    leaf_count, blk_count = lax.axis_size("leaf"), lax.axis_size("blk")
    node_dev, most_children, depth, state = leaf_rows.shape
    count = na_rows.shape[0]
    share = state // blk_count
    peers = blk_count - 1
    plan = Plan(leaf_count, node_dev, 3 * count // (2 * leaf_count * node_dev), state)
    place = lax.axis_index("blk").astype(I32).reshape(1)
    whole = [pltpu.VMEM((state, state), F32)] if share % LANES else []
    shape = jax.ShapeDtypeStruct

    with jax.named_scope("bucket"):
        blocks = call(
            functools.partial(bucket_kernel, plan),
            shape((leaf_count, plan.block, LANES), BF16),
            [VMEM, VMEM, VMEM],
            flops=2 * plan.leaf_count * plan.rows * count * state,
        )(na_route.reshape(1, count), na_weight.reshape(1, count), na_rows)
    got = lax.all_to_all(blocks, "leaf", split_axis=0, concat_axis=0, tiled=True)

    with jax.named_scope("leaf_products"):
        own_part, send_part = call(
            leaf_kernel,
            (shape((node_dev, share, state), F32), shape((peers, node_dev, share, state), F32)),
            [
                SMEM,
                SMEM,
                pl.BlockSpec((1, most_children, depth), lambda n: (n, 0, 0)),
                pl.BlockSpec((1, most_children, depth, state), lambda n: (n, 0, 0, 0)),
                pl.BlockSpec((1, share, state), lambda n: (n, 0, 0)),
            ],
            out_specs=(
                pl.BlockSpec((1, share, state), lambda n: (n, 0, 0)),
                pl.BlockSpec((peers, 1, share, state), lambda n: (0, n, 0, 0)),
            ),
            grid=(node_dev,),
            scratch_shapes=[pltpu.VMEM((state, state), F32)],
            flops=2 * node_dev * most_children * depth * state * state,
            moved=8 << 20,
        )(place, branching, leaf_weight, leaf_rows, jnp.transpose(node_block, (1, 0, 2)))

    with jax.named_scope("routed_send"):
        code, plain, scaled = call(
            functools.partial(send_kernel, plan),
            (
                shape((peers, node_dev * (share + GROUP), state), jnp.int16),
                shape((node_dev, max(plan.depth), state), BF16),
                shape((node_dev, max(plan.depth), state), BF16),
            ),
            [SMEM, VMEM, VMEM],
            scratch_shapes=whole,
            flops=2 * node_dev * max(plan.depth) * state * state,
        )(place, got, send_part)
    received = [
        lax.ppermute(code[e - 1], "blk", [(i, i ^ e) for i in range(blk_count)])
        for e in range(1, blk_count)
    ]
    with jax.named_scope("routed_own"):
        own = call(
            own_kernel,
            shape((node_dev, share, state), F32),
            [SMEM, VMEM, VMEM, VMEM],
            scratch_shapes=whole,
            flops=2 * node_dev * max(plan.depth) * share * state,
        )(place, own_part, plain, scaled)
    with jax.named_scope("node"):
        node_schur, node = call(
            node_kernel,
            (shape((share, node_dev, state), F32), shape((node_dev, share, state), F32)),
            [VMEM, VMEM],
        )(own, jnp.stack(received) if peers > 1 else received[0][None])
    partner = lax.ppermute(node, "leaf", [(i, i ^ 1) for i in range(leaf_count)])
    with jax.named_scope("merge"):
        merged = call(
            merge_kernel, shape((share, node_dev, state), F32), [SMEM, VMEM, VMEM]
        )(sibling, node, partner)
    return (node_schur, merged)


def solution(mesh):
    return jax.shard_map(
        shards,
        mesh=mesh,
        in_specs=(
            P("leaf", None, "blk", None),
            P("leaf", None, "blk"),
            P("leaf"),
            P("leaf", None),
            P("blk", "leaf", None),
            P(("leaf", "blk"), None),
            P(("leaf", "blk")),
            P(("leaf", "blk"), None),
        ),
        out_specs=(P("blk", "leaf", None), P("blk", "leaf", None)),
        check_vma=False,
    )
```

time: 146 us -> 54.4 us (0.37)
  local copies, waits for them, and re-layouts: 56 us -> 5.7 us
  waiting for transfers between devices: 44.2 us -> 27.5 us
  between operations: 14.2 us -> 0.7 us
  Pallas kernels: 0 us -> 11.6 us
  matrix products: 8.67 us -> 0 us
  other arithmetic: 7.19 us -> 0 us
  starting transfers between devices: 13.6 us -> 8.48 us
    gather x12 -> x0, local copies, waits for them, and re-layouts: 42.3 us -> none  [the longest x10 35.1 us: bucket_rows(): first = jnp.searchsorted(sorted_route, sorted_route, side='left')]
    reduce_scatter x1 -> x0, waiting for transfers between devices: 31.2 us -> none  [shards(): lax.psum_scatter(jnp.einsum('nbks,nbkt->snt', sliced, leaf_rows, preferre...]
    ppermute x1 -> x2, waiting for transfers between devices: 0.43 us -> 15 us  [the longest x1 12.8 us: shards(): lax.ppermute(code[e - 1], 'blk', [(i, i ^ e) for i in range(blk_count)])]
    pallas_call x0 -> x6, Pallas kernels: none -> 11.6 us  [the longest x1 5.1 us: shards(): call(leaf_kernel, (shape((node_dev, share, state), F32), shape((peers, no...]
    scatter x2 -> x0, local copies, waits for them, and re-layouts: 9.4 us -> none  [the longest x1 5.63 us: bucket_rows(): jnp.zeros((total_nodes * capacity, width), rows.dtype).at[slot]]
    dot_general x2 -> x0, matrix products: 8.67 us -> none  [the longest x1 6.56 us: shards(): jnp.einsum('nbks,nbkt->snt', sliced, leaf_rows, preferred_element_type=jn...]
    all_to_all x2 -> x1, starting transfers between devices: 12.6 us -> 6.61 us  [shards(): lax.all_to_all(blocks, 'leaf', split_axis=0, concat_axis=0, tiled=True)]
    sort x1 -> x0, other arithmetic: 4.5 us -> none  [bucket_rows(): order = jnp.argsort(route, stable=True)]
  transfers between devices with their start and end apart: 4 -> 3, of which waited for: 3 -> 3; matrix products, arithmetic and copies ran while one was open for 10% -> 2% of each run, Pallas kernels for 0% -> 10%
where the time goes in v1:
time: 54.4 us; the launch traced here: 54 us
  waiting for transfers between devices  27.5 us (51%)
  Pallas kernels  11.6 us (21%)
  starting transfers between devices  8.48 us (16%)
  local copies, waits for them, and re-layouts  5.7 us (10%)
  between operations  0.7 us (1%)
    ppermute x1, waiting for transfers between devices, shards(): lax.ppermute(code[e - 1], 'blk', [(i, i ^ e) for i in range(blk_count)])  12.8 us
    all_to_all x1, waiting for transfers between devices, shards(): lax.all_to_all(blocks, 'leaf', split_axis=0, concat_axis=0, tiled=True)  12.4 us
    all_to_all x1, starting transfers between devices, shards(): lax.all_to_all(blocks, 'leaf', split_axis=0, concat_axis=0, tiled=True)  6.61 us
    pallas_call x1, Pallas kernels, shards(): call(leaf_kernel, (shape((node_dev, share, state), F32), shape((peers, no...  5.1 us
    unnamed x13, local copies, waits for them, and re-layouts  5.01 us
    ppermute x1, waiting for transfers between devices, shards(): lax.ppermute(node, 'leaf', [(i, i ^ 1) for i in range(leaf_count)])  2.29 us
    pallas_call x1, Pallas kernels, shards(): call(functools.partial(bucket_kernel, plan), shape((leaf_count, plan.bloc...  1.91 us
    pallas_call x1, Pallas kernels, shards(): call(merge_kernel, shape((share, node_dev, state), F32), [SMEM, VMEM, VMEM])  1.78 us
  transfers between devices with their start and end apart: 3, of which 3 were waited for; matrix products, arithmetic and copies ran while one was open for 2% of the time, Pallas kernels for 10%

profile of v1, /device:TPU:9, one launch (start us, length us, event | category | flops | bytes accessed | tf_op | source)
XLA Modules:
  0.0 54.0 jit_solution(4026735892746486080)
XLA Ops:
  0.6 0.0 copy-start.5
  0.6 0.7 %reshape.15.weight_ref = bf16[1,512]{1,0:T(2,128)(2,1)S(1)} reshape(bf16[512]{0:T(512)(128)(2,1)} %param.14) | data formatting | bytes 2048 | tf_op jit(solution)/shard_map/bucket/reshape | solution.py:239
  1.3 0.0 copy-start.2
  1.3 1.0 %copy-done.2 = bf16[512,512]{1,0:T(8,128)(2,1)S(1)} copy-done((bf16[512,512]{1,0:T(8,128)(2,1)S(1)}, bf16[512,512]{1,0:T(8,128)(2,1)}, u32[]{:S(2)}) %copy-start.2) | copy-done | bytes 524312
  2.4 0.0 copy-start.4
  2.4 0.7 %copy-done.4 = s32[512,1]{0,1:T(1,128)S(1)} copy-done((s32[512,1]{0,1:T(1,128)S(1)}, s32[512,1]{0,1:T(1,128)}, u32[]{:S(2)}) %copy-start.4) | copy-done | bytes 2072
  3.1 0.0 copy-start.3
  3.1 1.9 %bucket.1 = bf16[16,208,128]{2,1,0:T(8,128)(2,1)} custom-call(s32[1,512]{1,0:T(1,128)S(1)} %bitcast.10, bf16[1,512]{1,0:T(2,128)(2,1)S(1)} %reshape.15.weight_ref, bf16[512,512]{1,0:T(8,128)(2,1)S(1)} %copy-done.2), custom_call_target="tpu_custom_call" | custom-call | flops 402653184 | bytes 1048576 | tf_op jit(solution)/shard_map/bucket/pallas_call | solution.py:234
  5.0 6.6 %all-to-all-start = ((bf16[16,208,128]{2,1,0:T(8,128)(2,1)}), bf16[16,208,128]{2,1,0:T(8,128)(2,1)S(1)}, u32[]{:S(2)}, u32[]{:S(2)}) async-start(bf16[16,208,128]{2,1,0:T(8,128)(2,1)} %bucket.1), calls=%async_computation | async-start | bytes 1703936 | tf_op jit(solution)/shard_map/all_to_all | solution.py:240
  11.6 1.1 %copy.12 = bf16[256,2,512]{2,0,1:T(8,128)(2,1)S(1)} copy(bf16[256,2,512]{2,1,0:T(2,128)(2,1)} %param.12) | data formatting | bytes 1048576 | tf_op args[4]
  12.7 0.0 copy-done.5
  12.7 0.0 copy-done.3
  12.7 0.0 copy-start.1
  12.7 2.2 %copy-done.1 = bf16[2,8,256,512]{3,2,1,0:T(8,128)(2,1)S(1)} copy-done((bf16[2,8,256,512]{3,2,1,0:T(8,128)(2,1)S(1)}, bf16[2,8,256,512]{3,2,1,0:T(8,128)(2,1)}, u32[]{:S(2)}) %copy-start.1) | copy-done | bytes 4194328
  14.9 5.1 %leaf_products.1 = (f32[2,256,512]{2,1,0:T(8,128)S(1)}, f32[1,2,256,512]{3,2,1,0:T(8,128)S(1)}) custom-call(s32[1]{0:T(128)} %bitcast.place_ref, s32[2]{0:T(128)S(1)} %copy-done.5, bf16[2,8,256]{2,1,0:T(8,128)(2,1)S(1)} %copy-done.3, bf16[2,8,256,512]{3,2,1,0:T(8,128)(2,1)S(1)} %copy-done.1, bf16[2,256,512]{2,1,0:T(8,128)(2,1)S(1)} %bitcast.8), custom_call_target="tpu_custom_call" | custom-call | flops 2147483648 | bytes 8388608 | tf_op jit(solution)/shard_map/leaf_products/pallas_call | solution.py:243
  20.0 0.0 copy-start
  20.0 12.4 %all-to-all-done.got_ref = bf16[16,208,128]{2,1,0:T(8,128)(2,1)S(1)} async-done(((bf16[16,208,128]{2,1,0:T(8,128)(2,1)}), bf16[16,208,128]{2,1,0:T(8,128)(2,1)S(1)}, u32[]{:S(2)}, u32[]{:S(2)}) %all-to-all-start) | async-done | bytes 852000 | tf_op jit(solution)/shard_map/all_to_all | solution.py:240
  32.4 0.9 %routed_send.1 = (s16[1,544,512]{2,1,0:T(8,128)(2,1)S(1)}, bf16[2,512,512]{2,1,0:T(8,128)(2,1)S(1)}, bf16[2,512,512]{2,1,0:T(8,128)(2,1)S(1)}) custom-call(s32[1]{0:T(128)} %bitcast.place_ref, bf16[16,208,128]{2,1,0:T(8,128)(2,1)S(1)} %all-to-all-done.got_ref, f32[1,2,256,512]{3,2,1,0:T(8,128)S(1)} %get-tuple-element.10.part_ref), custom_call_target="tpu_custom_call" | custom-call | flops 536870912 | bytes 1048576 | tf_op jit(solution)/shard_map/routed_send/pallas_call | solution.py:264
  33.3 1.3 %collective-permute-start = (s16[544,512]{1,0:T(8,128)(2,1)S(1)}, s16[544,512]{1,0:T(8,128)(2,1)S(1)}, u32[]{:S(2)}, u32[]{:S(2)}) collective-permute-start(s16[544,512]{1,0:T(8,128)(2,1)S(1)} %bitcast.9), channel_id=1, source_target_pairs={{0,1},{1,0},{2,3},{3,2},{4,5},{5,4},{6,7},{7,6},{8,9},{9,8},{10,11... | collective-permute-start | bytes 1671176 | tf_op jit(solution)/shard_map/ppermute | solution.py:276
  34.6 0.5 routed_own.1.own_ref
  35.1 12.8 %collective-permute-done = s16[544,512]{1,0:T(8,128)(2,1)S(1)} collective-permute-done((s16[544,512]{1,0:T(8,128)(2,1)S(1)}, s16[544,512]{1,0:T(8,128)(2,1)S(1)}, u32[]{:S(2)}, u32[]{:S(2)}) %collective-permute-start) | collective-permute-done | bytes 557088 | tf_op jit(solution)/shard_map/ppermute | solution.py:276
  47.9 1.4 %node.1 = (f32[256,2,512]{2,1,0:T(2,128)}, f32[2,256,512]{2,1,0:T(8,128)S(1)}) custom-call(f32[2,256,512]{2,1,0:T(8,128)S(1)} %routed_own.1.own_ref, s16[1,544,512]{2,1,0:T(8,128)(2,1)S(1)} %bitcast.7), custom_call_target="tpu_custom_call" | custom-call | bytes 1048576 | tf_op jit(solution)/shard_map/node/pallas_call | solution.py:288
  49.3 0.6 %collective-permute-start.1 = (f32[2,256,512]{2,1,0:T(8,128)S(1)}, f32[2,256,512]{2,1,0:T(8,128)S(1)}, u32[]{:S(2)}, u32[]{:S(2)}) collective-permute-start(f32[2,256,512]{2,1,0:T(8,128)S(1)} %get-tuple-element.15.node_ref), channel_id=1, source_target_pairs={{0,2},{2,0},{4,6},{6,4},{8,10},{10,8},{12,14},{14,12},{16,18},{18,... | collective-permute-start | bytes 3145736 | tf_op jit(solution)/shard_map/ppermute | solution.py:293
  49.9 2.3 %collective-permute-done.1.partner_ref = f32[2,256,512]{2,1,0:T(8,128)S(1)} collective-permute-done((f32[2,256,512]{2,1,0:T(8,128)S(1)}, f32[2,256,512]{2,1,0:T(8,128)S(1)}, u32[]{:S(2)}, u32[]{:S(2)}) %collective-permute-start.1) | collective-permute-done | bytes 1048608 | tf_op jit(solution)/shard_map/ppermute | solution.py:293
  52.2 0.0 copy-done
  52.2 1.8 %merge.1 = f32[256,2,512]{2,1,0:T(2,128)} custom-call(s32[1,2]{1,0:T(1,128)S(1)} %copy-done, f32[2,256,512]{2,1,0:T(8,128)S(1)} %get-tuple-element.15.node_ref, f32[2,256,512]{2,1,0:T(8,128)S(1)} %collective-permute-done.1.partner_ref), custom_call_target="tpu_custom_call" | custom-call | bytes 1048576 | tf_op jit(solution)/shard_map/merge/pallas_call | solution.py:295
Async XLA Ops:
  0.6 12.0 %copy-start.5 = (s32[2]{0:T(128)S(1)}, s32[2]{0:T(128)}, u32[]{:S(2)}) copy-start(s32[2]{0:T(128)} %branching_ref.1) | copy-start | bytes 28
  1.3 1.0 %copy-start.2 = (bf16[512,512]{1,0:T(8,128)(2,1)S(1)}, bf16[512,512]{1,0:T(8,128)(2,1)}, u32[]{:S(2)}) copy-start(bf16[512,512]{1,0:T(8,128)(2,1)} %rows_ref.3) | copy-start | bytes 1572868
  2.4 0.7 %copy-start.4 = (s32[512,1]{0,1:T(1,128)S(1)}, s32[512,1]{0,1:T(1,128)}, u32[]{:S(2)}) copy-start(s32[512,1]{0,1:T(1,128)} %param.15) | copy-start | bytes 6148
  3.1 9.6 %copy-start.3 = (bf16[2,8,256]{2,1,0:T(8,128)(2,1)S(1)}, bf16[2,8,256]{2,1,0:T(8,128)(2,1)}, u32[]{:S(2)}) copy-start(bf16[2,8,256]{2,1,0:T(8,128)(2,1)} %weight_ref.1) | copy-start | bytes 24580
  5.0 27.5 %all-to-all-start = ((bf16[16,208,128]{2,1,0:T(8,128)(2,1)}), bf16[16,208,128]{2,1,0:T(8,128)(2,1)S(1)}, u32[]{:S(2)}, u32[]{:S(2)}) async-start(bf16[16,208,128]{2,1,0:T(8,128)(2,1)} %bucket.1), calls=%async_computation | async-start | bytes 1703936 | tf_op jit(solution)/shard_map/all_to_all | solution.py:240
  12.7 2.2 %copy-start.1 = (bf16[2,8,256,512]{3,2,1,0:T(8,128)(2,1)S(1)}, bf16[2,8,256,512]{3,2,1,0:T(8,128)(2,1)}, u32[]{:S(2)}) copy-start(bf16[2,8,256,512]{3,2,1,0:T(8,128)(2,1)} %rows_ref.2) | copy-start | bytes 12582916
  20.0 32.2 %copy-start = (s32[1,2]{1,0:T(1,128)S(1)}, s32[1,2]{1,0:T(1,128)}, u32[]{:S(2)}) copy-start(s32[1,2]{1,0:T(1,128)} %sibling_ref.1) | copy-start | bytes 28
  33.3 14.5 %collective-permute-start = (s16[544,512]{1,0:T(8,128)(2,1)S(1)}, s16[544,512]{1,0:T(8,128)(2,1)S(1)}, u32[]{:S(2)}, u32[]{:S(2)}) collective-permute-start(s16[544,512]{1,0:T(8,128)(2,1)S(1)} %bitcast.9), channel_id=1, source_target_pairs={{0,1},{1,0},{2,3},{3,2},{4,5},{5,4},{6,7},{7,6},{8,9},{9,8},{10,11... | collective-permute-start | bytes 1671176 | tf_op jit(solution)/shard_map/ppermute | solution.py:276
  49.3 2.9 %collective-permute-start.1 = (f32[2,256,512]{2,1,0:T(8,128)S(1)}, f32[2,256,512]{2,1,0:T(8,128)S(1)}, u32[]{:S(2)}, u32[]{:S(2)}) collective-permute-start(f32[2,256,512]{2,1,0:T(8,128)S(1)} %get-tuple-element.15.node_ref), channel_id=1, source_target_pairs={{0,2},{2,0},{4,6},{6,4},{8,10},{10,8},{12,14},{14,12},{16,18},{18,... | collective-permute-start | bytes 3145736 | tf_op jit(solution)/shard_map/ppermute | solution.py:293

commit v2 on v1

--- a/solution.py
+++ b/solution.py
@@ -112,9 +112,19 @@
         send_ref[e - 1, 0] = total[pl.ds(at, share), :]
 
 
-def send_kernel(plan, place_ref, got_ref, part_ref, code_ref, plain_ref, scaled_ref, total=None):
-    blk = place_ref[0]
-    peers, _, share, state = part_ref.shape
+class Product:
+    def __init__(self, scaled_ref, plain_ref, total):
+        self.scaled_ref, self.plain_ref, self.total = scaled_ref, plain_ref, total
+        if total is not None:
+            total[...] = dot_t(scaled_ref[...], plain_ref[...])
+
+    def rows(self, at, share):
+        if self.total is not None:
+            return self.total[pl.ds(at, share), :]
+        return dot_t(self.scaled_ref[:, pl.ds(at, share)], self.plain_ref[...])
+
+
+def gather_rows(plan, got_ref, plain_ref, scaled_ref):
     for d in range(plan.leaf_count):
         extra = got_ref[d, plan.slabs * plan.rows :, :].astype(F32)
         for g in range(plan.groups):
@@ -133,55 +143,112 @@
                 j = g * plan.node_dev + q
                 plain_ref[q, at : at + GROUP, :] = rows
                 scaled_ref[q, at : at + GROUP, :] = (wide * extra[:, j : j + 1]).astype(BF16)
-    for q in range(plan.node_dev):
+
+
+def scale_of(most):
+    power = jnp.ceil(8.0 * jnp.log2(jnp.maximum(most, 1e-30)))
+    return power, CODE * jnp.exp2(-0.125 * power)
+
+
+def to_code(value):
+    return jnp.round(value).astype(I32).astype(jnp.int16)
+
+
+def from_code(code):
+    return code.astype(I32).astype(F32)
+
+
+def diagonal(width):
+    return lax.broadcasted_iota(I32, (width, width), 0) == lax.broadcasted_iota(I32, (width, width), 1)
+
+
+def as_line(column):
+    return jnp.sum(jnp.where(diagonal(column.shape[0]), column, 0.0), axis=0, keepdims=True)
+
+
+def as_column(line):
+    return jnp.sum(jnp.where(diagonal(line.shape[1]), line, 0.0), axis=1, keepdims=True)
+
+
+def send_plain(plan, place_ref, got_ref, part_ref, code_ref, plain_ref, scaled_ref, total=None):
+    blk = place_ref[0]
+    peers, nodes, share, state = part_ref.shape
+    gather_rows(plan, got_ref, plain_ref, scaled_ref)
+    for q in range(nodes):
         product = Product(scaled_ref.at[q], plain_ref.at[q], total)
         for e in range(1, peers + 1):
             at = pl.multiple_of((blk ^ e) * share, share)
-            encode(part_ref[e - 1, q] + product.rows(at, share), code_ref.at[e - 1], q, share)
-
-
-class Product:
-    def __init__(self, scaled_ref, plain_ref, total):
-        self.scaled_ref, self.plain_ref, self.total = scaled_ref, plain_ref, total
-        if total is not None:
-            total[...] = dot_t(scaled_ref[...], plain_ref[...])
-
-    def rows(self, at, share):
-        if self.total is not None:
-            return self.total[pl.ds(at, share), :]
-        return dot_t(self.scaled_ref[:, pl.ds(at, share)], self.plain_ref[...])
-
-
-def encode(value, code_ref, q, share):
-    state = value.shape[1]
-    most = jnp.max(jnp.abs(value), axis=1, keepdims=True)
-    power = jnp.ceil(jnp.log2(jnp.maximum(most, 1e-30)))
-    code_ref[q * share : (q + 1) * share, :] = (
-        jnp.round(value * (CODE * jnp.exp2(-power))).astype(I32).astype(jnp.int16)
-    )
-    width = min(share, LANES)
-    eye = lax.broadcasted_iota(I32, (width, LANES), 0) == lax.broadcasted_iota(I32, (width, LANES), 1)
-    parts = []
-    for k in range(0, share, width):
-        parts.append(jnp.sum(jnp.where(eye, power[k : k + width], 0.0), axis=0, keepdims=True))
-    line = jnp.concatenate(parts + [jnp.zeros((1, state - LANES * len(parts)), F32)], axis=1)
-    line = jnp.broadcast_to(line, (GROUP, state)).astype(I32).astype(jnp.int16)
-    base = code_ref.shape[0] - GROUP * (code_ref.shape[0] // share - q)
-    code_ref[base : base + GROUP, :] = line
-
-
-def decode(code_ref, q, share):
-    base = code_ref.shape[0] - GROUP * (code_ref.shape[0] // share - q)
-    line = code_ref[base : base + GROUP, :].astype(I32).astype(F32)[0:1, :]
-    width = min(share, LANES)
-    eye = lax.broadcasted_iota(I32, (width, LANES), 0) == lax.broadcasted_iota(I32, (width, LANES), 1)
-    parts = []
-    for k in range(share // width):
-        one = line[:, k * LANES : (k + 1) * LANES]
-        parts.append(jnp.sum(jnp.where(eye, one, 0.0), axis=1, keepdims=True))
-    power = jnp.concatenate(parts, axis=0)
-    value = code_ref[q * share : (q + 1) * share, :].astype(I32).astype(F32)
-    return value * (jnp.exp2(power) * (1.0 / CODE))
+            value = part_ref[e - 1, q] + product.rows(at, share)
+            power, factor = scale_of(jnp.max(jnp.abs(value), axis=1, keepdims=True))
+            code_ref[e - 1, q * share : (q + 1) * share, :] = to_code(value * factor)
+            line = jnp.concatenate([as_line(power), jnp.zeros((1, state - share), F32)], axis=1)
+            base = nodes * share + q * GROUP
+            code_ref[e - 1, base : base + GROUP, :] = to_code(jnp.broadcast_to(line, (GROUP, state)))
+
+
+def decode_plain(place, code_ref, nodes, share):
+    values = []
+    for q in range(nodes):
+        base = nodes * share + q * GROUP
+        value = None
+        for e in range(code_ref.shape[0]):
+            power = as_column(from_code(code_ref[e, base : base + GROUP, :])[0:1, :share])
+            term = from_code(code_ref[e, q * share : (q + 1) * share, :]) * (
+                jnp.exp2(0.125 * power) * (1.0 / CODE)
+            )
+            value = term if value is None else value + term
+        values.append(value)
+    return values
+
+
+def send_folded(plan, place_ref, got_ref, part_ref, code_ref, plain_ref, scaled_ref):
+    share = part_ref.shape[2]
+    mine = pl.ds(pl.multiple_of(place_ref[0] * share, share), share)
+    theirs = pl.ds(pl.multiple_of((1 - place_ref[0]) * share, share), share)
+    gather_rows(plan, got_ref, plain_ref, scaled_ref)
+    square, beside = [], []
+    for q in range(2):
+        scaled = scaled_ref[q, :, theirs]
+        square.append(part_ref[0, q, :, theirs] + dot_t(scaled, plain_ref[q, :, theirs]))
+        beside.append(part_ref[0, q, :, mine] + dot_t(scaled, plain_ref[q, :, mine]))
+    most = jnp.maximum(
+        jnp.maximum(jnp.abs(square[0]), jnp.abs(square[1])),
+        jnp.maximum(jnp.abs(beside[0]), jnp.abs(beside[1])),
+    )
+    power, factor = scale_of(jnp.max(most, axis=1, keepdims=True))
+    row = lax.broadcasted_iota(I32, (share, share), 0)
+    column = lax.broadcasted_iota(I32, (share, share), 1)
+    lower = square[1] * factor
+    code_ref[0, :share, 0:share] = to_code(jnp.where(column >= row, square[0] * factor, lower))
+    code_ref[0, :share, share : 2 * share] = to_code(beside[0] * factor)
+    code_ref[0, :share, 2 * share :] = to_code(beside[1] * factor)
+    corner = jnp.sum(jnp.where(column == row, jnp.round(lower), 0.0), axis=0, keepdims=True)
+    line = jnp.concatenate([as_line(power), corner, jnp.zeros((1, share), F32)], axis=1)
+    code_ref[0, share:, :] = to_code(jnp.broadcast_to(line, (GROUP, 3 * share)))
+
+
+def decode_folded(place, code_ref, nodes, share):
+    line = from_code(code_ref[0, share:, :])[0:1, :]
+    step = jnp.exp2(0.125 * as_column(line[:, :share])) * (1.0 / CODE)
+    both = from_code(code_ref[0, :share, 0:share]) * step
+    turned = jnp.transpose(both)
+    corner = as_column(line[:, share : 2 * share]) * step
+    row = lax.broadcasted_iota(I32, (share, share), 0)
+    column = lax.broadcasted_iota(I32, (share, share), 1)
+    squares = [
+        jnp.where(column >= row, both, turned),
+        jnp.where(column < row, both, jnp.where(column == row, corner, turned)),
+    ]
+    values = []
+    for q in range(2):
+        beside = from_code(code_ref[0, :share, (1 + q) * share : (2 + q) * share]) * step
+        first = place == 0
+        values.append(
+            jnp.concatenate(
+                [jnp.where(first, squares[q], beside), jnp.where(first, beside, squares[q])], axis=1
+            )
+        )
+    return values
 
 
 def own_kernel(place_ref, part_ref, plain_ref, scaled_ref, own_ref, total=None):
@@ -191,18 +258,21 @@
         own_ref[q] = part_ref[q] + Product(scaled_ref.at[q], plain_ref.at[q], total).rows(at, share)
 
 
-def node_kernel(own_ref, code_ref, out_ref, node_ref):
+def node_kernel(decode, place_ref, own_ref, code_ref, out_ref, node_ref):
     nodes, share, _ = own_ref.shape
-    for q in range(nodes):
-        value = own_ref[q]
-        for e in range(code_ref.shape[0]):
-            value = value + decode(code_ref.at[e], q, share)
+    arrived = decode(place_ref[0], code_ref, nodes, share)
+    for q in range(nodes):
+        value = own_ref[q] + arrived[q]
         node_ref[q] = value
         out_ref[:, q, :] = value
 
 
-def merge_kernel(sibling_ref, node_ref, partner_ref, out_ref):
-    for q in range(node_ref.shape[0]):
+def merge_kernel(decode, place_ref, sibling_ref, node_ref, own_ref, code_ref, out_ref, partner_ref):
+    nodes, share, _ = own_ref.shape
+    arrived = decode(place_ref[0], code_ref, nodes, share)
+    for q in range(nodes):
+        partner_ref[q] = own_ref[q] + arrived[q]
+    for q in range(nodes):
         out_ref[:, q, :] = node_ref[q] + partner_ref[sibling_ref[0, q]]
 
 
@@ -260,11 +330,14 @@
             moved=8 << 20,
         )(place, branching, leaf_weight, leaf_rows, jnp.transpose(node_block, (1, 0, 2)))
 
+    folded = blk_count == 2 and node_dev == 2 and share % LANES == 0
+    decode = decode_folded if folded else decode_plain
+    code_shape = (share + GROUP, 3 * share) if folded else (node_dev * (share + GROUP), state)
     with jax.named_scope("routed_send"):
         code, plain, scaled = call(
-            functools.partial(send_kernel, plan),
+            functools.partial(send_folded if folded else send_plain, plan),
             (
-                shape((peers, node_dev * (share + GROUP), state), jnp.int16),
+                shape((peers, *code_shape), jnp.int16),
                 shape((node_dev, max(plan.depth), state), BF16),
                 shape((node_dev, max(plan.depth), state), BF16),
             ),
@@ -272,10 +345,11 @@
             scratch_shapes=whole,
             flops=2 * node_dev * max(plan.depth) * state * state,
         )(place, got, send_part)
-    received = [
+    arrived = [
         lax.ppermute(code[e - 1], "blk", [(i, i ^ e) for i in range(blk_count)])
         for e in range(1, blk_count)
     ]
+    arrived = jnp.stack(arrived) if peers > 1 else arrived[0][None]
     with jax.named_scope("routed_own"):
         own = call(
             own_kernel,
@@ -284,17 +358,22 @@
             scratch_shapes=whole,
             flops=2 * node_dev * max(plan.depth) * share * state,
         )(place, own_part, plain, scaled)
+    to_partner = [(i, i ^ 1) for i in range(leaf_count)]
+    partner_own = lax.ppermute(own, "leaf", to_partner)
+    partner_arrived = lax.ppermute(arrived, "leaf", to_partner)
     with jax.named_scope("node"):
         node_schur, node = call(
-            node_kernel,
+            functools.partial(node_kernel, decode),
             (shape((share, node_dev, state), F32), shape((node_dev, share, state), F32)),
-            [VMEM, VMEM],
-        )(own, jnp.stack(received) if peers > 1 else received[0][None])
-    partner = lax.ppermute(node, "leaf", [(i, i ^ 1) for i in range(leaf_count)])
+            [SMEM, VMEM, VMEM],
+        )(place, own, arrived)
     with jax.named_scope("merge"):
         merged = call(
-            merge_kernel, shape((share, node_dev, state), F32), [SMEM, VMEM, VMEM]
-        )(sibling, node, partner)
+            functools.partial(merge_kernel, decode),
+            shape((share, node_dev, state), F32),
+            [SMEM, SMEM, VMEM, VMEM, VMEM],
+            scratch_shapes=[pltpu.VMEM((node_dev, share, state), F32)],
+        )(place, sibling, node, partner_own, partner_arrived)
     return (node_schur, merged)
 
 

time: 54.4 us -> 50.4 us (0.926)
  waiting for transfers between devices: 27.5 us -> 22.8 us
  starting transfers between devices: 8.48 us -> 9.24 us
    ppermute x1, waiting for transfers between devices: 12.8 us -> 9.56 us  [shards(): lax.ppermute(code[e - 1], 'blk', [(i, i ^ e) for i in range(blk_count)])]
    ppermute x1 -> x2, waiting for transfers between devices: 2.29 us -> 0.01 us  [the longest x1 0.01 us: shards(): partner_arrived = lax.ppermute(arrived, 'leaf', to_partner)]
    pallas_call x1, Pallas kernels: 5.1 us -> 4.31 us  [shards(): call(leaf_kernel, (shape((node_dev, share, state), F32), shape((peers, no...]
    all_to_all x1, waiting for transfers between devices: 12.4 us -> 13.2 us  [shards(): lax.all_to_all(blocks, 'leaf', split_axis=0, concat_axis=0, tiled=True)]
    ppermute x1 -> x2, starting transfers between devices: 0.6 us -> 1.34 us  [the longest x1 1.27 us: shards(): partner_arrived = lax.ppermute(arrived, 'leaf', to_partner)]
  transfers between devices with their start and end apart: 3 -> 4, of which waited for: 3 -> 2; matrix products, arithmetic and copies ran while one was open for 2% -> 2% of each run, Pallas kernels for 10% -> 12%
where the time goes in v2:
time: 50.4 us; the launch traced here: 49.7 us
  waiting for transfers between devices  22.8 us (45%)
  Pallas kernels  11.3 us (22%)
  starting transfers between devices  9.24 us (18%)
  local copies, waits for them, and re-layouts  5.7 us (11%)
  between operations  0.71 us (1%)
    all_to_all x1, waiting for transfers between devices, shards(): lax.all_to_all(blocks, 'leaf', split_axis=0, concat_axis=0, tiled=True)  13.2 us
    ppermute x1, waiting for transfers between devices, shards(): lax.ppermute(code[e - 1], 'blk', [(i, i ^ e) for i in range(blk_count)])  9.56 us
    all_to_all x1, starting transfers between devices, shards(): lax.all_to_all(blocks, 'leaf', split_axis=0, concat_axis=0, tiled=True)  6.61 us
    unnamed x13, local copies, waits for them, and re-layouts  5.01 us
    pallas_call x1, Pallas kernels, shards(): call(leaf_kernel, (shape((node_dev, share, state), F32), shape((peers, no...  4.31 us
    pallas_call x1, Pallas kernels, shards(): call(functools.partial(merge_kernel, decode), shape((share, node_dev, sta...  2.16 us
    pallas_call x1, Pallas kernels, shards(): call(functools.partial(bucket_kernel, plan), shape((leaf_count, plan.bloc...  1.91 us
    pallas_call x1, Pallas kernels, shards(): call(functools.partial(node_kernel, decode), (shape((share, node_dev, sta...  1.52 us
  transfers between devices with their start and end apart: 4, of which 2 were waited for; matrix products, arithmetic and copies ran while one was open for 2% of the time, Pallas kernels for 12%

profile of v2, /device:TPU:9, one launch (start us, length us, event | category | flops | bytes accessed | tf_op | source)
XLA Modules:
  0.0 49.7 jit_solution(12417579069525772891)
XLA Ops:
  0.6 0.0 copy-start.5
  0.6 0.7 %reshape.15.weight_ref = bf16[1,512]{1,0:T(2,128)(2,1)S(1)} reshape(bf16[512]{0:T(512)(128)(2,1)} %param.14) | data formatting | bytes 2048 | tf_op jit(solution)/shard_map/bucket/reshape | solution.py:309
  1.3 0.0 copy-start.2
  1.3 1.0 %copy-done.2 = bf16[512,512]{1,0:T(8,128)(2,1)S(1)} copy-done((bf16[512,512]{1,0:T(8,128)(2,1)S(1)}, bf16[512,512]{1,0:T(8,128)(2,1)}, u32[]{:S(2)}) %copy-start.2) | copy-done | bytes 524312
  2.4 0.0 copy-start.4
  2.4 0.7 %copy-done.4 = s32[512,1]{0,1:T(1,128)S(1)} copy-done((s32[512,1]{0,1:T(1,128)S(1)}, s32[512,1]{0,1:T(1,128)}, u32[]{:S(2)}) %copy-start.4) | copy-done | bytes 2072
  3.1 0.0 copy-start.3
  3.1 1.9 %bucket.1 = bf16[16,208,128]{2,1,0:T(8,128)(2,1)} custom-call(s32[1,512]{1,0:T(1,128)S(1)} %bitcast.11, bf16[1,512]{1,0:T(2,128)(2,1)S(1)} %reshape.15.weight_ref, bf16[512,512]{1,0:T(8,128)(2,1)S(1)} %copy-done.2), custom_call_target="tpu_custom_call" | custom-call | flops 402653184 | bytes 1048576 | tf_op jit(solution)/shard_map/bucket/pallas_call | solution.py:304
  5.0 6.6 %all-to-all-start = ((bf16[16,208,128]{2,1,0:T(8,128)(2,1)}), bf16[16,208,128]{2,1,0:T(8,128)(2,1)S(1)}, u32[]{:S(2)}, u32[]{:S(2)}) async-start(bf16[16,208,128]{2,1,0:T(8,128)(2,1)} %bucket.1), calls=%async_computation | async-start | bytes 1703936 | tf_op jit(solution)/shard_map/all_to_all | solution.py:310
  11.6 1.1 %copy.12 = bf16[256,2,512]{2,0,1:T(8,128)(2,1)S(1)} copy(bf16[256,2,512]{2,1,0:T(2,128)(2,1)} %param.12) | data formatting | bytes 1048576 | tf_op args[4]
  12.7 0.0 copy-done.5
  12.7 0.0 copy-done.3
  12.7 0.0 copy-start.1
  12.7 2.2 %copy-done.1 = bf16[2,8,256,512]{3,2,1,0:T(8,128)(2,1)S(1)} copy-done((bf16[2,8,256,512]{3,2,1,0:T(8,128)(2,1)S(1)}, bf16[2,8,256,512]{3,2,1,0:T(8,128)(2,1)}, u32[]{:S(2)}) %copy-start.1) | copy-done | bytes 4194328
  14.9 4.3 %leaf_products.1 = (f32[2,256,512]{2,1,0:T(8,128)S(1)}, f32[1,2,256,512]{3,2,1,0:T(8,128)S(1)}) custom-call(s32[1]{0:T(128)} %bitcast.place_ref, s32[2]{0:T(128)S(1)} %copy-done.5, bf16[2,8,256]{2,1,0:T(8,128)(2,1)S(1)} %copy-done.3, bf16[2,8,256,512]{3,2,1,0:T(8,128)(2,1)S(1)} %copy-done.1, bf16[2,256,512]{2,1,0:T(8,128)(2,1)S(1)} %bitcast.7), custom_call_target="tpu_custom_call" | custom-call | flops 2147483648 | bytes 8388608 | tf_op jit(solution)/shard_map/leaf_products/pallas_call | solution.py:313
  19.2 0.0 copy-start
  19.2 13.2 %all-to-all-done.got_ref = bf16[16,208,128]{2,1,0:T(8,128)(2,1)S(1)} async-done(((bf16[16,208,128]{2,1,0:T(8,128)(2,1)}), bf16[16,208,128]{2,1,0:T(8,128)(2,1)S(1)}, u32[]{:S(2)}, u32[]{:S(2)}) %all-to-all-start) | async-done | bytes 852000 | tf_op jit(solution)/shard_map/all_to_all | solution.py:310
  32.4 0.9 %routed_send.1 = (s16[1,272,768]{2,1,0:T(8,128)(2,1)S(1)}, bf16[2,512,512]{2,1,0:T(8,128)(2,1)S(1)}, bf16[2,512,512]{2,1,0:T(8,128)(2,1)S(1)}) custom-call(s32[1]{0:T(128)} %bitcast.place_ref, bf16[16,208,128]{2,1,0:T(8,128)(2,1)S(1)} %all-to-all-done.got_ref, f32[1,2,256,512]{3,2,1,0:T(8,128)S(1)} %get-tuple-element.10.part_ref), custom_call_target="tpu_custom_call" | custom-call | flops 536870912 | bytes 1048576 | tf_op jit(solution)/shard_map/routed_send/pallas_call | solution.py:337
  33.4 0.5 routed_own.1.own_ref
  33.9 0.1 collective-permute-start.1
  33.9 1.3 %collective-permute-start = (s16[272,768]{1,0:T(8,128)(2,1)S(1)}, s16[272,768]{1,0:T(8,128)(2,1)S(1)}, u32[]{:S(2)}, u32[]{:S(2)}) collective-permute-start(s16[272,768]{1,0:T(8,128)(2,1)S(1)} %bitcast.10), channel_id=1, source_target_pairs={{0,1},{1,0},{2,3},{3,2},{4,5},{5,4},{6,7},{7,6},{8,9},{9,8},{10,11... | collective-permute-start | bytes 1253384 | tf_op jit(solution)/shard_map/ppermute | solution.py:349
  35.2 9.6 %collective-permute-done = s16[272,768]{1,0:T(8,128)(2,1)S(1)} collective-permute-done((s16[272,768]{1,0:T(8,128)(2,1)S(1)}, s16[272,768]{1,0:T(8,128)(2,1)S(1)}, u32[]{:S(2)}, u32[]{:S(2)}) %collective-permute-start) | collective-permute-done | bytes 417824 | tf_op jit(solution)/shard_map/ppermute | solution.py:349
  44.8 1.3 %collective-permute-start.2 = (s16[1,272,768]{2,1,0:T(8,128)(2,1)S(1)}, s16[1,272,768]{2,1,0:T(8,128)(2,1)S(1)}, u32[]{:S(2)}, u32[]{:S(2)}) collective-permute-start(s16[1,272,768]{2,1,0:T(8,128)(2,1)S(1)} %bitcast.8), channel_id=1, source_target_pairs={{0,2},{2,0},{4,6},{6,4},{8,10},{10,8},{12,14},{14,12},{16,18},{18,... | collective-permute-start | bytes 1253384 | tf_op jit(solution)/shard_map/ppermute | solution.py:363
  46.1 1.5 %node.1 = (f32[256,2,512]{2,1,0:T(2,128)}, f32[2,256,512]{2,1,0:T(8,128)S(1)}) custom-call(s32[1]{0:T(128)} %bitcast.place_ref, f32[2,256,512]{2,1,0:T(8,128)S(1)} %routed_own.1.own_ref, s16[1,272,768]{2,1,0:T(8,128)(2,1)S(1)} %bitcast.9), custom_call_target="tpu_custom_call" | custom-call | bytes 1048576 | tf_op jit(solution)/shard_map/node/pallas_call | solution.py:365
  47.6 0.0 collective-permute-done.2.code_ref
  47.6 0.0 collective-permute-done.1.own_ref
  47.6 0.0 copy-done
  47.6 2.2 %merge.1 = f32[256,2,512]{2,1,0:T(2,128)} custom-call(s32[1]{0:T(128)} %bitcast.place_ref, s32[1,2]{1,0:T(1,128)S(1)} %copy-done, f32[2,256,512]{2,1,0:T(8,128)S(1)} %get-tuple-element.15.node_ref, f32[2,256,512]{2,1,0:T(8,128)S(1)} %collective-permute-done.1.own_ref, s16[1,272,768]{2,1,0:T(8,128)(2,1)S(1)} %collective-permute-done.2.code_ref), custom_call_target="tpu_custom_call" | custom-call | bytes 1048576 | tf_op jit(solution)/shard_map/merge/pallas_call | solution.py:371
Async XLA Ops:
  0.6 12.0 %copy-start.5 = (s32[2]{0:T(128)S(1)}, s32[2]{0:T(128)}, u32[]{:S(2)}) copy-start(s32[2]{0:T(128)} %branching_ref.1) | copy-start | bytes 28
  1.3 1.0 %copy-start.2 = (bf16[512,512]{1,0:T(8,128)(2,1)S(1)}, bf16[512,512]{1,0:T(8,128)(2,1)}, u32[]{:S(2)}) copy-start(bf16[512,512]{1,0:T(8,128)(2,1)} %rows_ref.3) | copy-start | bytes 1572868
  2.4 0.7 %copy-start.4 = (s32[512,1]{0,1:T(1,128)S(1)}, s32[512,1]{0,1:T(1,128)}, u32[]{:S(2)}) copy-start(s32[512,1]{0,1:T(1,128)} %param.15) | copy-start | bytes 6148
  3.1 9.6 %copy-start.3 = (bf16[2,8,256]{2,1,0:T(8,128)(2,1)S(1)}, bf16[2,8,256]{2,1,0:T(8,128)(2,1)}, u32[]{:S(2)}) copy-start(bf16[2,8,256]{2,1,0:T(8,128)(2,1)} %weight_ref.1) | copy-start | bytes 24580
  5.0 27.5 %all-to-all-start = ((bf16[16,208,128]{2,1,0:T(8,128)(2,1)}), bf16[16,208,128]{2,1,0:T(8,128)(2,1)S(1)}, u32[]{:S(2)}, u32[]{:S(2)}) async-start(bf16[16,208,128]{2,1,0:T(8,128)(2,1)} %bucket.1), calls=%async_computation | async-start | bytes 1703936 | tf_op jit(solution)/shard_map/all_to_all | solution.py:310
  12.7 2.2 %copy-start.1 = (bf16[2,8,256,512]{3,2,1,0:T(8,128)(2,1)S(1)}, bf16[2,8,256,512]{3,2,1,0:T(8,128)(2,1)}, u32[]{:S(2)}) copy-start(bf16[2,8,256,512]{3,2,1,0:T(8,128)(2,1)} %rows_ref.2) | copy-start | bytes 12582916
  19.2 28.4 %copy-start = (s32[1,2]{1,0:T(1,128)S(1)}, s32[1,2]{1,0:T(1,128)}, u32[]{:S(2)}) copy-start(s32[1,2]{1,0:T(1,128)} %sibling_ref.1) | copy-start | bytes 28
  33.9 13.7 %collective-permute-start.1 = (f32[2,256,512]{2,1,0:T(8,128)S(1)}, f32[2,256,512]{2,1,0:T(8,128)S(1)}, u32[]{:S(2)}, u32[]{:S(2)}) collective-permute-start(f32[2,256,512]{2,1,0:T(8,128)S(1)} %routed_own.1.own_ref), channel_id=1, source_target_pairs={{0,2},{2,0},{4,6},{6,4},{8,10},{10,8},{12,14},{14,12},{16,18},{18,... | collective-permute-start | bytes 3145736 | tf_op jit(solution)/shard_map/ppermute | solution.py:362
  33.9 10.8 %collective-permute-start = (s16[272,768]{1,0:T(8,128)(2,1)S(1)}, s16[272,768]{1,0:T(8,128)(2,1)S(1)}, u32[]{:S(2)}, u32[]{:S(2)}) collective-permute-start(s16[272,768]{1,0:T(8,128)(2,1)S(1)} %bitcast.10), channel_id=1, source_target_pairs={{0,1},{1,0},{2,3},{3,2},{4,5},{5,4},{6,7},{7,6},{8,9},{9,8},{10,11... | collective-permute-start | bytes 1253384 | tf_op jit(solution)/shard_map/ppermute | solution.py:349
  44.8 2.8 %collective-permute-start.2 = (s16[1,272,768]{2,1,0:T(8,128)(2,1)S(1)}, s16[1,272,768]{2,1,0:T(8,128)(2,1)S(1)}, u32[]{:S(2)}, u32[]{:S(2)}) collective-permute-start(s16[1,272,768]{2,1,0:T(8,128)(2,1)S(1)} %bitcast.8), channel_id=1, source_target_pairs={{0,2},{2,0},{4,6},{6,4},{8,10},{10,8},{12,14},{14,12},{16,18},{18,... | collective-permute-start | bytes 1253384 | tf_op jit(solution)/shard_map/ppermute | solution.py:363

commit v3 on v2

v3 whole, which is shorter than its diff:
```python
import functools

import jax
import jax.numpy as jnp
from jax import lax
from jax.experimental import pallas as pl
from jax.experimental.pallas import tpu as pltpu
from jax.sharding import PartitionSpec as P

F32 = jnp.float32
BF16 = jnp.bfloat16
I32 = jnp.int32
LANES = 128
GROUP = 16
EXTRA = 8
VMEM = pl.BlockSpec(memory_space=pltpu.VMEM)
SMEM = pl.BlockSpec(memory_space=pltpu.SMEM)
CODE = 32000.0


class Plan:
    def __init__(self, leaf_count, node_dev, capacity, state):
        self.leaf_count, self.node_dev, self.capacity, self.state = leaf_count, node_dev, capacity, state
        self.full = capacity // GROUP * GROUP
        self.rest = capacity - self.full
        self.rows = -(-node_dev * capacity // GROUP) * GROUP
        self.groups = self.rows // GROUP
        self.slabs = state // LANES
        self.block = self.slabs * self.rows + EXTRA
        self.groups_of = [
            [g for g in range(self.groups) if q in {self.node_at(g * GROUP + i) for i in range(GROUP)}]
            for q in range(node_dev)
        ]
        self.depth = [leaf_count * GROUP * len(g) for g in self.groups_of]

    def node_at(self, row):
        if row < self.node_dev * self.full:
            return row // self.full
        return min((row - self.node_dev * self.full) // self.rest, self.node_dev - 1) if self.rest else 0


def dot_t(a, b):
    return lax.dot_general(a, b, (((0,), (0,)), ((), ())), preferred_element_type=F32)


def bucket_kernel(plan, route_hbm, weight_hbm, rows_hbm, out_ref, route_ref, weight_ref, rows_ref, sems):
    count = rows_hbm.shape[0]
    state = plan.state
    copies = [
        pltpu.make_async_copy(route_hbm, route_ref, sems.at[0]),
        pltpu.make_async_copy(weight_hbm, weight_ref, sems.at[1]),
        pltpu.make_async_copy(rows_hbm, rows_ref.at[:, pl.ds(0, state)], sems.at[2]),
    ]
    for copy in copies:
        copy.start()
    nodes = plan.leaf_count * plan.node_dev
    before = (
        lax.broadcasted_iota(I32, (count, count), 0) < lax.broadcasted_iota(I32, (count, count), 1)
    ).astype(BF16)
    copies[0].wait()
    route = route_ref[...]
    member = lax.broadcasted_iota(I32, (nodes, count), 0) == route
    seen = jnp.dot(member.astype(BF16), before, preferred_element_type=F32)
    position = jnp.sum(jnp.where(member, seen, 0.0), axis=0, keepdims=True).astype(I32)
    owner = route // plan.node_dev
    q = route - owner * plan.node_dev
    slot = owner * plan.rows + jnp.where(
        position < plan.full,
        q * plan.full + position,
        plan.node_dev * plan.full + q * plan.rest + position - plan.full,
    )
    total = plan.leaf_count * plan.rows
    hit = jnp.where(lax.broadcasted_iota(I32, (total, count), 0) == slot, 1.0, 0.0).astype(BF16)
    copies[1].wait()
    rows_ref[:, state:] = dot_t(weight_ref[...], jnp.ones((1, LANES), BF16)).astype(BF16)
    copies[2].wait()
    filled = jnp.dot(hit, rows_ref[...], preferred_element_type=F32)
    weights = filled[:, state:]
    filled = filled[:, :state].astype(BF16)
    lane = lax.broadcasted_iota(I32, (EXTRA, LANES), 1)
    sub = lax.broadcasted_iota(I32, (EXTRA, LANES), 0)
    want = []
    for g in range(plan.rows // EXTRA):
        q_of = jnp.full((EXTRA, LANES), plan.node_at(g * EXTRA), I32)
        for i in range(1, EXTRA):
            step = plan.node_at(g * EXTRA + i) - plan.node_at(g * EXTRA + i - 1)
            if step:
                q_of = q_of + jnp.where(sub >= i, step, 0)
        want.append(lane == g * plan.node_dev + q_of)
    for d in range(plan.leaf_count):
        at = d * plan.rows
        for c in range(plan.slabs):
            out_ref[d, c * plan.rows : (c + 1) * plan.rows, :] = filled[
                at : at + plan.rows, c * LANES : (c + 1) * LANES
            ]
        extra = jnp.zeros((EXTRA, LANES), F32)
        for g in range(plan.rows // EXTRA):
            extra = jnp.where(want[g], weights[at + g * EXTRA : at + (g + 1) * EXTRA, :], extra)
        out_ref[d, plan.slabs * plan.rows :, :] = extra.astype(BF16)


def leaf_kernel(place_ref, branching_ref, weight_ref, rows_ref, block_ref, own_ref, send_ref, total):
    n = pl.program_id(0)
    share = own_ref.shape[1]
    peers = send_ref.shape[0]
    blk = place_ref[0]
    columns = jnp.transpose(weight_ref[0].astype(F32))
    total[...] = jnp.zeros_like(total)
    for b in range(rows_ref.shape[1]):

        @pl.when(b < branching_ref[n])
        def _():
            rows = rows_ref[0, b]
            scaled = (rows.astype(F32) * columns[:, b : b + 1]).astype(BF16)
            total[...] += dot_t(scaled, rows)

    own_ref[0] = total[pl.ds(pl.multiple_of(blk * share, share), share), :] + block_ref[0].astype(F32)
    for e in range(1, peers + 1):
        at = pl.multiple_of((blk ^ e) * share, share)
        send_ref[e - 1, 0] = total[pl.ds(at, share), :]


class Product:
    def __init__(self, scaled_ref, plain_ref, total):
        self.scaled_ref, self.plain_ref, self.total = scaled_ref, plain_ref, total
        if total is not None:
            total[...] = dot_t(scaled_ref[...], plain_ref[...])

    def rows(self, at, share):
        if self.total is not None:
            return self.total[pl.ds(at, share), :]
        return dot_t(self.scaled_ref[:, pl.ds(at, share)], self.plain_ref[...])


def gather_rows(plan, got_ref, plain_ref, scaled_ref):
    for d in range(plan.leaf_count):
        extra = got_ref[d, plan.slabs * plan.rows :, :].astype(F32)
        for g in range(plan.groups):
            rows = jnp.concatenate(
                [
                    got_ref[d, c * plan.rows + g * GROUP : c * plan.rows + (g + 1) * GROUP, :]
                    for c in range(plan.slabs)
                ],
                axis=1,
            )
            wide = rows.astype(F32)
            for q in range(plan.node_dev):
                if g not in plan.groups_of[q]:
                    continue
                at = (plan.groups_of[q].index(g) * plan.leaf_count + d) * GROUP
                first = g * GROUP // EXTRA * plan.node_dev + q
                places = range(first, first + GROUP // EXTRA * plan.node_dev, plan.node_dev)
                weight = jnp.concatenate([extra[:, j : j + 1] for j in places], axis=0)
                plain_ref[q, at : at + GROUP, :] = rows
                scaled_ref[q, at : at + GROUP, :] = (wide * weight).astype(BF16)


def scale_of(most):
    power = jnp.ceil(8.0 * jnp.log2(jnp.maximum(most, 1e-30)))
    return power, CODE * jnp.exp2(-0.125 * power)


def to_code(value):
    return jnp.round(value).astype(I32).astype(jnp.int16)


def from_code(code):
    return code.astype(I32).astype(F32)


def diagonal(width):
    return lax.broadcasted_iota(I32, (width, width), 0) == lax.broadcasted_iota(I32, (width, width), 1)


def as_line(column):
    return jnp.sum(jnp.where(diagonal(column.shape[0]), column, 0.0), axis=0, keepdims=True)


def as_column(line):
    return jnp.sum(jnp.where(diagonal(line.shape[1]), line, 0.0), axis=1, keepdims=True)


def send_plain(plan, place_ref, got_ref, part_ref, code_ref, plain_ref, scaled_ref, total=None):
    blk = place_ref[0]
    peers, nodes, share, state = part_ref.shape
    gather_rows(plan, got_ref, plain_ref, scaled_ref)
    for q in range(nodes):
        product = Product(scaled_ref.at[q], plain_ref.at[q], total)
        for e in range(1, peers + 1):
            at = pl.multiple_of((blk ^ e) * share, share)
            value = part_ref[e - 1, q] + product.rows(at, share)
            power, factor = scale_of(jnp.max(jnp.abs(value), axis=1, keepdims=True))
            code_ref[e - 1, q * share : (q + 1) * share, :] = to_code(value * factor)
            line = jnp.concatenate([as_line(power), jnp.zeros((1, state - share), F32)], axis=1)
            base = nodes * share + q * GROUP
            code_ref[e - 1, base : base + GROUP, :] = to_code(jnp.broadcast_to(line, (GROUP, state)))


def decode_plain(code_ref, nodes, share):
    values = []
    for q in range(nodes):
        base = nodes * share + q * GROUP
        value = None
        for e in range(code_ref.shape[0]):
            power = as_column(from_code(code_ref[e, base : base + GROUP, :])[0:1, :share])
            term = from_code(code_ref[e, q * share : (q + 1) * share, :]) * (
                jnp.exp2(0.125 * power) * (1.0 / CODE)
            )
            value = term if value is None else value + term
        values.append(value)
    return values


def send_folded(plan, place_ref, got_ref, part_ref, first_ref, second_ref, plain_ref, scaled_ref):
    share = part_ref.shape[2]
    half = share // 2
    mine = pl.ds(pl.multiple_of(place_ref[0] * share, share), share)
    theirs = pl.ds(pl.multiple_of((1 - place_ref[0]) * share, share), share)
    gather_rows(plan, got_ref, plain_ref, scaled_ref)
    square, beside = [], []
    for q in range(2):
        scaled = scaled_ref[q, :, theirs]
        square.append(part_ref[0, q, :, theirs] + dot_t(scaled, plain_ref[q, :, theirs]))
        beside.append(part_ref[0, q, :, mine] + dot_t(scaled, plain_ref[q, :, mine]))
    up, low = slice(0, half), slice(half, share)
    encode_part(
        first_ref, square[0][up, up], square[1][up, up], [s[up, low] for s in square] + [s[up, :] for s in beside]
    )
    encode_part(second_ref, square[0][low, low], square[1][low, low], [s[low, :] for s in beside])


def encode_part(code_ref, upper, lower, others):
    half = upper.shape[0]
    width = upper.shape[1]
    pieces = [o[:, c : c + width] for o in others for c in range(0, o.shape[1], width)]
    most = jnp.maximum(jnp.abs(upper), jnp.abs(lower))
    for piece in pieces:
        most = jnp.maximum(most, jnp.abs(piece))
    power, factor = scale_of(jnp.max(most, axis=1, keepdims=True))
    row = lax.broadcasted_iota(I32, (half, width), 0)
    column = lax.broadcasted_iota(I32, (half, width), 1)
    lower = lower * factor
    code_ref[:half, :] = to_code(jnp.where(column >= row, upper * factor, lower))
    for k, piece in enumerate(pieces):
        code_ref[(k + 1) * half : (k + 2) * half, :] = to_code(piece * factor)
    corner = jnp.sum(jnp.where(column == row, jnp.round(lower), 0.0), axis=0, keepdims=True)
    line = lax.broadcasted_iota(I32, (GROUP, width), 0)
    code_ref[(len(pieces) + 1) * half :, :] = to_code(
        jnp.where(line == 0, as_line(power), jnp.where(line == 1, corner, 0.0))
    )


def decode_part(code_ref):
    width = code_ref.shape[1]
    half = width
    count = code_ref.shape[0] // half
    lines = from_code(code_ref[count * half :, :])
    step = jnp.exp2(0.125 * as_column(lines[0:1, :])) * (1.0 / CODE)
    pieces = [from_code(code_ref[k * half : (k + 1) * half, :]) * step for k in range(count)]
    both = pieces[0]
    turned = jnp.transpose(both)
    corner = as_column(lines[1:2, :]) * step
    row = lax.broadcasted_iota(I32, (half, width), 0)
    column = lax.broadcasted_iota(I32, (half, width), 1)
    squares = [
        jnp.where(column >= row, both, turned),
        jnp.where(column < row, both, jnp.where(column == row, corner, turned)),
    ]
    return squares, pieces[1:]


def first_node_kernel(
    place_ref, part_ref, plain_ref, scaled_ref, code_ref, out_ref, node_ref, rest_ref
):
    share = part_ref.shape[1]
    half = share // 2
    at = pl.multiple_of(place_ref[0] * share, share)
    to = pl.multiple_of((1 - place_ref[0]) * share, share)
    squares, pieces = decode_part(code_ref)
    for q in range(2):
        own = part_ref[q] + dot_t(scaled_ref[q, :, pl.ds(at, share)], plain_ref[q])
        node_ref[q] = own[:half, :]
        rest_ref[q] = own[half:, :]
        node_ref[q, :, pl.ds(at, half)] += squares[q]
        node_ref[q, :, pl.ds(at + half, half)] += pieces[q]
        node_ref[q, :, pl.ds(to, half)] += pieces[2 + 2 * q]
        node_ref[q, :, pl.ds(to + half, half)] += pieces[3 + 2 * q]
        rest_ref[q, :, pl.ds(at, half)] += jnp.transpose(pieces[q])
        out_ref[:, q, :] = node_ref[q]


def add_second(place, code_ref, rest_ref, node_ref):
    half = rest_ref.shape[1]
    at = pl.multiple_of(place * 2 * half, half)
    to = pl.multiple_of((1 - place) * 2 * half, half)
    squares, pieces = decode_part(code_ref)
    for q in range(2):
        node_ref[q] = rest_ref[q]
        node_ref[q, :, pl.ds(at + half, half)] += squares[q]
        node_ref[q, :, pl.ds(to, half)] += pieces[2 * q]
        node_ref[q, :, pl.ds(to + half, half)] += pieces[2 * q + 1]


def second_node_kernel(place_ref, rest_ref, code_ref, _, out_ref, node_ref):
    add_second(place_ref[0], code_ref, rest_ref, node_ref)
    for q in range(2):
        out_ref[:, q, :] = node_ref[q]


def first_merge_kernel(sibling_ref, node_ref, partner_ref, out_ref):
    for q in range(2):
        out_ref[:, q, :] = node_ref[q] + partner_ref[sibling_ref[0, q]]


def second_merge_kernel(place_ref, sibling_ref, node_ref, rest_ref, code_ref, _, out_ref, partner_ref):
    add_second(place_ref[0], code_ref, rest_ref, partner_ref)
    for q in range(2):
        out_ref[:, q, :] = node_ref[q] + partner_ref[sibling_ref[0, q]]


def own_kernel(place_ref, part_ref, plain_ref, scaled_ref, own_ref, total=None):
    nodes, share, _ = part_ref.shape
    at = pl.multiple_of(place_ref[0] * share, share)
    for q in range(nodes):
        own_ref[q] = part_ref[q] + Product(scaled_ref.at[q], plain_ref.at[q], total).rows(at, share)


def node_kernel(own_ref, code_ref, out_ref, node_ref):
    nodes, share, _ = own_ref.shape
    arrived = decode_plain(code_ref, nodes, share)
    for q in range(nodes):
        value = own_ref[q] + arrived[q]
        node_ref[q] = value
        out_ref[:, q, :] = value


def merge_kernel(sibling_ref, node_ref, own_ref, code_ref, out_ref, partner_ref):
    nodes, share, _ = own_ref.shape
    arrived = decode_plain(code_ref, nodes, share)
    for q in range(nodes):
        partner_ref[q] = own_ref[q] + arrived[q]
    for q in range(nodes):
        out_ref[:, q, :] = node_ref[q] + partner_ref[sibling_ref[0, q]]


def call(kernel, out_shape, in_specs, flops=0, moved=1 << 20, vmem=32 << 20, **more):
    outs = jax.tree.map(lambda _: VMEM, out_shape)
    more.setdefault("out_specs", outs)
    return pl.pallas_call(
        kernel,
        out_shape=out_shape,
        in_specs=in_specs,
        compiler_params=pltpu.CompilerParams(vmem_limit_bytes=vmem),
        cost_estimate=pl.CostEstimate(flops=flops, bytes_accessed=moved, transcendentals=0),
        **more,
    )


def exchange_plain(plan, place, got, own_part, send_part, sibling, blk_count):
    peers, node_dev, share, state = send_part.shape
    shape = jax.ShapeDtypeStruct
    whole = [pltpu.VMEM((state, state), F32)] if share % LANES else []
    depth = max(plan.depth)
    to_partner = [(i, i ^ 1) for i in range(plan.leaf_count)]
    with jax.named_scope("routed_send"):
        code, plain, scaled = call(
            functools.partial(send_plain, plan),
            (
                shape((peers, node_dev * (share + GROUP), state), jnp.int16),
                shape((node_dev, depth, state), BF16),
                shape((node_dev, depth, state), BF16),
            ),
            [SMEM, VMEM, VMEM],
            scratch_shapes=whole,
            flops=2 * node_dev * depth * state * state,
        )(place, got, send_part)
    arrived = jnp.stack(
        [
            lax.ppermute(code[e - 1], "blk", [(i, i ^ e) for i in range(blk_count)])
            for e in range(1, blk_count)
        ]
    )
    with jax.named_scope("routed_own"):
        own = call(
            own_kernel,
            shape((node_dev, share, state), F32),
            [SMEM, VMEM, VMEM, VMEM],
            scratch_shapes=whole,
            flops=2 * node_dev * depth * share * state,
        )(place, own_part, plain, scaled)
    partner_own = lax.ppermute(own, "leaf", to_partner)
    partner_arrived = lax.ppermute(arrived, "leaf", to_partner)
    with jax.named_scope("node"):
        node_schur, node = call(
            node_kernel,
            (shape((share, node_dev, state), F32), shape((node_dev, share, state), F32)),
            [VMEM, VMEM],
        )(own, arrived)
    with jax.named_scope("merge"):
        merged = call(
            merge_kernel,
            shape((share, node_dev, state), F32),
            [SMEM, VMEM, VMEM, VMEM],
            scratch_shapes=[pltpu.VMEM((node_dev, share, state), F32)],
        )(sibling, node, partner_own, partner_arrived)
    return node_schur, merged


def exchange_folded(plan, place, got, own_part, send_part, sibling):
    _, node_dev, share, state = send_part.shape
    half = share // 2
    shape = jax.ShapeDtypeStruct
    depth = max(plan.depth)
    to_partner = [(i, i ^ 1) for i in range(plan.leaf_count)]
    across = [(0, 1), (1, 0)]
    result = shape((share, node_dev, state), F32)
    rows = shape((node_dev, half, state), F32)
    any_spec = pl.BlockSpec(memory_space=pl.ANY)
    part = [pl.BlockSpec((half, node_dev, state), lambda i, k=k: (k, 0, 0)) for k in range(2)]
    with jax.named_scope("routed_send"):
        first, second, plain, scaled = call(
            functools.partial(send_folded, plan),
            (
                shape((7 * half + GROUP, half), jnp.int16),
                shape((5 * half + GROUP, half), jnp.int16),
                shape((node_dev, depth, state), BF16),
                shape((node_dev, depth, state), BF16),
            ),
            [SMEM, VMEM, VMEM],
            flops=2 * node_dev * depth * share * state,
        )(place, got, send_part)
    first = lax.ppermute(first, "blk", across)
    second = lax.ppermute(second, "blk", across)
    with jax.named_scope("first_node"):
        node_schur, node, rest = call(
            first_node_kernel,
            (result, rows, rows),
            [SMEM, VMEM, VMEM, VMEM, VMEM],
            out_specs=(part[0], VMEM, VMEM),
            grid=(1,),
            flops=2 * node_dev * depth * share * state,
        )(place, own_part, plain, scaled, first)
    partner_node = lax.ppermute(node, "leaf", to_partner)
    partner_rest = lax.ppermute(rest, "leaf", to_partner)
    with jax.named_scope("first_merge"):
        merged = call(
            first_merge_kernel, result, [SMEM, VMEM, VMEM], out_specs=part[0], grid=(1,)
        )(sibling, node, partner_node)
    partner_second = lax.ppermute(second, "leaf", to_partner)
    with jax.named_scope("second_node"):
        node_schur, node = call(
            second_node_kernel,
            (result, rows),
            [SMEM, VMEM, VMEM, any_spec],
            out_specs=(part[1], VMEM),
            grid=(1,),
            input_output_aliases={3: 0},
        )(place, rest, second, node_schur)
    with jax.named_scope("second_merge"):
        merged = call(
            second_merge_kernel,
            result,
            [SMEM, SMEM, VMEM, VMEM, VMEM, any_spec],
            out_specs=part[1],
            grid=(1,),
            scratch_shapes=[pltpu.VMEM((node_dev, half, state), F32)],
            input_output_aliases={5: 0},
        )(place, sibling, node, partner_rest, partner_second, merged)
    return node_schur, merged


def shards(leaf_rows, leaf_weight, branching, sibling, node_block, na_rows, na_weight, na_route):
    leaf_count, blk_count = lax.axis_size("leaf"), lax.axis_size("blk")
    node_dev, most_children, depth, state = leaf_rows.shape
    count = na_rows.shape[0]
    share = state // blk_count
    peers = blk_count - 1
    plan = Plan(leaf_count, node_dev, 3 * count // (2 * leaf_count * node_dev), state)
    place = lax.axis_index("blk").astype(I32).reshape(1)
    shape = jax.ShapeDtypeStruct
    any_spec = pl.BlockSpec(memory_space=pl.ANY)

    with jax.named_scope("bucket"):
        blocks = call(
            functools.partial(bucket_kernel, plan),
            shape((leaf_count, plan.block, LANES), BF16),
            [any_spec, any_spec, any_spec],
            scratch_shapes=[
                pltpu.VMEM((1, count), I32),
                pltpu.VMEM((1, count), BF16),
                pltpu.VMEM((count, state + LANES), BF16),
                pltpu.SemaphoreType.DMA((3,)),
            ],
            vmem=60 << 20,
            flops=2 * plan.leaf_count * plan.rows * count * state,
        )(na_route.reshape(1, count), na_weight.reshape(1, count), na_rows)
    got = lax.all_to_all(blocks, "leaf", split_axis=0, concat_axis=0, tiled=True)

    with jax.named_scope("leaf_products"):
        own_part, send_part = call(
            leaf_kernel,
            (shape((node_dev, share, state), F32), shape((peers, node_dev, share, state), F32)),
            [
                SMEM,
                SMEM,
                pl.BlockSpec((1, most_children, depth), lambda n: (n, 0, 0)),
                pl.BlockSpec((1, most_children, depth, state), lambda n: (n, 0, 0, 0)),
                pl.BlockSpec((1, share, state), lambda n: (n, 0, 0)),
            ],
            out_specs=(
                pl.BlockSpec((1, share, state), lambda n: (n, 0, 0)),
                pl.BlockSpec((peers, 1, share, state), lambda n: (0, n, 0, 0)),
            ),
            grid=(node_dev,),
            scratch_shapes=[pltpu.VMEM((state, state), F32)],
            flops=2 * node_dev * most_children * depth * state * state,
            moved=8 << 20,
        )(place, branching, leaf_weight, leaf_rows, jnp.transpose(node_block, (1, 0, 2)))

    if blk_count == 2 and node_dev == 2 and share == 2 * LANES:
        return exchange_folded(plan, place, got, own_part, send_part, sibling)
    return exchange_plain(plan, place, got, own_part, send_part, sibling, blk_count)


def solution(mesh):
    return jax.shard_map(
        shards,
        mesh=mesh,
        in_specs=(
            P("leaf", None, "blk", None),
            P("leaf", None, "blk"),
            P("leaf"),
            P("leaf", None),
            P("blk", "leaf", None),
            P(("leaf", "blk"), None),
            P(("leaf", "blk")),
            P(("leaf", "blk"), None),
        ),
        out_specs=(P("blk", "leaf", None), P("blk", "leaf", None)),
        check_vma=False,
    )
```

time: 50.4 us -> 53.9 us (1.069)
  Pallas kernels: 11.3 us -> 15.8 us
  waiting for transfers between devices: 22.8 us -> 20 us
  starting transfers between devices: 9.24 us -> 11.1 us
    all_to_all x1, waiting for transfers between devices: 13.2 us -> 9.63 us  [shards(): lax.all_to_all(blocks, 'leaf', split_axis=0, concat_axis=0, tiled=True)]
    ppermute x3 -> x5, starting transfers between devices: 2.63 us -> 4.47 us  [the longest x1 1.36 us: exchange_folded(): partner_second = lax.ppermute(second, 'leaf', to_partner)]
    pallas_call x4 -> x5, Pallas kernels: 5.07 us -> 6.84 us  [the longest x1 1.78 us: exchange_folded(): call(second_merge_kernel, result, [SMEM, SMEM, VMEM, VMEM, VMEM, any_spec...]
    pallas_call x1, Pallas kernels: 4.31 us -> 5.92 us  [shards(): call(leaf_kernel, (shape((node_dev, share, state), F32), shape((peers, no...]
    pallas_call x1, Pallas kernels: 1.91 us -> 3.04 us  [shards(): call(functools.partial(bucket_kernel, plan), shape((leaf_count, plan.bloc...]
    ppermute x3 -> x5, waiting for transfers between devices: 9.57 us -> 10.4 us  [the longest x1 6.29 us: exchange_folded(): first = lax.ppermute(first, 'blk', across)]
    reshape x1, local copies, waits for them, and re-layouts: 0.69 us -> 1.26 us  [shards(): na_weight.reshape(1, count)]
    unnamed x13 -> x9, local copies, waits for them, and re-layouts: 5.01 us -> 4.63 us
  transfers between devices with their start and end apart: 4 -> 6, of which waited for: 2 -> 3; matrix products, arithmetic and copies ran while one was open for 2% -> 2% of each run, Pallas kernels for 12% -> 16%
where the time goes in v3:
time: 53.9 us; the launch traced here: 53.5 us
  waiting for transfers between devices  20 us (37%)
  Pallas kernels  15.8 us (29%)
  starting transfers between devices  11.1 us (21%)
  local copies, waits for them, and re-layouts  5.89 us (11%)
  between operations  0.68 us (1%)
    all_to_all x1, waiting for transfers between devices, shards(): lax.all_to_all(blocks, 'leaf', split_axis=0, concat_axis=0, tiled=True)  9.63 us
    all_to_all x1, starting transfers between devices, shards(): lax.all_to_all(blocks, 'leaf', split_axis=0, concat_axis=0, tiled=True)  6.62 us
    ppermute x1, waiting for transfers between devices, exchange_folded(): first = lax.ppermute(first, 'blk', across)  6.29 us
    pallas_call x1, Pallas kernels, shards(): call(leaf_kernel, (shape((node_dev, share, state), F32), shape((peers, no...  5.92 us
    unnamed x9, local copies, waits for them, and re-layouts  4.63 us
    ppermute x1, waiting for transfers between devices, exchange_folded(): second = lax.ppermute(second, 'blk', across)  4.11 us
    pallas_call x1, Pallas kernels, shards(): call(functools.partial(bucket_kernel, plan), shape((leaf_count, plan.bloc...  3.04 us
    pallas_call x1, Pallas kernels, exchange_folded(): call(second_merge_kernel, result, [SMEM, SMEM, VMEM, VMEM, VMEM, any_spec...  1.78 us
  transfers between devices with their start and end apart: 6, of which 3 were waited for; matrix products, arithmetic and copies ran while one was open for 2% of the time, Pallas kernels for 16%

profile of v3, /device:TPU:9, one launch (start us, length us, event | category | flops | bytes accessed | tf_op | source)
XLA Modules:
  0.0 53.5 jit_solution(14560243159717191914)
XLA Ops:
  0.6 1.3 %reshape.15.weight_hbm = bf16[1,512]{1,0:T(2,128)(2,1)} reshape(bf16[512]{0:T(512)(128)(2,1)} %param.14) | data formatting | bytes 2048 | tf_op jit(solution)/shard_map/bucket/reshape | solution.py:496
  1.9 3.0 %bucket.1 = bf16[16,200,128]{2,1,0:T(8,128)(2,1)} custom-call(s32[1,512]{1,0:T(1,128)} %bitcast.6, bf16[1,512]{1,0:T(2,128)(2,1)} %reshape.15.weight_hbm, bf16[512,512]{1,0:T(8,128)(2,1)} %rows_hbm.1), custom_call_target="tpu_custom_call" | custom-call | flops 402653184 | bytes 1048576 | tf_op jit(solution)/shard_map/bucket/pallas_call | solution.py:484
  4.9 6.6 %all-to-all-start = ((bf16[16,200,128]{2,1,0:T(8,128)(2,1)}), bf16[16,200,128]{2,1,0:T(8,128)(2,1)S(1)}, u32[]{:S(2)}, u32[]{:S(2)}) async-start(bf16[16,200,128]{2,1,0:T(8,128)(2,1)} %bucket.1), calls=%async_computation | async-start | bytes 1638400 | tf_op jit(solution)/shard_map/all_to_all | solution.py:497
  11.6 1.1 %copy.14 = bf16[256,2,512]{2,0,1:T(8,128)(2,1)S(1)} copy(bf16[256,2,512]{2,1,0:T(2,128)(2,1)} %param.12) | data formatting | bytes 1048576 | tf_op args[4]
  12.7 0.0 copy-start.1
  12.7 2.2 %copy-done.1 = bf16[2,8,256,512]{3,2,1,0:T(8,128)(2,1)S(1)} copy-done((bf16[2,8,256,512]{3,2,1,0:T(8,128)(2,1)S(1)}, bf16[2,8,256,512]{3,2,1,0:T(8,128)(2,1)}, u32[]{:S(2)}) %copy-start.1) | copy-done | bytes 4194328
  14.9 0.0 copy-start.2
  14.9 0.7 %copy-done.2 = bf16[2,8,256]{2,1,0:T(8,128)(2,1)S(1)} copy-done((bf16[2,8,256]{2,1,0:T(8,128)(2,1)S(1)}, bf16[2,8,256]{2,1,0:T(8,128)(2,1)}, u32[]{:S(2)}) %copy-start.2) | copy-done | bytes 8216
  15.5 0.0 copy-start.3
  15.6 0.7 %copy-done.3 = s32[2]{0:T(128)S(1)} copy-done((s32[2]{0:T(128)S(1)}, s32[2]{0:T(128)}, u32[]{:S(2)}) %copy-start.3) | copy-done | bytes 32
  16.2 5.9 %leaf_products.1 = (f32[2,256,512]{2,1,0:T(8,128)S(1)}, f32[1,2,256,512]{3,2,1,0:T(8,128)S(1)}) custom-call(s32[1]{0:T(128)} %bitcast.place_ref, s32[2]{0:T(128)S(1)} %copy-done.3, bf16[2,8,256]{2,1,0:T(8,128)(2,1)S(1)} %copy-done.2, bf16[2,8,256,512]{3,2,1,0:T(8,128)(2,1)S(1)} %copy-done.1, bf16[2,256,512]{2,1,0:T(8,128)(2,1)S(1)} %bitcast.5), custom_call_target="tpu_custom_call" | custom-call | flops 2147483648 | bytes 8388608 | tf_op jit(solution)/shard_map/leaf_products/pallas_call | solution.py:500
  22.1 0.0 copy-start
  22.1 9.6 %all-to-all-done.got_ref = bf16[16,200,128]{2,1,0:T(8,128)(2,1)S(1)} async-done(((bf16[16,200,128]{2,1,0:T(8,128)(2,1)}), bf16[16,200,128]{2,1,0:T(8,128)(2,1)S(1)}, u32[]{:S(2)}, u32[]{:S(2)}) %all-to-all-start) | async-done | bytes 819232 | tf_op jit(solution)/shard_map/all_to_all | solution.py:497
  31.8 1.0 %routed_send.1 = (s16[912,128]{1,0:T(8,128)(2,1)S(1)}, s16[656,128]{1,0:T(8,128)(2,1)S(1)}, bf16[2,512,512]{2,1,0:T(8,128)(2,1)S(1)}, bf16[2,512,512]{2,1,0:T(8,128)(2,1)S(1)}) custom-call(s32[1]{0:T(128)} %bitcast.place_ref, bf16[16,200,128]{2,1,0:T(8,128)(2,1)S(1)} %all-to-all-done.got_ref, f32[1,2,256,512]{3,2,1,0:T(8,128)S(1)} %get-tuple-element.14.part_ref), custom_call_target="tpu_custom_call" | custom-call | flops 268435456 | bytes 1048576 | tf_op jit(solution)/shard_map/routed_send/pallas_call | solution.py:421
  32.8 1.3 %collective-permute-start = (s16[912,128]{1,0:T(8,128)(2,1)S(1)}, s16[912,128]{1,0:T(8,128)(2,1)S(1)}, u32[]{:S(2)}, u32[]{:S(2)}) collective-permute-start(s16[912,128]{1,0:T(8,128)(2,1)S(1)} %get-tuple-element.17), channel_id=1, source_target_pairs={{0,1},{1,0},{2,3},{3,2},{4,5},{5,4},{6,7},{7,6},{8,9},{9,8},{10,11... | collective-permute-start | bytes 700424 | tf_op jit(solution)/shard_map/ppermute | solution.py:432
  34.1 6.3 %collective-permute-done.code_ref = s16[912,128]{1,0:T(8,128)(2,1)S(1)} collective-permute-done((s16[912,128]{1,0:T(8,128)(2,1)S(1)}, s16[912,128]{1,0:T(8,128)(2,1)S(1)}, u32[]{:S(2)}, u32[]{:S(2)}) %collective-permute-start) | collective-permute-done | bytes 233504 | tf_op jit(solution)/shard_map/ppermute | solution.py:432
  40.4 1.4 %first_node.1 = (f32[256,2,512]{2,1,0:T(2,128)}, f32[2,128,512]{2,1,0:T(8,128)S(1)}, f32[2,128,512]{2,1,0:T(8,128)S(1)}) custom-call(s32[1]{0:T(128)} %bitcast.place_ref, f32[2,256,512]{2,1,0:T(8,128)S(1)} %get-tuple-element.13.part_ref, bf16[2,512,512]{2,1,0:T(8,128)(2,1)S(1)} %get-tuple-element.15.plain_ref, ...), custom_call_target="tpu_custom_call" | custom-call | flops 268435456 | bytes 1048576 | tf_op jit(solution)/shard_map/first_node/pallas_call | solution.py:435
  41.8 0.6 %collective-permute-start.4 = (f32[2,128,512]{2,1,0:T(8,128)S(1)}, f32[2,128,512]{2,1,0:T(8,128)S(1)}, u32[]{:S(2)}, u32[]{:S(2)}) collective-permute-start(f32[2,128,512]{2,1,0:T(8,128)S(1)} %get-tuple-element.23.node_ref), channel_id=1, source_target_pairs={{0,2},{2,0},{4,6},{6,4},{8,10},{10,8},{12,14},{14,12},{16,18},{18,... | collective-permute-start | bytes 1572872 | tf_op jit(solution)/shard_map/ppermute | solution.py:443
  42.4 0.0 collective-permute-start.2
  42.4 1.2 %collective-permute-start.1 = (s16[656,128]{1,0:T(8,128)(2,1)S(1)}, s16[656,128]{1,0:T(8,128)(2,1)S(1)}, u32[]{:S(2)}, u32[]{:S(2)}) collective-permute-start(s16[656,128]{1,0:T(8,128)(2,1)S(1)} %get-tuple-element.19), channel_id=1, source_target_pairs={{0,1},{1,0},{2,3},{3,2},{4,5},{5,4},{6,7},{7,6},{8,9},{9,8},{10,11... | collective-permute-start | bytes 503816 | tf_op jit(solution)/shard_map/ppermute | solution.py:433
  43.6 4.1 %collective-permute-done.1.code_ref = s16[656,128]{1,0:T(8,128)(2,1)S(1)} collective-permute-done((s16[656,128]{1,0:T(8,128)(2,1)S(1)}, s16[656,128]{1,0:T(8,128)(2,1)S(1)}, u32[]{:S(2)}, u32[]{:S(2)}) %collective-permute-start.1) | collective-permute-done | bytes 167968 | tf_op jit(solution)/shard_map/ppermute | solution.py:433
  47.7 1.4 %collective-permute-start.3 = (s16[656,128]{1,0:T(8,128)(2,1)S(1)}, s16[656,128]{1,0:T(8,128)(2,1)S(1)}, u32[]{:S(2)}, u32[]{:S(2)}) collective-permute-start(s16[656,128]{1,0:T(8,128)(2,1)S(1)} %collective-permute-done.1.code_ref), channel_id=1, source_target_pairs={{0,2},{2,0},{4,6},{6,4},{8,10},{10,8},{12,14},{14,12},{16,18},{18,... | collective-permute-start | bytes 503816 | tf_op jit(solution)/shard_map/ppermute | solution.py:449
  49.1 1.2 %second_node.1 = (f32[256,2,512]{2,1,0:T(2,128)}, f32[2,128,512]{2,1,0:T(8,128)S(1)}) custom-call(s32[1]{0:T(128)} %bitcast.place_ref, f32[2,128,512]{2,1,0:T(8,128)S(1)} %get-tuple-element.18.rest_ref, s16[656,128]{1,0:T(8,128)(2,1)S(1)} %collective-permute-done.1.code_ref, f32[256,2,512]{2,1,0:T(2,128)} %get-tuple-element.20._), custom_call_target="tpu_custom_call", output_to_operand_aliasing={{0}: (3, {})} | custom-call | bytes 1048576 | tf_op jit(solution)/shard_map/second_node/pallas_call | solution.py:451
  50.3 0.0 collective-permute-done.4.partner_ref
  50.3 0.0 copy-done
  50.3 1.5 %first_merge.1._ = f32[256,2,512]{2,1,0:T(2,128)} custom-call(s32[1,2]{1,0:T(1,128)S(1)} %copy-done, f32[2,128,512]{2,1,0:T(8,128)S(1)} %get-tuple-element.23.node_ref, f32[2,128,512]{2,1,0:T(8,128)S(1)} %collective-permute-done.4.partner_ref), custom_call_target="tpu_custom_call" | custom-call | bytes 1048576 | tf_op jit(solution)/shard_map/first_merge/pallas_call | solution.py:446
  51.7 0.0 collective-permute-done.3.code_ref
  51.7 0.0 collective-permute-done.2.rest_ref
  51.7 1.8 %second_merge.1 = f32[256,2,512]{2,1,0:T(2,128)} custom-call(s32[1]{0:T(128)} %bitcast.place_ref, s32[1,2]{1,0:T(1,128)S(1)} %copy-done, f32[2,128,512]{2,1,0:T(8,128)S(1)} %get-tuple-element.22.node_ref, f32[2,128,512]{2,1,0:T(8,128)S(1)} %collective-permute-done.2.rest_ref, ...), custom_call_target="tpu_custom_call", output_to_operand_aliasing={{}: (5, {})} | custom-call | bytes 1048576 | tf_op jit(solution)/shard_map/second_merge/pallas_call | solution.py:460
Async XLA Ops:
  4.9 26.8 %all-to-all-start = ((bf16[16,200,128]{2,1,0:T(8,128)(2,1)}), bf16[16,200,128]{2,1,0:T(8,128)(2,1)S(1)}, u32[]{:S(2)}, u32[]{:S(2)}) async-start(bf16[16,200,128]{2,1,0:T(8,128)(2,1)} %bucket.1), calls=%async_computation | async-start | bytes 1638400 | tf_op jit(solution)/shard_map/all_to_all | solution.py:497
  12.7 2.2 %copy-start.1 = (bf16[2,8,256,512]{3,2,1,0:T(8,128)(2,1)S(1)}, bf16[2,8,256,512]{3,2,1,0:T(8,128)(2,1)}, u32[]{:S(2)}) copy-start(bf16[2,8,256,512]{3,2,1,0:T(8,128)(2,1)} %rows_ref.1) | copy-start | bytes 12582916
  14.9 0.7 %copy-start.2 = (bf16[2,8,256]{2,1,0:T(8,128)(2,1)S(1)}, bf16[2,8,256]{2,1,0:T(8,128)(2,1)}, u32[]{:S(2)}) copy-start(bf16[2,8,256]{2,1,0:T(8,128)(2,1)} %weight_ref.1) | copy-start | bytes 24580
  15.5 0.7 %copy-start.3 = (s32[2]{0:T(128)S(1)}, s32[2]{0:T(128)}, u32[]{:S(2)}) copy-start(s32[2]{0:T(128)} %branching_ref.1) | copy-start | bytes 28
  22.1 28.1 %copy-start = (s32[1,2]{1,0:T(1,128)S(1)}, s32[1,2]{1,0:T(1,128)}, u32[]{:S(2)}) copy-start(s32[1,2]{1,0:T(1,128)} %sibling_ref.3) | copy-start | bytes 28
  32.8 7.6 %collective-permute-start = (s16[912,128]{1,0:T(8,128)(2,1)S(1)}, s16[912,128]{1,0:T(8,128)(2,1)S(1)}, u32[]{:S(2)}, u32[]{:S(2)}) collective-permute-start(s16[912,128]{1,0:T(8,128)(2,1)S(1)} %get-tuple-element.17), channel_id=1, source_target_pairs={{0,1},{1,0},{2,3},{3,2},{4,5},{5,4},{6,7},{7,6},{8,9},{9,8},{10,11... | collective-permute-start | bytes 700424 | tf_op jit(solution)/shard_map/ppermute | solution.py:432
  41.8 8.5 %collective-permute-start.4 = (f32[2,128,512]{2,1,0:T(8,128)S(1)}, f32[2,128,512]{2,1,0:T(8,128)S(1)}, u32[]{:S(2)}, u32[]{:S(2)}) collective-permute-start(f32[2,128,512]{2,1,0:T(8,128)S(1)} %get-tuple-element.23.node_ref), channel_id=1, source_target_pairs={{0,2},{2,0},{4,6},{6,4},{8,10},{10,8},{12,14},{14,12},{16,18},{18,... | collective-permute-start | bytes 1572872 | tf_op jit(solution)/shard_map/ppermute | solution.py:443
  42.4 9.4 %collective-permute-start.2 = (f32[2,128,512]{2,1,0:T(8,128)S(1)}, f32[2,128,512]{2,1,0:T(8,128)S(1)}, u32[]{:S(2)}, u32[]{:S(2)}) collective-permute-start(f32[2,128,512]{2,1,0:T(8,128)S(1)} %get-tuple-element.18.rest_ref), channel_id=1, source_target_pairs={{0,2},{2,0},{4,6},{6,4},{8,10},{10,8},{12,14},{14,12},{16,18},{18,... | collective-permute-start | bytes 1572872 | tf_op jit(solution)/shard_map/ppermute | solution.py:444
  42.4 5.3 %collective-permute-start.1 = (s16[656,128]{1,0:T(8,128)(2,1)S(1)}, s16[656,128]{1,0:T(8,128)(2,1)S(1)}, u32[]{:S(2)}, u32[]{:S(2)}) collective-permute-start(s16[656,128]{1,0:T(8,128)(2,1)S(1)} %get-tuple-element.19), channel_id=1, source_target_pairs={{0,1},{1,0},{2,3},{3,2},{4,5},{5,4},{6,7},{7,6},{8,9},{9,8},{10,11... | collective-permute-start | bytes 503816 | tf_op jit(solution)/shard_map/ppermute | solution.py:433
  47.7 4.0 %collective-permute-start.3 = (s16[656,128]{1,0:T(8,128)(2,1)S(1)}, s16[656,128]{1,0:T(8,128)(2,1)S(1)}, u32[]{:S(2)}, u32[]{:S(2)}) collective-permute-start(s16[656,128]{1,0:T(8,128)(2,1)S(1)} %collective-permute-done.1.code_ref), channel_id=1, source_target_pairs={{0,2},{2,0},{4,6},{6,4},{8,10},{10,8},{12,14},{14,12},{16,18},{18,... | collective-permute-start | bytes 503816 | tf_op jit(solution)/shard_map/ppermute | solution.py:449

commit v4 on v3

--- a/solution.py
+++ b/solution.py
@@ -13,9 +13,11 @@
 LANES = 128
 GROUP = 16
 EXTRA = 8
+PIECES = 4
 VMEM = pl.BlockSpec(memory_space=pltpu.VMEM)
 SMEM = pl.BlockSpec(memory_space=pltpu.SMEM)
 CODE = 32000.0
+LONG = 20_000_000_000
 
 
 class Plan:
@@ -43,7 +45,7 @@
     return lax.dot_general(a, b, (((0,), (0,)), ((), ())), preferred_element_type=F32)
 
 
-def bucket_kernel(plan, route_hbm, weight_hbm, rows_hbm, out_ref, route_ref, weight_ref, rows_ref, sems):
+def bucket_kernel(plan, route_hbm, weight_hbm, rows_hbm, out_hbm, route_ref, weight_ref, rows_ref, out_ref, sems):
     count = rows_hbm.shape[0]
     state = plan.state
     copies = [
@@ -69,14 +71,9 @@
         q * plan.full + position,
         plan.node_dev * plan.full + q * plan.rest + position - plan.full,
     )
-    total = plan.leaf_count * plan.rows
-    hit = jnp.where(lax.broadcasted_iota(I32, (total, count), 0) == slot, 1.0, 0.0).astype(BF16)
     copies[1].wait()
-    rows_ref[:, state:] = dot_t(weight_ref[...], jnp.ones((1, LANES), BF16)).astype(BF16)
-    copies[2].wait()
-    filled = jnp.dot(hit, rows_ref[...], preferred_element_type=F32)
-    weights = filled[:, state:]
-    filled = filled[:, :state].astype(BF16)
+    weight = weight_ref[...].reshape(1, count)
+    rows_ref[:, state:] = dot_t(weight, jnp.ones((1, LANES), BF16)).astype(BF16)
     lane = lax.broadcasted_iota(I32, (EXTRA, LANES), 1)
     sub = lax.broadcasted_iota(I32, (EXTRA, LANES), 0)
     want = []
@@ -87,16 +84,31 @@
             if step:
                 q_of = q_of + jnp.where(sub >= i, step, 0)
         want.append(lane == g * plan.node_dev + q_of)
-    for d in range(plan.leaf_count):
-        at = d * plan.rows
-        for c in range(plan.slabs):
-            out_ref[d, c * plan.rows : (c + 1) * plan.rows, :] = filled[
-                at : at + plan.rows, c * LANES : (c + 1) * LANES
-            ]
-        extra = jnp.zeros((EXTRA, LANES), F32)
-        for g in range(plan.rows // EXTRA):
-            extra = jnp.where(want[g], weights[at + g * EXTRA : at + (g + 1) * EXTRA, :], extra)
-        out_ref[d, plan.slabs * plan.rows :, :] = extra.astype(BF16)
+    copies[2].wait()
+    each = plan.leaf_count // PIECES
+    leaving = []
+    for p in range(PIECES):
+        place = lax.broadcasted_iota(I32, (each * plan.rows, count), 0) + p * each * plan.rows
+        hit = jnp.where(place == slot, 1.0, 0.0).astype(BF16)
+        filled = jnp.dot(hit, rows_ref[...], preferred_element_type=F32)
+        weights = filled[:, state:]
+        filled = filled[:, :state].astype(BF16)
+        for i in range(each):
+            at = i * plan.rows
+            d = p * each + i
+            for c in range(plan.slabs):
+                out_ref[d, c * plan.rows : (c + 1) * plan.rows, :] = filled[
+                    at : at + plan.rows, c * LANES : (c + 1) * LANES
+                ]
+            extra = jnp.zeros((EXTRA, LANES), F32)
+            for g in range(plan.rows // EXTRA):
+                extra = jnp.where(want[g], weights[at + g * EXTRA : at + (g + 1) * EXTRA, :], extra)
+            out_ref[d, plan.slabs * plan.rows :, :] = extra.astype(BF16)
+        span = pl.ds(p * each, each)
+        leaving.append(pltpu.make_async_copy(out_ref.at[span], out_hbm.at[span], sems.at[3 + p]))
+        leaving[-1].start()
+    for copy in leaving:
+        copy.wait()
 
 
 def leaf_kernel(place_ref, branching_ref, weight_ref, rows_ref, block_ref, own_ref, send_ref, total):
@@ -211,9 +223,8 @@
     return values
 
 
-def send_folded(plan, place_ref, got_ref, part_ref, first_ref, second_ref, plain_ref, scaled_ref):
+def send_folded(plan, place_ref, got_ref, part_ref, code_ref, plain_ref, scaled_ref):
     share = part_ref.shape[2]
-    half = share // 2
     mine = pl.ds(pl.multiple_of(place_ref[0] * share, share), share)
     theirs = pl.ds(pl.multiple_of((1 - place_ref[0]) * share, share), share)
     gather_rows(plan, got_ref, plain_ref, scaled_ref)
@@ -222,100 +233,87 @@
         scaled = scaled_ref[q, :, theirs]
         square.append(part_ref[0, q, :, theirs] + dot_t(scaled, plain_ref[q, :, theirs]))
         beside.append(part_ref[0, q, :, mine] + dot_t(scaled, plain_ref[q, :, mine]))
-    up, low = slice(0, half), slice(half, share)
-    encode_part(
-        first_ref, square[0][up, up], square[1][up, up], [s[up, low] for s in square] + [s[up, :] for s in beside]
-    )
-    encode_part(second_ref, square[0][low, low], square[1][low, low], [s[low, :] for s in beside])
-
-
-def encode_part(code_ref, upper, lower, others):
-    half = upper.shape[0]
-    width = upper.shape[1]
-    pieces = [o[:, c : c + width] for o in others for c in range(0, o.shape[1], width)]
-    most = jnp.maximum(jnp.abs(upper), jnp.abs(lower))
-    for piece in pieces:
-        most = jnp.maximum(most, jnp.abs(piece))
+    most = jnp.maximum(
+        jnp.maximum(jnp.abs(square[0]), jnp.abs(square[1])),
+        jnp.maximum(jnp.abs(beside[0]), jnp.abs(beside[1])),
+    )
     power, factor = scale_of(jnp.max(most, axis=1, keepdims=True))
-    row = lax.broadcasted_iota(I32, (half, width), 0)
-    column = lax.broadcasted_iota(I32, (half, width), 1)
-    lower = lower * factor
-    code_ref[:half, :] = to_code(jnp.where(column >= row, upper * factor, lower))
-    for k, piece in enumerate(pieces):
-        code_ref[(k + 1) * half : (k + 2) * half, :] = to_code(piece * factor)
+    row = lax.broadcasted_iota(I32, (share, share), 0)
+    column = lax.broadcasted_iota(I32, (share, share), 1)
+    lower = square[1] * factor
+    code_ref[:share, :] = to_code(jnp.where(column >= row, square[0] * factor, lower))
+    for q in range(2):
+        code_ref[(q + 1) * share : (q + 2) * share, :] = to_code(beside[q] * factor)
     corner = jnp.sum(jnp.where(column == row, jnp.round(lower), 0.0), axis=0, keepdims=True)
-    line = lax.broadcasted_iota(I32, (GROUP, width), 0)
-    code_ref[(len(pieces) + 1) * half :, :] = to_code(
+    line = lax.broadcasted_iota(I32, (GROUP, share), 0)
+    code_ref[3 * share :, :] = to_code(
         jnp.where(line == 0, as_line(power), jnp.where(line == 1, corner, 0.0))
     )
 
 
-def decode_part(code_ref):
-    width = code_ref.shape[1]
-    half = width
-    count = code_ref.shape[0] // half
-    lines = from_code(code_ref[count * half :, :])
-    step = jnp.exp2(0.125 * as_column(lines[0:1, :])) * (1.0 / CODE)
-    pieces = [from_code(code_ref[k * half : (k + 1) * half, :]) * step for k in range(count)]
-    both = pieces[0]
+def decode_folded(code_ref):
+    share = code_ref.shape[1]
+    lines = from_code(code_ref[3 * share :, :])
+    step = jnp.transpose(jnp.exp2(0.125 * jnp.broadcast_to(lines[0:1, :], (8, share))) * (1.0 / CODE))[:, 0:1]
+    both = from_code(code_ref[:share, :]) * step
     turned = jnp.transpose(both)
-    corner = as_column(lines[1:2, :]) * step
-    row = lax.broadcasted_iota(I32, (half, width), 0)
-    column = lax.broadcasted_iota(I32, (half, width), 1)
-    squares = [
+    row = lax.broadcasted_iota(I32, (share, share), 0)
+    column = lax.broadcasted_iota(I32, (share, share), 1)
+    return step, (
         jnp.where(column >= row, both, turned),
-        jnp.where(column < row, both, jnp.where(column == row, corner, turned)),
-    ]
-    return squares, pieces[1:]
-
-
-def first_node_kernel(
-    place_ref, part_ref, plain_ref, scaled_ref, code_ref, out_ref, node_ref, rest_ref
-):
-    share = part_ref.shape[1]
-    half = share // 2
-    at = pl.multiple_of(place_ref[0] * share, share)
-    to = pl.multiple_of((1 - place_ref[0]) * share, share)
-    squares, pieces = decode_part(code_ref)
-    for q in range(2):
-        own = part_ref[q] + dot_t(scaled_ref[q, :, pl.ds(at, share)], plain_ref[q])
-        node_ref[q] = own[:half, :]
-        rest_ref[q] = own[half:, :]
-        node_ref[q, :, pl.ds(at, half)] += squares[q]
-        node_ref[q, :, pl.ds(at + half, half)] += pieces[q]
-        node_ref[q, :, pl.ds(to, half)] += pieces[2 + 2 * q]
-        node_ref[q, :, pl.ds(to + half, half)] += pieces[3 + 2 * q]
-        rest_ref[q, :, pl.ds(at, half)] += jnp.transpose(pieces[q])
-        out_ref[:, q, :] = node_ref[q]
-
-
-def add_second(place, code_ref, rest_ref, node_ref):
-    half = rest_ref.shape[1]
-    at = pl.multiple_of(place * 2 * half, half)
-    to = pl.multiple_of((1 - place) * 2 * half, half)
-    squares, pieces = decode_part(code_ref)
-    for q in range(2):
-        node_ref[q] = rest_ref[q]
-        node_ref[q, :, pl.ds(at + half, half)] += squares[q]
-        node_ref[q, :, pl.ds(to, half)] += pieces[2 * q]
-        node_ref[q, :, pl.ds(to + half, half)] += pieces[2 * q + 1]
-
-
-def second_node_kernel(place_ref, rest_ref, code_ref, _, out_ref, node_ref):
-    add_second(place_ref[0], code_ref, rest_ref, node_ref)
-    for q in range(2):
-        out_ref[:, q, :] = node_ref[q]
-
-
-def first_merge_kernel(sibling_ref, node_ref, partner_ref, out_ref):
-    for q in range(2):
-        out_ref[:, q, :] = node_ref[q] + partner_ref[sibling_ref[0, q]]
-
-
-def second_merge_kernel(place_ref, sibling_ref, node_ref, rest_ref, code_ref, _, out_ref, partner_ref):
-    add_second(place_ref[0], code_ref, rest_ref, partner_ref)
-    for q in range(2):
-        out_ref[:, q, :] = node_ref[q] + partner_ref[sibling_ref[0, q]]
+        jnp.where(column < row, both, jnp.where(column == row, lines[1:2, :] * step, turned)),
+    )
+
+
+def leave(out_ref, out_hbm, sems, p):
+    each = out_ref.shape[0] // PIECES
+    span = pl.ds(p * each, each)
+    copy = pltpu.make_async_copy(out_ref.at[span], out_hbm.at[span], sems.at[p])
+    copy.start()
+    return copy
+
+
+def node_folded(place_ref, own_ref, code_ref, out_hbm, node_ref, out_ref, sems):
+    share = own_ref.shape[1]
+    mine = pl.ds(pl.multiple_of(place_ref[0] * share, share), share)
+    theirs = pl.ds(pl.multiple_of((1 - place_ref[0]) * share, share), share)
+    step, squares = decode_folded(code_ref)
+    each = share // PIECES
+    copies = []
+    for p in range(PIECES):
+        rows = slice(p * each, (p + 1) * each)
+        for q in range(2):
+            beside = from_code(code_ref[(q + 1) * share + p * each : (q + 1) * share + (p + 1) * each, :])
+            for columns, term in ((mine, squares[q][rows]), (theirs, beside * step[rows])):
+                value = own_ref[q, rows, columns] + term
+                out_ref[rows, q, columns] = value
+                node_ref[q, rows, columns] = value
+        copies.append(leave(out_ref, out_hbm, sems, p))
+    for copy in copies:
+        copy.wait()
+
+
+def merge_folded(place_ref, sibling_ref, node_ref, own_ref, code_ref, out_hbm, out_ref, sems):
+    share = node_ref.shape[1]
+    mine = pl.ds(pl.multiple_of(place_ref[0] * share, share), share)
+    theirs = pl.ds(pl.multiple_of((1 - place_ref[0]) * share, share), share)
+    step, squares = decode_folded(code_ref)
+    each = share // PIECES
+    copies = []
+    for p in range(PIECES):
+        rows = slice(p * each, (p + 1) * each)
+        for q in range(2):
+            match = sibling_ref[0, q]
+            square = jnp.where(match == 0, squares[0][rows], squares[1][rows])
+            at = pl.multiple_of((match + 1) * share + p * each, each)
+            beside = from_code(code_ref[pl.ds(at, each), :]) * step[rows]
+            for columns, term in ((mine, square), (theirs, beside)):
+                out_ref[rows, q, columns] = (
+                    node_ref[q, rows, columns] + own_ref[match, rows, columns] + term
+                )
+        copies.append(leave(out_ref, out_hbm, sems, p))
+    for copy in copies:
+        copy.wait()
 
 
 def own_kernel(place_ref, part_ref, plain_ref, scaled_ref, own_ref, total=None):
@@ -408,64 +406,46 @@
 
 def exchange_folded(plan, place, got, own_part, send_part, sibling):
     _, node_dev, share, state = send_part.shape
-    half = share // 2
     shape = jax.ShapeDtypeStruct
     depth = max(plan.depth)
     to_partner = [(i, i ^ 1) for i in range(plan.leaf_count)]
-    across = [(0, 1), (1, 0)]
     result = shape((share, node_dev, state), F32)
-    rows = shape((node_dev, half, state), F32)
+    rows = shape((node_dev, share, state), F32)
     any_spec = pl.BlockSpec(memory_space=pl.ANY)
-    part = [pl.BlockSpec((half, node_dev, state), lambda i, k=k: (k, 0, 0)) for k in range(2)]
+    scratch = [pltpu.VMEM((share, node_dev, state), F32), pltpu.SemaphoreType.DMA((PIECES,))]
     with jax.named_scope("routed_send"):
-        first, second, plain, scaled = call(
+        code, plain, scaled = call(
             functools.partial(send_folded, plan),
             (
-                shape((7 * half + GROUP, half), jnp.int16),
-                shape((5 * half + GROUP, half), jnp.int16),
+                shape((3 * share + GROUP, share), jnp.int16),
                 shape((node_dev, depth, state), BF16),
                 shape((node_dev, depth, state), BF16),
             ),
             [SMEM, VMEM, VMEM],
             flops=2 * node_dev * depth * share * state,
         )(place, got, send_part)
-    first = lax.ppermute(first, "blk", across)
-    second = lax.ppermute(second, "blk", across)
-    with jax.named_scope("first_node"):
-        node_schur, node, rest = call(
-            first_node_kernel,
-            (result, rows, rows),
-            [SMEM, VMEM, VMEM, VMEM, VMEM],
-            out_specs=(part[0], VMEM, VMEM),
-            grid=(1,),
-            flops=2 * node_dev * depth * share * state,
-        )(place, own_part, plain, scaled, first)
-    partner_node = lax.ppermute(node, "leaf", to_partner)
-    partner_rest = lax.ppermute(rest, "leaf", to_partner)
-    with jax.named_scope("first_merge"):
+    arrived = lax.ppermute(code, "blk", [(0, 1), (1, 0)])
+    with jax.named_scope("routed_own"):
+        own = call(own_kernel, rows, [SMEM, VMEM, VMEM, VMEM], flops=LONG)(place, own_part, plain, scaled)
+    partner_own = lax.ppermute(own, "leaf", to_partner)
+    partner_arrived = lax.ppermute(arrived, "leaf", to_partner)
+    with jax.named_scope("node"):
+        node_schur, node = call(
+            node_folded,
+            (result, rows),
+            [SMEM, VMEM, VMEM],
+            out_specs=(any_spec, VMEM),
+            scratch_shapes=scratch,
+            flops=LONG,
+        )(place, own, arrived)
+    with jax.named_scope("merge"):
         merged = call(
-            first_merge_kernel, result, [SMEM, VMEM, VMEM], out_specs=part[0], grid=(1,)
-        )(sibling, node, partner_node)
-    partner_second = lax.ppermute(second, "leaf", to_partner)
-    with jax.named_scope("second_node"):
-        node_schur, node = call(
-            second_node_kernel,
-            (result, rows),
-            [SMEM, VMEM, VMEM, any_spec],
-            out_specs=(part[1], VMEM),
-            grid=(1,),
-            input_output_aliases={3: 0},
-        )(place, rest, second, node_schur)
-    with jax.named_scope("second_merge"):
-        merged = call(
-            second_merge_kernel,
+            merge_folded,
             result,
-            [SMEM, SMEM, VMEM, VMEM, VMEM, any_spec],
-            out_specs=part[1],
-            grid=(1,),
-            scratch_shapes=[pltpu.VMEM((node_dev, half, state), F32)],
-            input_output_aliases={5: 0},
-        )(place, sibling, node, partner_rest, partner_second, merged)
+            [SMEM, SMEM, VMEM, VMEM, VMEM],
+            out_specs=any_spec,
+            scratch_shapes=scratch,
+        )(place, sibling, node, partner_own, partner_arrived)
     return node_schur, merged
 
 
@@ -487,13 +467,15 @@
             [any_spec, any_spec, any_spec],
             scratch_shapes=[
                 pltpu.VMEM((1, count), I32),
-                pltpu.VMEM((1, count), BF16),
+                pltpu.VMEM((count,), BF16),
                 pltpu.VMEM((count, state + LANES), BF16),
-                pltpu.SemaphoreType.DMA((3,)),
+                pltpu.VMEM((leaf_count, plan.block, LANES), BF16),
+                pltpu.SemaphoreType.DMA((3 + PIECES,)),
             ],
+            out_specs=any_spec,
             vmem=60 << 20,
             flops=2 * plan.leaf_count * plan.rows * count * state,
-        )(na_route.reshape(1, count), na_weight.reshape(1, count), na_rows)
+        )(na_route.reshape(1, count), na_weight, na_rows)
     got = lax.all_to_all(blocks, "leaf", split_axis=0, concat_axis=0, tiled=True)
 
     with jax.named_scope("leaf_products"):

time: 53.9 us -> 47.2 us (0.88)
  starting transfers between devices: 11.1 us -> 8.58 us
  waiting for transfers between devices: 20 us -> 18.2 us
  local copies, waits for them, and re-layouts: 5.89 us -> 4.63 us
  Pallas kernels: 15.8 us -> 14.7 us
    ppermute x5 -> x3, starting transfers between devices: 4.47 us -> 1.96 us  [the longest x1 1.27 us: exchange_folded(): arrived = lax.ppermute(code, 'blk', [(0, 1), (1, 0)])]
    pallas_call x5 -> x4, Pallas kernels: 6.84 us -> 5.3 us  [the longest x1 2.2 us: exchange_folded(): call(merge_folded, result, [SMEM, SMEM, VMEM, VMEM, VMEM], out_specs=any_...]
    reshape x1 -> x0, local copies, waits for them, and re-layouts: 1.26 us -> none  [shards(): na_weight.reshape(1, count)]
    ppermute x5 -> x3, waiting for transfers between devices: 10.4 us -> 9.33 us  [the longest x1 9.32 us: exchange_folded(): arrived = lax.ppermute(code, 'blk', [(0, 1), (1, 0)])]
    pallas_call x1, Pallas kernels: 5.92 us -> 6.73 us  [shards(): call(leaf_kernel, (shape((node_dev, share, state), F32), shape((peers, no...]
    all_to_all x1, waiting for transfers between devices: 9.63 us -> 8.84 us  [shards(): lax.all_to_all(blocks, 'leaf', split_axis=0, concat_axis=0, tiled=True)]
  transfers between devices with their start and end apart: 6 -> 4, of which waited for: 3 -> 2; matrix products, arithmetic and copies ran while one was open for 2% -> 2% of each run, Pallas kernels for 16% -> 19%
where the time goes in v4:
time: 47.2 us; the launch traced here: 46.8 us
  waiting for transfers between devices  18.2 us (39%)
  Pallas kernels  14.7 us (31%)
  starting transfers between devices  8.58 us (18%)
  local copies, waits for them, and re-layouts  4.63 us (10%)
  between operations  0.71 us (2%)
    ppermute x1, waiting for transfers between devices, exchange_folded(): arrived = lax.ppermute(code, 'blk', [(0, 1), (1, 0)])  9.32 us
    all_to_all x1, waiting for transfers between devices, shards(): lax.all_to_all(blocks, 'leaf', split_axis=0, concat_axis=0, tiled=True)  8.84 us
    pallas_call x1, Pallas kernels, shards(): call(leaf_kernel, (shape((node_dev, share, state), F32), shape((peers, no...  6.73 us
    all_to_all x1, starting transfers between devices, shards(): lax.all_to_all(blocks, 'leaf', split_axis=0, concat_axis=0, tiled=True)  6.62 us
    unnamed x9, local copies, waits for them, and re-layouts  4.63 us
    pallas_call x1, Pallas kernels, shards(): call(functools.partial(bucket_kernel, plan), shape((leaf_count, plan.bloc...  2.68 us
    pallas_call x1, Pallas kernels, exchange_folded(): call(merge_folded, result, [SMEM, SMEM, VMEM, VMEM, VMEM], out_specs=any_...  2.2 us
    pallas_call x1, Pallas kernels, exchange_folded(): call(node_folded, (result, rows), [SMEM, VMEM, VMEM], out_specs=(any_spec...  1.61 us
  transfers between devices with their start and end apart: 4, of which 2 were waited for; matrix products, arithmetic and copies ran while one was open for 2% of the time, Pallas kernels for 19%

profile of v4, /device:TPU:9, one launch (start us, length us, event | category | flops | bytes accessed | tf_op | source)
XLA Modules:
  0.0 46.8 jit_solution(4239671917578745587)
XLA Ops:
  0.6 2.7 %bucket.1 = bf16[16,200,128]{2,1,0:T(8,128)(2,1)} custom-call(s32[1,512]{1,0:T(1,128)} %bitcast.6, bf16[512]{0:T(512)(128)(2,1)} %weight_hbm.1, bf16[512,512]{1,0:T(8,128)(2,1)} %rows_hbm.1), custom_call_target="tpu_custom_call" | custom-call | flops 402653184 | bytes 1048576 | tf_op jit(solution)/shard_map/bucket/pallas_call | solution.py:464
  3.3 6.6 %all-to-all-start = ((bf16[16,200,128]{2,1,0:T(8,128)(2,1)}), bf16[16,200,128]{2,1,0:T(8,128)(2,1)S(1)}, u32[]{:S(2)}, u32[]{:S(2)}) async-start(bf16[16,200,128]{2,1,0:T(8,128)(2,1)} %bucket.1), calls=%async_computation | async-start | bytes 1638400 | tf_op jit(solution)/shard_map/all_to_all | solution.py:479
  9.9 1.1 %copy.12 = bf16[256,2,512]{2,0,1:T(8,128)(2,1)S(1)} copy(bf16[256,2,512]{2,1,0:T(2,128)(2,1)} %param.12) | data formatting | bytes 1048576 | tf_op args[4]
  11.0 0.0 copy-start.1
  11.0 2.2 %copy-done.1 = bf16[2,8,256,512]{3,2,1,0:T(8,128)(2,1)S(1)} copy-done((bf16[2,8,256,512]{3,2,1,0:T(8,128)(2,1)S(1)}, bf16[2,8,256,512]{3,2,1,0:T(8,128)(2,1)}, u32[]{:S(2)}) %copy-start.1) | copy-done | bytes 4194328
  13.2 0.0 copy-start.2
  13.2 0.7 %copy-done.2 = bf16[2,8,256]{2,1,0:T(8,128)(2,1)S(1)} copy-done((bf16[2,8,256]{2,1,0:T(8,128)(2,1)S(1)}, bf16[2,8,256]{2,1,0:T(8,128)(2,1)}, u32[]{:S(2)}) %copy-start.2) | copy-done | bytes 8216
  13.9 0.0 copy-start.3
  13.9 0.7 %copy-done.3 = s32[2]{0:T(128)S(1)} copy-done((s32[2]{0:T(128)S(1)}, s32[2]{0:T(128)}, u32[]{:S(2)}) %copy-start.3) | copy-done | bytes 32
  14.6 6.7 %leaf_products.1 = (f32[2,256,512]{2,1,0:T(8,128)S(1)}, f32[1,2,256,512]{3,2,1,0:T(8,128)S(1)}) custom-call(s32[1]{0:T(128)} %bitcast.place_ref, s32[2]{0:T(128)S(1)} %copy-done.3, bf16[2,8,256]{2,1,0:T(8,128)(2,1)S(1)} %copy-done.2, bf16[2,8,256,512]{3,2,1,0:T(8,128)(2,1)S(1)} %copy-done.1, bf16[2,256,512]{2,1,0:T(8,128)(2,1)S(1)} %bitcast.5), custom_call_target="tpu_custom_call" | custom-call | flops 2147483648 | bytes 8388608 | tf_op jit(solution)/shard_map/leaf_products/pallas_call | solution.py:482
  21.3 8.8 %all-to-all-done.got_ref = bf16[16,200,128]{2,1,0:T(8,128)(2,1)S(1)} async-done(((bf16[16,200,128]{2,1,0:T(8,128)(2,1)}), bf16[16,200,128]{2,1,0:T(8,128)(2,1)S(1)}, u32[]{:S(2)}, u32[]{:S(2)}) %all-to-all-start) | async-done | bytes 819232 | tf_op jit(solution)/shard_map/all_to_all | solution.py:479
  30.2 1.0 %routed_send.1 = (s16[784,256]{1,0:T(8,128)(2,1)S(1)}, bf16[2,512,512]{2,1,0:T(8,128)(2,1)S(1)}, bf16[2,512,512]{2,1,0:T(8,128)(2,1)S(1)}) custom-call(s32[1]{0:T(128)} %bitcast.place_ref, bf16[16,200,128]{2,1,0:T(8,128)(2,1)S(1)} %all-to-all-done.got_ref, f32[1,2,256,512]{3,2,1,0:T(8,128)S(1)} %get-tuple-element.10.part_ref), custom_call_target="tpu_custom_call" | custom-call | flops 268435456 | bytes 1048576 | tf_op jit(solution)/shard_map/routed_send/pallas_call | solution.py:417
  31.2 1.3 %collective-permute-start = (s16[784,256]{1,0:T(8,128)(2,1)S(1)}, s16[784,256]{1,0:T(8,128)(2,1)S(1)}, u32[]{:S(2)}, u32[]{:S(2)}) collective-permute-start(s16[784,256]{1,0:T(8,128)(2,1)S(1)} %get-tuple-element.13), channel_id=1, source_target_pairs={{0,1},{1,0},{2,3},{3,2},{4,5},{5,4},{6,7},{7,6},{8,9},{9,8},{10,11... | collective-permute-start | bytes 1204232 | tf_op jit(solution)/shard_map/ppermute | solution.py:427
  32.4 0.5 %routed_own.1.own_ref = f32[2,256,512]{2,1,0:T(8,128)S(1)} custom-call(s32[1]{0:T(128)} %bitcast.place_ref, f32[2,256,512]{2,1,0:T(8,128)S(1)} %get-tuple-element.9.part_ref, bf16[2,512,512]{2,1,0:T(8,128)(2,1)S(1)} %get-tuple-element.11.plain_ref, bf16[2,512,512]{2,1,0:T(8,128)(2,1)S(1)} %get-tuple-element.12.scaled_ref), custom_call_target="tpu_custom_call" | custom-call | flops 20000000000 | bytes 1048576 | tf_op jit(solution)/shard_map/routed_own/pallas_call | solution.py:429
  32.9 0.0 copy-start
  32.9 0.1 collective-permute-start.1
  33.0 9.3 %collective-permute-done.code_ref = s16[784,256]{1,0:T(8,128)(2,1)S(1)} collective-permute-done((s16[784,256]{1,0:T(8,128)(2,1)S(1)}, s16[784,256]{1,0:T(8,128)(2,1)S(1)}, u32[]{:S(2)}, u32[]{:S(2)}) %collective-permute-start) | collective-permute-done | bytes 401440 | tf_op jit(solution)/shard_map/ppermute | solution.py:427
  42.3 0.6 %collective-permute-start.2 = (s16[784,256]{1,0:T(8,128)(2,1)S(1)}, s16[784,256]{1,0:T(8,128)(2,1)S(1)}, u32[]{:S(2)}, u32[]{:S(2)}) collective-permute-start(s16[784,256]{1,0:T(8,128)(2,1)S(1)} %collective-permute-done.code_ref), channel_id=1, source_target_pairs={{0,2},{2,0},{4,6},{6,4},{8,10},{10,8},{12,14},{14,12},{16,18},{18,... | collective-permute-start | bytes 1204232 | tf_op jit(solution)/shard_map/ppermute | solution.py:431
  42.9 1.6 %node.1 = (f32[256,2,512]{2,1,0:T(2,128)}, f32[2,256,512]{2,1,0:T(8,128)S(1)}) custom-call(s32[1]{0:T(128)} %bitcast.place_ref, f32[2,256,512]{2,1,0:T(8,128)S(1)} %routed_own.1.own_ref, s16[784,256]{1,0:T(8,128)(2,1)S(1)} %collective-permute-done.code_ref), custom_call_target="tpu_custom_call" | custom-call | flops 20000000000 | bytes 1048576 | tf_op jit(solution)/shard_map/node/pallas_call | solution.py:433
  44.6 0.0 collective-permute-done.2.code_ref
  44.6 0.0 collective-permute-done.1.own_ref
  44.6 0.0 copy-done
  44.6 2.2 %merge.1 = f32[256,2,512]{2,1,0:T(2,128)} custom-call(s32[1]{0:T(128)} %bitcast.place_ref, s32[1,2]{1,0:T(1,128)S(1)} %copy-done, f32[2,256,512]{2,1,0:T(8,128)S(1)} %get-tuple-element.15.node_ref, f32[2,256,512]{2,1,0:T(8,128)S(1)} %collective-permute-done.1.own_ref, s16[784,256]{1,0:T(8,128)(2,1)S(1)} %collective-permute-done.2.code_ref), custom_call_target="tpu_custom_call" | custom-call | bytes 1048576 | tf_op jit(solution)/shard_map/merge/pallas_call | solution.py:442
Async XLA Ops:
  3.3 26.8 %all-to-all-start = ((bf16[16,200,128]{2,1,0:T(8,128)(2,1)}), bf16[16,200,128]{2,1,0:T(8,128)(2,1)S(1)}, u32[]{:S(2)}, u32[]{:S(2)}) async-start(bf16[16,200,128]{2,1,0:T(8,128)(2,1)} %bucket.1), calls=%async_computation | async-start | bytes 1638400 | tf_op jit(solution)/shard_map/all_to_all | solution.py:479
  11.0 2.2 %copy-start.1 = (bf16[2,8,256,512]{3,2,1,0:T(8,128)(2,1)S(1)}, bf16[2,8,256,512]{3,2,1,0:T(8,128)(2,1)}, u32[]{:S(2)}) copy-start(bf16[2,8,256,512]{3,2,1,0:T(8,128)(2,1)} %rows_ref.1) | copy-start | bytes 12582916
  13.2 0.7 %copy-start.2 = (bf16[2,8,256]{2,1,0:T(8,128)(2,1)S(1)}, bf16[2,8,256]{2,1,0:T(8,128)(2,1)}, u32[]{:S(2)}) copy-start(bf16[2,8,256]{2,1,0:T(8,128)(2,1)} %weight_ref.1) | copy-start | bytes 24580
  13.9 0.7 %copy-start.3 = (s32[2]{0:T(128)S(1)}, s32[2]{0:T(128)}, u32[]{:S(2)}) copy-start(s32[2]{0:T(128)} %branching_ref.1) | copy-start | bytes 28
  31.2 11.2 %collective-permute-start = (s16[784,256]{1,0:T(8,128)(2,1)S(1)}, s16[784,256]{1,0:T(8,128)(2,1)S(1)}, u32[]{:S(2)}, u32[]{:S(2)}) collective-permute-start(s16[784,256]{1,0:T(8,128)(2,1)S(1)} %get-tuple-element.13), channel_id=1, source_target_pairs={{0,1},{1,0},{2,3},{3,2},{4,5},{5,4},{6,7},{7,6},{8,9},{9,8},{10,11... | collective-permute-start | bytes 1204232 | tf_op jit(solution)/shard_map/ppermute | solution.py:427
  32.9 11.7 %copy-start = (s32[1,2]{1,0:T(1,128)S(1)}, s32[1,2]{1,0:T(1,128)}, u32[]{:S(2)}) copy-start(s32[1,2]{1,0:T(1,128)} %sibling_ref.1) | copy-start | bytes 28
  32.9 11.6 %collective-permute-start.1 = (f32[2,256,512]{2,1,0:T(8,128)S(1)}, f32[2,256,512]{2,1,0:T(8,128)S(1)}, u32[]{:S(2)}, u32[]{:S(2)}) collective-permute-start(f32[2,256,512]{2,1,0:T(8,128)S(1)} %routed_own.1.own_ref), channel_id=1, source_target_pairs={{0,2},{2,0},{4,6},{6,4},{8,10},{10,8},{12,14},{14,12},{16,18},{18,... | collective-permute-start | bytes 3145736 | tf_op jit(solution)/shard_map/ppermute | solution.py:430
  42.3 2.2 %collective-permute-start.2 = (s16[784,256]{1,0:T(8,128)(2,1)S(1)}, s16[784,256]{1,0:T(8,128)(2,1)S(1)}, u32[]{:S(2)}, u32[]{:S(2)}) collective-permute-start(s16[784,256]{1,0:T(8,128)(2,1)S(1)} %collective-permute-done.code_ref), channel_id=1, source_target_pairs={{0,2},{2,0},{4,6},{6,4},{8,10},{10,8},{12,14},{14,12},{16,18},{18,... | collective-permute-start | bytes 1204232 | tf_op jit(solution)/shard_map/ppermute | solution.py:431

commit v5 on v4

--- a/solution.py
+++ b/solution.py
@@ -17,15 +17,18 @@
 VMEM = pl.BlockSpec(memory_space=pltpu.VMEM)
 SMEM = pl.BlockSpec(memory_space=pltpu.SMEM)
 CODE = 32000.0
+SPLIT = ("outer", "inner")
+INNER = 4
 LONG = 20_000_000_000
 
 
 class Plan:
-    def __init__(self, leaf_count, node_dev, capacity, state):
+    def __init__(self, leaf_count, node_dev, capacity, state, unit, inner=0):
+        self.inner = inner
         self.leaf_count, self.node_dev, self.capacity, self.state = leaf_count, node_dev, capacity, state
         self.full = capacity // GROUP * GROUP
         self.rest = capacity - self.full
-        self.rows = -(-node_dev * capacity // GROUP) * GROUP
+        self.rows = -(-node_dev * capacity // unit) * unit
         self.groups = self.rows // GROUP
         self.slabs = state // LANES
         self.block = self.slabs * self.rows + EXTRA
@@ -34,6 +37,13 @@
             for q in range(node_dev)
         ]
         self.depth = [leaf_count * GROUP * len(g) for g in self.groups_of]
+
+    def block_of(self, node):
+        if not self.inner:
+            return node
+        group = node // (2 * self.inner) * (2 * self.inner)
+        leaf = node // 2
+        return group + (node - 2 * leaf) * self.inner + (leaf - group // 2)
 
     def node_at(self, row):
         if row < self.node_dev * self.full:
@@ -64,6 +74,7 @@
     member = lax.broadcasted_iota(I32, (nodes, count), 0) == route
     seen = jnp.dot(member.astype(BF16), before, preferred_element_type=F32)
     position = jnp.sum(jnp.where(member, seen, 0.0), axis=0, keepdims=True).astype(I32)
+    route = plan.block_of(route)
     owner = route // plan.node_dev
     q = route - owner * plan.node_dev
     slot = owner * plan.rows + jnp.where(
@@ -223,95 +234,202 @@
     return values
 
 
-def send_folded(plan, place_ref, got_ref, part_ref, code_ref, plain_ref, scaled_ref):
-    share = part_ref.shape[2]
-    mine = pl.ds(pl.multiple_of(place_ref[0] * share, share), share)
-    theirs = pl.ds(pl.multiple_of((1 - place_ref[0]) * share, share), share)
-    gather_rows(plan, got_ref, plain_ref, scaled_ref)
-    square, beside = [], []
-    for q in range(2):
-        scaled = scaled_ref[q, :, theirs]
-        square.append(part_ref[0, q, :, theirs] + dot_t(scaled, plain_ref[q, :, theirs]))
-        beside.append(part_ref[0, q, :, mine] + dot_t(scaled, plain_ref[q, :, mine]))
-    most = jnp.maximum(
-        jnp.maximum(jnp.abs(square[0]), jnp.abs(square[1])),
-        jnp.maximum(jnp.abs(beside[0]), jnp.abs(beside[1])),
-    )
+def encode_node(code_ref, square, beside):
+    half = code_ref.shape[1]
+    upper, lower = square[:half, :half], square[half:, half:]
+    pieces = [square[:half, half:]]
+    pieces += [beside[r : r + half, c : c + half] for r in (0, half) for c in (0, half)]
+    most = jnp.maximum(jnp.abs(upper), jnp.abs(lower))
+    for piece in pieces:
+        most = jnp.maximum(most, jnp.abs(piece))
     power, factor = scale_of(jnp.max(most, axis=1, keepdims=True))
-    row = lax.broadcasted_iota(I32, (share, share), 0)
-    column = lax.broadcasted_iota(I32, (share, share), 1)
-    lower = square[1] * factor
-    code_ref[:share, :] = to_code(jnp.where(column >= row, square[0] * factor, lower))
-    for q in range(2):
-        code_ref[(q + 1) * share : (q + 2) * share, :] = to_code(beside[q] * factor)
+    row = lax.broadcasted_iota(I32, (half, half), 0)
+    column = lax.broadcasted_iota(I32, (half, half), 1)
+    lower = lower * factor
+    code_ref[:half, :] = to_code(jnp.where(column >= row, upper * factor, lower))
+    for k, piece in enumerate(pieces):
+        code_ref[(k + 1) * half : (k + 2) * half, :] = to_code(piece * factor)
     corner = jnp.sum(jnp.where(column == row, jnp.round(lower), 0.0), axis=0, keepdims=True)
-    line = lax.broadcasted_iota(I32, (GROUP, share), 0)
-    code_ref[3 * share :, :] = to_code(
+    line = lax.broadcasted_iota(I32, (GROUP, half), 0)
+    code_ref[6 * half :, :] = to_code(
         jnp.where(line == 0, as_line(power), jnp.where(line == 1, corner, 0.0))
     )
 
 
-def decode_folded(code_ref):
-    share = code_ref.shape[1]
-    lines = from_code(code_ref[3 * share :, :])
-    step = jnp.transpose(jnp.exp2(0.125 * jnp.broadcast_to(lines[0:1, :], (8, share))) * (1.0 / CODE))[:, 0:1]
-    both = from_code(code_ref[:share, :]) * step
+def decode_node(code_ref):
+    half = code_ref.shape[1]
+    lines = from_code(code_ref[6 * half :, :])
+    step = jnp.transpose(jnp.exp2(0.125 * jnp.broadcast_to(lines[0:1, :], (8, half))) * (1.0 / CODE))[:, 0:1]
+    pieces = [from_code(code_ref[k * half : (k + 1) * half, :]) * step for k in range(6)]
+    both = pieces[0]
     turned = jnp.transpose(both)
-    row = lax.broadcasted_iota(I32, (share, share), 0)
-    column = lax.broadcasted_iota(I32, (share, share), 1)
-    return step, (
-        jnp.where(column >= row, both, turned),
-        jnp.where(column < row, both, jnp.where(column == row, lines[1:2, :] * step, turned)),
-    )
-
-
-def leave(out_ref, out_hbm, sems, p):
-    each = out_ref.shape[0] // PIECES
-    span = pl.ds(p * each, each)
-    copy = pltpu.make_async_copy(out_ref.at[span], out_hbm.at[span], sems.at[p])
-    copy.start()
-    return copy
-
-
-def node_folded(place_ref, own_ref, code_ref, out_hbm, node_ref, out_ref, sems):
-    share = own_ref.shape[1]
-    mine = pl.ds(pl.multiple_of(place_ref[0] * share, share), share)
-    theirs = pl.ds(pl.multiple_of((1 - place_ref[0]) * share, share), share)
-    step, squares = decode_folded(code_ref)
+    row = lax.broadcasted_iota(I32, (half, half), 0)
+    column = lax.broadcasted_iota(I32, (half, half), 1)
+    upper = jnp.where(column >= row, both, turned)
+    lower = jnp.where(column < row, both, jnp.where(column == row, lines[1:2, :] * step, turned))
+    square = ((upper, pieces[1]), (jnp.transpose(pieces[1]), lower))
+    beside = ((pieces[2], pieces[3]), (pieces[4], pieces[5]))
+    return square, beside
+
+
+def halves(place, share):
+    mine = pl.ds(pl.multiple_of(place * share, share), share)
+    theirs = pl.ds(pl.multiple_of((1 - place) * share, share), share)
+    return mine, theirs
+
+
+def turned(rows, first, count):
+    width = rows.shape[1]
+    pick = lax.broadcasted_iota(I32, (count, width), 1) == lax.broadcasted_iota(I32, (count, width), 0) + first
+    return lax.dot_general(
+        jnp.where(pick, 1.0, 0.0).astype(BF16), rows, (((1,), (1,)), ((), ())), preferred_element_type=F32
+    )
+
+
+def leaf_sum(node, branching_ref, weight_hbm, rows_hbm, weight_ref, rows_ref, total, sems):
+    pairs = rows_hbm.shape[1] // 2
+    depth, state = rows_hbm.shape[2:]
+    count = branching_ref[node]
+    weights = pltpu.make_async_copy(weight_hbm.at[node], weight_ref, sems.at[pairs])
+    copies = [
+        pltpu.make_async_copy(rows_hbm.at[node, pl.ds(2 * p, 2)], rows_ref.at[p], sems.at[p])
+        for p in range(pairs)
+    ]
+    copies[0].start()
+    weights.start()
+    for p in range(1, pairs):
+        pl.when(2 * p < count)(copies[p].start)
+    weights.wait()
+    live = lax.broadcasted_iota(I32, weight_ref.shape, 0) < count
+    factor = jnp.where(live, weight_ref[...].astype(F32), 0.0)
+
+    def term(p):
+        copies[p].wait()
+        rows = rows_ref[p].reshape(2 * depth, state)
+        weight = jnp.concatenate([factor[2 * p : 2 * p + 1, :], factor[2 * p + 1 : 2 * p + 2, :]], axis=1)
+        scaled = (turned(rows, 0, state) * weight).astype(BF16)
+        return jnp.dot(scaled, rows, preferred_element_type=F32)
+
+    total[...] = term(0)
+    for p in range(1, pairs):
+
+        @pl.when(2 * p < count)
+        def _():
+            total[...] += term(p)
+
+
+def far_leaf_kernel(
+    branching_ref, weight_hbm, rows_hbm, own_ref, code_ref, weight_ref, rows_ref, total, sems
+):
+    share = own_ref.shape[0]
+    mine, theirs = halves(lax.axis_index("blk"), share)
+    node = 1 - lax.axis_index("blk")
+    leaf_sum(node, branching_ref, weight_hbm, rows_hbm, weight_ref, rows_ref, total, sems)
+    encode_node(code_ref, total[theirs, theirs], total[theirs, mine])
+    own_ref[...] = total[mine, :]
+
+
+def near_leaf_kernel(
+    branching_ref, weight_hbm, rows_hbm, block_ref, far_ref,
+    own_ref, send_ref, far_out, weight_ref, rows_ref, total, sems,
+):
+    share = own_ref.shape[0]
+    mine, theirs = halves(lax.axis_index("blk"), share)
+    node = lax.axis_index("blk")
+    leaf_sum(node, branching_ref, weight_hbm, rows_hbm, weight_ref, rows_ref, total, sems)
+    send_ref[...] = total[theirs, :]
+    own_ref[...] = total[mine, :] + block_ref[node].astype(F32)
+    far_out[...] = far_ref[...] + block_ref[1 - node].astype(F32)
+
+
+def send_folded(plan, got_ref, part_ref, code_ref, plain_ref, scaled_ref):
+    share = part_ref.shape[0]
+    mine, theirs = halves(lax.axis_index("blk"), share)
+    cap = plan.rows
+    for d in range(0, plan.leaf_count, 2):
+        blocks = [got_ref[d + i].astype(F32) for i in range(2)]
+        weight = jnp.concatenate(
+            [
+                block[plan.slabs * cap :, g : g + 1]
+                for block in blocks
+                for g in range(cap // EXTRA)
+            ],
+            axis=0,
+        )
+        at = d * cap
+        for c in range(plan.slabs):
+            rows = jnp.concatenate([block[c * cap : (c + 1) * cap, :] for block in blocks], axis=0)
+            plain_ref[at : at + 2 * cap, c * LANES : (c + 1) * LANES] = rows.astype(BF16)
+            scaled_ref[at : at + 2 * cap, c * LANES : (c + 1) * LANES] = (rows * weight).astype(BF16)
+    scaled = turned(scaled_ref[...], (1 - lax.axis_index("blk")) * share, share).astype(BF16)
+    encode_node(
+        code_ref,
+        part_ref[:, theirs] + jnp.dot(scaled, plain_ref[:, theirs], preferred_element_type=F32),
+        part_ref[:, mine] + jnp.dot(scaled, plain_ref[:, mine], preferred_element_type=F32),
+    )
+
+
+def in_columns(place, square, beside):
+    first = place == 0
+    return [
+        [jnp.where(first, s, b) for s, b in zip(*pair)] + [jnp.where(first, b, s) for s, b in zip(*pair)]
+        for pair in zip(square, beside)
+    ]
+
+
+def tiles_of(ref):
+    half = ref.shape[0] // 2
+    for i in range(2):
+        for k in range(ref.shape[1] // half):
+            yield i, k, slice(i * half, (i + 1) * half), slice(k * half, (k + 1) * half)
+
+
+def near_node_kernel(own_ref, plain_ref, scaled_ref, code_ref, node_ref):
+    share = own_ref.shape[0]
+    scaled = turned(scaled_ref[...], lax.axis_index("blk") * share, share).astype(BF16)
+    node_ref[...] = own_ref[...] + jnp.dot(scaled, plain_ref[...], preferred_element_type=F32)
+    terms = in_columns(lax.axis_index("blk"), *decode_node(code_ref))
+    for i, k, rows, columns in tiles_of(node_ref):
+        node_ref[rows, columns] += terms[i][k]
+
+
+def far_node_kernel(near_ref, own_ref, code_ref, node_ref, out_ref):
+    first = lax.axis_index("blk") == 0
+    terms = in_columns(lax.axis_index("blk"), *decode_node(code_ref))
+    for i, k, rows, columns in tiles_of(node_ref):
+        far = own_ref[rows, columns] + terms[i][k]
+        near = near_ref[rows, columns]
+        node_ref[rows, columns] = far
+        out_ref[rows, 0, columns] = jnp.where(first, near, far)
+        out_ref[rows, 1, columns] = jnp.where(first, far, near)
+
+
+def merge_folded(
+    sibling_ref, near_ref, far_ref, node_ref, their_near_ref, their_own_ref, code_ref,
+    node_hbm, out_hbm, out_ref, sems,
+):
+    share = far_ref.shape[0]
+    half = share // 2
     each = share // PIECES
-    copies = []
+    copies = [pltpu.make_async_copy(node_ref, node_hbm, sems.at[PIECES])]
+    copies[0].start()
+    first = lax.axis_index("blk") == 0
+    straight = jnp.broadcast_to(sibling_ref[0:1, 0:1], (each, LANES)) == 0
+    terms = in_columns(lax.axis_index("blk"), *decode_node(code_ref))
     for p in range(PIECES):
         rows = slice(p * each, (p + 1) * each)
-        for q in range(2):
-            beside = from_code(code_ref[(q + 1) * share + p * each : (q + 1) * share + (p + 1) * each, :])
-            for columns, term in ((mine, squares[q][rows]), (theirs, beside * step[rows])):
-                value = own_ref[q, rows, columns] + term
-                out_ref[rows, q, columns] = value
-                node_ref[q, rows, columns] = value
-        copies.append(leave(out_ref, out_hbm, sems, p))
-    for copy in copies:
-        copy.wait()
-
-
-def merge_folded(place_ref, sibling_ref, node_ref, own_ref, code_ref, out_hbm, out_ref, sems):
-    share = node_ref.shape[1]
-    mine = pl.ds(pl.multiple_of(place_ref[0] * share, share), share)
-    theirs = pl.ds(pl.multiple_of((1 - place_ref[0]) * share, share), share)
-    step, squares = decode_folded(code_ref)
-    each = share // PIECES
-    copies = []
-    for p in range(PIECES):
-        rows = slice(p * each, (p + 1) * each)
-        for q in range(2):
-            match = sibling_ref[0, q]
-            square = jnp.where(match == 0, squares[0][rows], squares[1][rows])
-            at = pl.multiple_of((match + 1) * share + p * each, each)
-            beside = from_code(code_ref[pl.ds(at, each), :]) * step[rows]
-            for columns, term in ((mine, square), (theirs, beside)):
-                out_ref[rows, q, columns] = (
-                    node_ref[q, rows, columns] + own_ref[match, rows, columns] + term
-                )
-        copies.append(leave(out_ref, out_hbm, sems, p))
+        inner = slice(p * each % half, p * each % half + each)
+        for k in range(far_ref.shape[1] // half):
+            columns = slice(k * half, (k + 1) * half)
+            their_near = their_near_ref[rows, columns]
+            their_far = their_own_ref[rows, columns] + terms[p * each // half][k][inner]
+            near = near_ref[rows, columns] + jnp.where(straight, their_near, their_far)
+            far = far_ref[rows, columns] + jnp.where(straight, their_far, their_near)
+            out_ref[rows, 0, columns] = jnp.where(first, near, far)
+            out_ref[rows, 1, columns] = jnp.where(first, far, near)
+        span = pl.ds(p * each, each)
+        copies.append(pltpu.make_async_copy(out_ref.at[span], out_hbm.at[span], sems.at[p]))
+        copies[-1].start()
     for copy in copies:
         copy.wait()
 
@@ -404,80 +522,38 @@
     return node_schur, merged
 
 
-def exchange_folded(plan, place, got, own_part, send_part, sibling):
-    _, node_dev, share, state = send_part.shape
-    shape = jax.ShapeDtypeStruct
-    depth = max(plan.depth)
-    to_partner = [(i, i ^ 1) for i in range(plan.leaf_count)]
-    result = shape((share, node_dev, state), F32)
-    rows = shape((node_dev, share, state), F32)
+def bucket(plan, na_route, na_weight, na_rows):
+    count, state = na_rows.shape
     any_spec = pl.BlockSpec(memory_space=pl.ANY)
-    scratch = [pltpu.VMEM((share, node_dev, state), F32), pltpu.SemaphoreType.DMA((PIECES,))]
-    with jax.named_scope("routed_send"):
-        code, plain, scaled = call(
-            functools.partial(send_folded, plan),
-            (
-                shape((3 * share + GROUP, share), jnp.int16),
-                shape((node_dev, depth, state), BF16),
-                shape((node_dev, depth, state), BF16),
-            ),
-            [SMEM, VMEM, VMEM],
-            flops=2 * node_dev * depth * share * state,
-        )(place, got, send_part)
-    arrived = lax.ppermute(code, "blk", [(0, 1), (1, 0)])
-    with jax.named_scope("routed_own"):
-        own = call(own_kernel, rows, [SMEM, VMEM, VMEM, VMEM], flops=LONG)(place, own_part, plain, scaled)
-    partner_own = lax.ppermute(own, "leaf", to_partner)
-    partner_arrived = lax.ppermute(arrived, "leaf", to_partner)
-    with jax.named_scope("node"):
-        node_schur, node = call(
-            node_folded,
-            (result, rows),
-            [SMEM, VMEM, VMEM],
-            out_specs=(any_spec, VMEM),
-            scratch_shapes=scratch,
-            flops=LONG,
-        )(place, own, arrived)
-    with jax.named_scope("merge"):
-        merged = call(
-            merge_folded,
-            result,
-            [SMEM, SMEM, VMEM, VMEM, VMEM],
-            out_specs=any_spec,
-            scratch_shapes=scratch,
-        )(place, sibling, node, partner_own, partner_arrived)
-    return node_schur, merged
-
-
-def shards(leaf_rows, leaf_weight, branching, sibling, node_block, na_rows, na_weight, na_route):
-    leaf_count, blk_count = lax.axis_size("leaf"), lax.axis_size("blk")
-    node_dev, most_children, depth, state = leaf_rows.shape
-    count = na_rows.shape[0]
-    share = state // blk_count
-    peers = blk_count - 1
-    plan = Plan(leaf_count, node_dev, 3 * count // (2 * leaf_count * node_dev), state)
-    place = lax.axis_index("blk").astype(I32).reshape(1)
-    shape = jax.ShapeDtypeStruct
-    any_spec = pl.BlockSpec(memory_space=pl.ANY)
-
     with jax.named_scope("bucket"):
-        blocks = call(
+        return call(
             functools.partial(bucket_kernel, plan),
-            shape((leaf_count, plan.block, LANES), BF16),
+            jax.ShapeDtypeStruct((plan.leaf_count, plan.block, LANES), BF16),
             [any_spec, any_spec, any_spec],
             scratch_shapes=[
                 pltpu.VMEM((1, count), I32),
                 pltpu.VMEM((count,), BF16),
                 pltpu.VMEM((count, state + LANES), BF16),
-                pltpu.VMEM((leaf_count, plan.block, LANES), BF16),
+                pltpu.VMEM((plan.leaf_count, plan.block, LANES), BF16),
                 pltpu.SemaphoreType.DMA((3 + PIECES,)),
             ],
             out_specs=any_spec,
             vmem=60 << 20,
             flops=2 * plan.leaf_count * plan.rows * count * state,
         )(na_route.reshape(1, count), na_weight, na_rows)
+
+
+def shards_plain(leaf_rows, leaf_weight, branching, sibling, node_block, na_rows, na_weight, na_route):
+    leaf_count, blk_count = lax.axis_size("leaf"), lax.axis_size("blk")
+    node_dev, most_children, depth, state = leaf_rows.shape
+    count = na_rows.shape[0]
+    share = state // blk_count
+    peers = blk_count - 1
+    plan = Plan(leaf_count, node_dev, 3 * count // (2 * leaf_count * node_dev), state, GROUP)
+    place = lax.axis_index("blk").astype(I32).reshape(1)
+    shape = jax.ShapeDtypeStruct
+    blocks = bucket(plan, na_route, na_weight, na_rows)
     got = lax.all_to_all(blocks, "leaf", split_axis=0, concat_axis=0, tiled=True)
-
     with jax.named_scope("leaf_products"):
         own_part, send_part = call(
             leaf_kernel,
@@ -498,26 +574,117 @@
             flops=2 * node_dev * most_children * depth * state * state,
             moved=8 << 20,
         )(place, branching, leaf_weight, leaf_rows, jnp.transpose(node_block, (1, 0, 2)))
-
-    if blk_count == 2 and node_dev == 2 and share == 2 * LANES:
-        return exchange_folded(plan, place, got, own_part, send_part, sibling)
     return exchange_plain(plan, place, got, own_part, send_part, sibling, blk_count)
 
 
+def shards_folded(leaf_rows, leaf_weight, branching, sibling, node_block, na_rows, na_weight, na_route):
+    leaf_count = lax.axis_size(SPLIT)
+    node_dev, most_children, depth, state = leaf_rows.shape
+    count = na_rows.shape[0]
+    share = state // 2
+    half = share // 2
+    nodes = leaf_count * node_dev
+    plan = Plan(nodes, 1, 3 * count // (2 * nodes), state, EXTRA, INNER)
+    shape = jax.ShapeDtypeStruct
+    any_spec = pl.BlockSpec(memory_space=pl.ANY)
+    across = [(0, 1), (1, 0)]
+    to_partner = [(i, i ^ 1) for i in range(leaf_count)]
+    result = shape((share, node_dev, state), F32)
+    rows = shape((share, state), F32)
+    codes = shape((6 * half + GROUP, half), jnp.int16)
+    gathered = shape((nodes * plan.rows, state), BF16)
+
+    blocks = bucket(plan, na_route, na_weight, na_rows)
+    got = lax.all_to_all(blocks, (SPLIT[0], "blk", SPLIT[1]), split_axis=0, concat_axis=0, tiled=True)
+
+    own_block = jnp.transpose(node_block, (1, 0, 2))
+    leaf = dict(
+        scratch_shapes=[
+            pltpu.VMEM((most_children, depth), BF16),
+            pltpu.VMEM((most_children // 2, 2, depth, state), BF16),
+            pltpu.VMEM((state, state), F32),
+            pltpu.SemaphoreType.DMA((most_children // 2 + 1,)),
+        ],
+        flops=1,
+        moved=1,
+        vmem=24 << 20,
+    )
+    with jax.named_scope("far_leaf_products"):
+        far_own, far_code = call(
+            far_leaf_kernel, (rows, codes), [SMEM, any_spec, any_spec], **leaf
+        )(branching, leaf_weight, leaf_rows)
+    near_code = lax.ppermute(far_code, "blk", across)
+    with jax.named_scope("near_leaf_products"):
+        near_own, send_part, far_own = call(
+            near_leaf_kernel, (rows, rows, rows), [SMEM, any_spec, any_spec, VMEM, VMEM], **leaf
+        )(branching, leaf_weight, leaf_rows, own_block, far_own)
+    their_own = lax.ppermute(far_own, SPLIT, to_partner)
+    with jax.named_scope("routed_send"):
+        code, plain, scaled = call(
+            functools.partial(send_folded, plan),
+            (codes, gathered, gathered),
+            [VMEM, VMEM],
+            flops=2 * nodes * plan.rows * share * state,
+        )(got, send_part)
+    arrived = lax.ppermute(code, "blk", across)
+    with jax.named_scope("near_node"):
+        near = call(near_node_kernel, rows, [VMEM, VMEM, VMEM, VMEM], flops=LONG)(
+            near_own, plain, scaled, near_code
+        )
+    their_near = lax.ppermute(near, SPLIT, to_partner)
+    their_arrived = lax.ppermute(arrived, SPLIT, to_partner)
+    with jax.named_scope("far_node"):
+        far, node = call(far_node_kernel, (rows, result), [VMEM, VMEM, VMEM], flops=LONG)(
+            near, far_own, arrived
+        )
+    with jax.named_scope("merge"):
+        return call(
+            merge_folded,
+            (result, result),
+            [VMEM] * 7,
+            out_specs=(any_spec, any_spec),
+            scratch_shapes=[
+                pltpu.VMEM((share, node_dev, state), F32),
+                pltpu.SemaphoreType.DMA((PIECES + 1,)),
+            ],
+        )(sibling, near, far, node, their_near, their_own, their_arrived)
+
+
 def solution(mesh):
-    return jax.shard_map(
-        shards,
-        mesh=mesh,
-        in_specs=(
-            P("leaf", None, "blk", None),
-            P("leaf", None, "blk"),
-            P("leaf"),
-            P("leaf", None),
-            P("blk", "leaf", None),
-            P(("leaf", "blk"), None),
-            P(("leaf", "blk")),
-            P(("leaf", "blk"), None),
-        ),
-        out_specs=(P("blk", "leaf", None), P("blk", "leaf", None)),
-        check_vma=False,
-    )
+    leaf_count, blk_count = mesh.shape["leaf"], mesh.shape["blk"]
+    plain = jax.shard_map(
+        shards_plain, mesh=mesh, in_specs=in_specs("leaf"), out_specs=out_specs("leaf"), check_vma=False
+    )
+    if blk_count != 2 or leaf_count % INNER:
+        return plain
+    split = jax.sharding.Mesh(
+        mesh.devices.reshape(leaf_count // INNER, INNER, blk_count), (*SPLIT, "blk")
+    )
+    folded = jax.shard_map(
+        shards_folded, mesh=split, in_specs=in_specs(SPLIT), out_specs=out_specs(SPLIT), check_vma=False
+    )
+
+    def choose(leaf_rows, *more):
+        nodes, children, _, state = leaf_rows.shape
+        fits = nodes == 2 * leaf_count and children % 2 == 0 and state == 4 * LANES
+        return (folded if fits else plain)(leaf_rows, *more)
+
+    return choose
+
+
+def in_specs(leaf):
+    every = ((leaf,) if isinstance(leaf, str) else leaf) + ("blk",)
+    return (
+        P(leaf, None, "blk", None),
+        P(leaf, None, "blk"),
+        P(leaf),
+        P(leaf, None),
+        P("blk", leaf, None),
+        P(every, None),
+        P(every),
+        P(every, None),
+    )
+
+
+def out_specs(leaf):
+    return (P("blk", leaf, None), P("blk", leaf, None))

time: 47.2 us -> 44.2 us (0.936)
  the two profiles are of different devices: /device:TPU:9 before, /device:TPU:0 now
where the time goes in v5:
time: 44.2 us; the launch traced here: 43.9 us
  waiting for transfers between devices  16.4 us (37%)
  Pallas kernels  12.3 us (28%)
  starting transfers between devices  10.9 us (25%)
  local copies, waits for them, and re-layouts  3.6 us (8%)
  between operations  0.74 us (2%)
    all_to_all x1, waiting for transfers between devices, shards_folded(): lax.all_to_all(blocks, (SPLIT[0], 'blk', SPLIT[1]), split_axis=0, concat_...  11.6 us
    all_to_all x1, starting transfers between devices, shards_folded(): lax.all_to_all(blocks, (SPLIT[0], 'blk', SPLIT[1]), split_axis=0, concat_...  7.31 us
    ppermute x1, waiting for transfers between devices, shards_folded(): arrived = lax.ppermute(code, 'blk', across)  4.22 us
    unnamed x11, local copies, waits for them, and re-layouts  3.6 us
    pallas_call x1, Pallas kernels, bucket(): call(functools.partial(bucket_kernel, plan), jax.ShapeDtypeStruct((plan.l...  2.72 us
    pallas_call x1, Pallas kernels, shards_folded(): call(far_leaf_kernel, (rows, codes), [SMEM, any_spec, any_spec], **leaf)  2.46 us
    pallas_call x1, Pallas kernels, shards_folded(): call(near_leaf_kernel, (rows, rows, rows), [SMEM, any_spec, any_spec, VME...  2.41 us
    pallas_call x1, Pallas kernels, shards_folded(): call(merge_folded, (result, result), [VMEM] * 7, out_specs=(any_spec, any...  2.03 us
  transfers between devices with their start and end apart: 6, of which 3 were waited for; matrix products, arithmetic and copies ran while one was open for 0% of the time, Pallas kernels for 17%

profile of v5, /device:TPU:0, one launch (start us, length us, event | category | flops | bytes accessed | tf_op | source)
XLA Modules:
  0.0 43.9 jit_solution(9293551137575155045)
XLA Ops:
  0.6 0.0 copy-start.4
  0.6 2.7 %bucket.1 = bf16[32,104,128]{2,1,0:T(8,128)(2,1)} custom-call(s32[1,512]{1,0:T(1,128)} %bitcast.5, bf16[512]{0:T(512)(128)(2,1)} %weight_hbm.5, bf16[512,512]{1,0:T(8,128)(2,1)} %rows_hbm.5), custom_call_target="tpu_custom_call" | custom-call | flops 402653184 | bytes 1048576 | tf_op jit(solution)/shard_map/bucket/pallas_call | solution.py:529
  3.4 7.3 %all-to-all-start = ((bf16[32,104,128]{2,1,0:T(8,128)(2,1)}), bf16[32,104,128]{2,1,0:T(8,128)(2,1)S(1)}, u32[]{:S(2)}, u32[]{:S(2)}) async-start(bf16[32,104,128]{2,1,0:T(8,128)(2,1)} %bucket.1), calls=%async_computation | async-start | bytes 1703936 | tf_op jit(solution)/shard_map/all_to_all | solution.py:598
  10.7 0.0 copy-start
  10.7 2.2 %copy-done = bf16[2,8,256,512]{3,2,1,0:T(8,128)(2,1)S(1)} copy-done((bf16[2,8,256,512]{3,2,1,0:T(8,128)(2,1)S(1)}, bf16[2,8,256,512]{3,2,1,0:T(8,128)(2,1)}, u32[]{:S(2)}) %copy-start) | copy-done | bytes 4194328
  12.9 0.0 copy-start.1
  12.9 0.7 %copy-done.1 = bf16[2,8,256]{2,1,0:T(8,128)(2,1)S(1)} copy-done((bf16[2,8,256]{2,1,0:T(8,128)(2,1)S(1)}, bf16[2,8,256]{2,1,0:T(8,128)(2,1)}, u32[]{:S(2)}) %copy-start.1) | copy-done | bytes 8216
  13.6 0.0 copy-start.2
  13.6 0.7 %copy-done.2 = s32[2]{0:T(128)S(1)} copy-done((s32[2]{0:T(128)S(1)}, s32[2]{0:T(128)}, u32[]{:S(2)}) %copy-start.2) | copy-done | bytes 32
  14.2 2.5 %far_leaf_products.1 = (f32[256,512]{1,0:T(8,128)S(1)}, s16[784,128]{1,0:T(8,128)(2,1)S(1)}) custom-call(s32[2]{0:T(128)S(1)} %copy-done.2, bf16[2,8,256]{2,1,0:T(8,128)(2,1)S(1)} %copy-done.1, bf16[2,8,256,512]{3,2,1,0:T(8,128)(2,1)S(1)} %copy-done), custom_call_target="tpu_custom_call" | custom-call | flops 1 | bytes 1 | tf_op jit(solution)/shard_map/far_leaf_products/pallas_call | solution.py:613
  16.7 1.8 %collective-permute-start = (s16[784,128]{1,0:T(8,128)(2,1)S(1)}, s16[784,128]{1,0:T(8,128)(2,1)S(1)}, u32[]{:S(2)}, u32[]{:S(2)}) collective-permute-start(s16[784,128]{1,0:T(8,128)(2,1)S(1)} %get-tuple-element.17), channel_id=1, source_target_pairs={{0,1},{1,0},{2,3},{3,2},{4,5},{5,4},{6,7},{7,6},{8,9},{9,8},{10,11... | collective-permute-start | bytes 602120 | tf_op jit(solution)/shard_map/ppermute | solution.py:616
  18.5 0.0 copy-done.4
  18.5 0.1 copy.12
  18.6 2.4 %near_leaf_products.1 = (f32[256,512]{1,0:T(8,128)S(1)}, f32[256,512]{1,0:T(8,128)S(1)}, f32[256,512]{1,0:T(8,128)S(1)}) custom-call(s32[2]{0:T(128)S(1)} %copy-done.2, bf16[2,8,256]{2,1,0:T(8,128)(2,1)S(1)} %copy-done.1, bf16[2,8,256,512]{3,2,1,0:T(8,128)(2,1)S(1)} %copy-done, bf16[2,256,512]{2,1,0:T(8,128)(2,1)S(1)} %bitcast.4, ...), custom_call_target="tpu_custom_call" | custom-call | flops 1 | bytes 1 | tf_op jit(solution)/shard_map/near_leaf_products/pallas_call | solution.py:618
  21.0 0.1 collective-permute-start.3
  21.1 11.6 %all-to-all-done.got_ref = bf16[32,104,128]{2,1,0:T(8,128)(2,1)S(1)} async-done(((bf16[32,104,128]{2,1,0:T(8,128)(2,1)}), bf16[32,104,128]{2,1,0:T(8,128)(2,1)S(1)}, u32[]{:S(2)}, u32[]{:S(2)}) %all-to-all-start) | async-done | bytes 852000 | tf_op jit(solution)/shard_map/all_to_all | solution.py:598
  32.7 1.2 %routed_send.1 = (s16[784,128]{1,0:T(8,128)(2,1)S(1)}, bf16[768,512]{1,0:T(8,128)(2,1)S(1)}, bf16[768,512]{1,0:T(8,128)(2,1)S(1)}) custom-call(bf16[32,104,128]{2,1,0:T(8,128)(2,1)S(1)} %all-to-all-done.got_ref, f32[256,512]{1,0:T(8,128)S(1)} %get-tuple-element.14.part_ref), custom_call_target="tpu_custom_call" | custom-call | flops 201326592 | bytes 1048576 | tf_op jit(solution)/shard_map/routed_send/pallas_call | solution.py:623
  33.9 1.6 %collective-permute-start.1 = (s16[784,128]{1,0:T(8,128)(2,1)S(1)}, s16[784,128]{1,0:T(8,128)(2,1)S(1)}, u32[]{:S(2)}, u32[]{:S(2)}) collective-permute-start(s16[784,128]{1,0:T(8,128)(2,1)S(1)} %get-tuple-element.19), channel_id=1, source_target_pairs={{0,1},{1,0},{2,3},{3,2},{4,5},{5,4},{6,7},{7,6},{8,9},{9,8},{10,11... | collective-permute-start | bytes 602120 | tf_op jit(solution)/shard_map/ppermute | solution.py:629
  35.5 0.0 collective-permute-done.code_ref
  35.5 0.6 %near_node.1.near_ref = f32[256,512]{1,0:T(8,128)S(1)} custom-call(f32[256,512]{1,0:T(8,128)S(1)} %get-tuple-element.13.own_ref, bf16[768,512]{1,0:T(8,128)(2,1)S(1)} %get-tuple-element.15.plain_ref, bf16[768,512]{1,0:T(8,128)(2,1)S(1)} %get-tuple-element.16.scaled_ref, s16[784,128]{1,0:T(8,128)(2,1)S(1)} %collective-permute-done.code_ref), custom_call_target="tpu_custom_call" | custom-call | flops 20000000000 | bytes 1048576 | tf_op jit(solution)/shard_map/near_node/pallas_call | solution.py:631
  36.1 0.0 copy-start.3
  36.1 0.1 collective-permute-start.2
  36.2 4.2 %collective-permute-done.1.code_ref = s16[784,128]{1,0:T(8,128)(2,1)S(1)} collective-permute-done((s16[784,128]{1,0:T(8,128)(2,1)S(1)}, s16[784,128]{1,0:T(8,128)(2,1)S(1)}, u32[]{:S(2)}, u32[]{:S(2)}) %collective-permute-start.1) | collective-permute-done | bytes 200736 | tf_op jit(solution)/shard_map/ppermute | solution.py:629
  40.4 0.0 collective-permute-start.4
  40.4 0.8 %far_node.1 = (f32[256,512]{1,0:T(8,128)S(1)}, f32[256,2,512]{2,1,0:T(2,128)S(1)}) custom-call(f32[256,512]{1,0:T(8,128)S(1)} %near_node.1.near_ref, f32[256,512]{1,0:T(8,128)S(1)} %get-tuple-element.18.own_ref, s16[784,128]{1,0:T(8,128)(2,1)S(1)} %collective-permute-done.1.code_ref), custom_call_target="tpu_custom_call" | custom-call | flops 20000000000 | bytes 1048576 | tf_op jit(solution)/shard_map/far_node/pallas_call | solution.py:637
  41.3 0.0 collective-permute-done.3.their_own_ref
  41.3 0.6 %collective-permute-done.4.code_ref = s16[784,128]{1,0:T(8,128)(2,1)S(1)} collective-permute-done((s16[784,128]{1,0:T(8,128)(2,1)S(1)}, s16[784,128]{1,0:T(8,128)(2,1)S(1)}, u32[]{:S(2)}, u32[]{:S(2)}) %collective-permute-start.4) | collective-permute-done | bytes 200736 | tf_op jit(solution)/shard_map/ppermute | solution.py:635
  41.9 0.0 collective-permute-done.2.their_near_ref
  41.9 0.0 copy-done.3
  41.9 2.0 %merge.1 = (f32[256,2,512]{2,1,0:T(2,128)}, f32[256,2,512]{2,1,0:T(2,128)}) custom-call(s32[1,2]{1,0:T(1,128)S(1)} %copy-done.3, f32[256,512]{1,0:T(8,128)S(1)} %near_node.1.near_ref, f32[256,512]{1,0:T(8,128)S(1)} %get-tuple-element.20.far_ref, f32[256,2,512]{2,1,0:T(2,128)S(1)} %get-tuple-element.21.node_ref, ...), custom_call_target="tpu_custom_call" | custom-call | bytes 1048576 | tf_op jit(solution)/shard_map/merge/pallas_call | solution.py:641
Async XLA Ops:
  0.6 17.9 %copy-start.4 = (bf16[256,2,512]{2,1,0:T(2,128)(2,1)S(1)}, bf16[256,2,512]{2,1,0:T(2,128)(2,1)}, u32[]{:S(2)}) copy-start(bf16[256,2,512]{2,1,0:T(2,128)(2,1)} %param.12) | copy-start | bytes 1572868
  3.4 29.3 %all-to-all-start = ((bf16[32,104,128]{2,1,0:T(8,128)(2,1)}), bf16[32,104,128]{2,1,0:T(8,128)(2,1)S(1)}, u32[]{:S(2)}, u32[]{:S(2)}) async-start(bf16[32,104,128]{2,1,0:T(8,128)(2,1)} %bucket.1), calls=%async_computation | async-start | bytes 1703936 | tf_op jit(solution)/shard_map/all_to_all | solution.py:598
  10.7 2.2 %copy-start = (bf16[2,8,256,512]{3,2,1,0:T(8,128)(2,1)S(1)}, bf16[2,8,256,512]{3,2,1,0:T(8,128)(2,1)}, u32[]{:S(2)}) copy-start(bf16[2,8,256,512]{3,2,1,0:T(8,128)(2,1)} %rows_hbm.4) | copy-start | bytes 12582916
  12.9 0.7 %copy-start.1 = (bf16[2,8,256]{2,1,0:T(8,128)(2,1)S(1)}, bf16[2,8,256]{2,1,0:T(8,128)(2,1)}, u32[]{:S(2)}) copy-start(bf16[2,8,256]{2,1,0:T(8,128)(2,1)} %weight_hbm.4) | copy-start | bytes 24580
  13.6 0.7 %copy-start.2 = (s32[2]{0:T(128)S(1)}, s32[2]{0:T(128)}, u32[]{:S(2)}) copy-start(s32[2]{0:T(128)} %branching_ref.3) | copy-start | bytes 28
  16.7 18.8 %collective-permute-start = (s16[784,128]{1,0:T(8,128)(2,1)S(1)}, s16[784,128]{1,0:T(8,128)(2,1)S(1)}, u32[]{:S(2)}, u32[]{:S(2)}) collective-permute-start(s16[784,128]{1,0:T(8,128)(2,1)S(1)} %get-tuple-element.17), channel_id=1, source_target_pairs={{0,1},{1,0},{2,3},{3,2},{4,5},{5,4},{6,7},{7,6},{8,9},{9,8},{10,11... | collective-permute-start | bytes 602120 | tf_op jit(solution)/shard_map/ppermute | solution.py:616
  21.0 20.3 %collective-permute-start.3 = (f32[256,512]{1,0:T(8,128)S(1)}, f32[256,512]{1,0:T(8,128)S(1)}, u32[]{:S(2)}, u32[]{:S(2)}) collective-permute-start(f32[256,512]{1,0:T(8,128)S(1)} %get-tuple-element.18.own_ref), channel_id=1, source_target_pairs={{0,2},{2,0},{4,6},{6,4},{8,10},{10,8},{12,14},{14,12},{16,18},{18,... | collective-permute-start | bytes 1572872 | tf_op jit(solution)/shard_map/ppermute | solution.py:621
  33.9 6.5 %collective-permute-start.1 = (s16[784,128]{1,0:T(8,128)(2,1)S(1)}, s16[784,128]{1,0:T(8,128)(2,1)S(1)}, u32[]{:S(2)}, u32[]{:S(2)}) collective-permute-start(s16[784,128]{1,0:T(8,128)(2,1)S(1)} %get-tuple-element.19), channel_id=1, source_target_pairs={{0,1},{1,0},{2,3},{3,2},{4,5},{5,4},{6,7},{7,6},{8,9},{9,8},{10,11... | collective-permute-start | bytes 602120 | tf_op jit(solution)/shard_map/ppermute | solution.py:629
  36.1 5.8 %copy-start.3 = (s32[1,2]{1,0:T(1,128)S(1)}, s32[1,2]{1,0:T(1,128)}, u32[]{:S(2)}) copy-start(s32[1,2]{1,0:T(1,128)} %sibling_ref.1) | copy-start | bytes 28
  36.1 5.7 %collective-permute-start.2 = (f32[256,512]{1,0:T(8,128)S(1)}, f32[256,512]{1,0:T(8,128)S(1)}, u32[]{:S(2)}, u32[]{:S(2)}) collective-permute-start(f32[256,512]{1,0:T(8,128)S(1)} %near_node.1.near_ref), channel_id=1, source_target_pairs={{0,2},{2,0},{4,6},{6,4},{8,10},{10,8},{12,14},{14,12},{16,18},{18,... | collective-permute-start | bytes 1572872 | tf_op jit(solution)/shard_map/ppermute | solution.py:634
  40.4 1.4 %collective-permute-start.4 = (s16[784,128]{1,0:T(8,128)(2,1)S(1)}, s16[784,128]{1,0:T(8,128)(2,1)S(1)}, u32[]{:S(2)}, u32[]{:S(2)}) collective-permute-start(s16[784,128]{1,0:T(8,128)(2,1)S(1)} %collective-permute-done.1.code_ref), channel_id=1, source_target_pairs={{0,2},{2,0},{4,6},{6,4},{8,10},{10,8},{12,14},{14,12},{16,18},{18,... | collective-permute-start | bytes 602120 | tf_op jit(solution)/shard_map/ppermute | solution.py:635

commit v6 on v5

--- a/solution.py
+++ b/solution.py
@@ -17,14 +17,14 @@
 VMEM = pl.BlockSpec(memory_space=pltpu.VMEM)
 SMEM = pl.BlockSpec(memory_space=pltpu.SMEM)
 CODE = 32000.0
-SPLIT = ("outer", "inner")
-INNER = 4
+SPLIT = ("z1", "z0", "y", "core")
+ORDER = ("blk", "y", "z1", "core", "z0")
 LONG = 20_000_000_000
 
 
 class Plan:
-    def __init__(self, leaf_count, node_dev, capacity, state, unit, inner=0):
-        self.inner = inner
+    def __init__(self, leaf_count, node_dev, capacity, state, unit, order=()):
+        self.order = order
         self.leaf_count, self.node_dev, self.capacity, self.state = leaf_count, node_dev, capacity, state
         self.full = capacity // GROUP * GROUP
         self.rest = capacity - self.full
@@ -39,11 +39,12 @@
         self.depth = [leaf_count * GROUP * len(g) for g in self.groups_of]
 
     def block_of(self, node):
-        if not self.inner:
+        if not self.order:
             return node
-        group = node // (2 * self.inner) * (2 * self.inner)
-        leaf = node // 2
-        return group + (node - 2 * leaf) * self.inner + (leaf - group // 2)
+        block = jnp.zeros_like(node)
+        for name in self.order:
+            block = 2 * block + (node >> (len(SPLIT) - (*SPLIT, "blk").index(name)) & 1)
+        return block
 
     def node_at(self, row):
         if row < self.node_dev * self.full:
@@ -278,14 +279,6 @@
     return mine, theirs
 
 
-def turned(rows, first, count):
-    width = rows.shape[1]
-    pick = lax.broadcasted_iota(I32, (count, width), 1) == lax.broadcasted_iota(I32, (count, width), 0) + first
-    return lax.dot_general(
-        jnp.where(pick, 1.0, 0.0).astype(BF16), rows, (((1,), (1,)), ((), ())), preferred_element_type=F32
-    )
-
-
 def leaf_sum(node, branching_ref, weight_hbm, rows_hbm, weight_ref, rows_ref, total, sems):
     pairs = rows_hbm.shape[1] // 2
     depth, state = rows_hbm.shape[2:]
@@ -301,14 +294,13 @@
         pl.when(2 * p < count)(copies[p].start)
     weights.wait()
     live = lax.broadcasted_iota(I32, weight_ref.shape, 0) < count
-    factor = jnp.where(live, weight_ref[...].astype(F32), 0.0)
+    columns = jnp.transpose(jnp.where(live, weight_ref[...].astype(F32), 0.0))
 
     def term(p):
         copies[p].wait()
         rows = rows_ref[p].reshape(2 * depth, state)
-        weight = jnp.concatenate([factor[2 * p : 2 * p + 1, :], factor[2 * p + 1 : 2 * p + 2, :]], axis=1)
-        scaled = (turned(rows, 0, state) * weight).astype(BF16)
-        return jnp.dot(scaled, rows, preferred_element_type=F32)
+        weight = jnp.concatenate([columns[:, 2 * p : 2 * p + 1], columns[:, 2 * p + 1 : 2 * p + 2]], axis=0)
+        return dot_t((rows.astype(F32) * weight).astype(BF16), rows)
 
     total[...] = term(0)
     for p in range(1, pairs):
@@ -361,11 +353,11 @@
             rows = jnp.concatenate([block[c * cap : (c + 1) * cap, :] for block in blocks], axis=0)
             plain_ref[at : at + 2 * cap, c * LANES : (c + 1) * LANES] = rows.astype(BF16)
             scaled_ref[at : at + 2 * cap, c * LANES : (c + 1) * LANES] = (rows * weight).astype(BF16)
-    scaled = turned(scaled_ref[...], (1 - lax.axis_index("blk")) * share, share).astype(BF16)
+    scaled = scaled_ref[:, theirs]
     encode_node(
         code_ref,
-        part_ref[:, theirs] + jnp.dot(scaled, plain_ref[:, theirs], preferred_element_type=F32),
-        part_ref[:, mine] + jnp.dot(scaled, plain_ref[:, mine], preferred_element_type=F32),
+        part_ref[:, theirs] + dot_t(scaled, plain_ref[:, theirs]),
+        part_ref[:, mine] + dot_t(scaled, plain_ref[:, mine]),
     )
 
 
@@ -386,8 +378,8 @@
 
 def near_node_kernel(own_ref, plain_ref, scaled_ref, code_ref, node_ref):
     share = own_ref.shape[0]
-    scaled = turned(scaled_ref[...], lax.axis_index("blk") * share, share).astype(BF16)
-    node_ref[...] = own_ref[...] + jnp.dot(scaled, plain_ref[...], preferred_element_type=F32)
+    mine, _ = halves(lax.axis_index("blk"), share)
+    node_ref[...] = own_ref[...] + dot_t(scaled_ref[:, mine], plain_ref[...])
     terms = in_columns(lax.axis_index("blk"), *decode_node(code_ref))
     for i, k, rows, columns in tiles_of(node_ref):
         node_ref[rows, columns] += terms[i][k]
@@ -584,7 +576,7 @@
     share = state // 2
     half = share // 2
     nodes = leaf_count * node_dev
-    plan = Plan(nodes, 1, 3 * count // (2 * nodes), state, EXTRA, INNER)
+    plan = Plan(nodes, 1, 3 * count // (2 * nodes), state, EXTRA, ORDER)
     shape = jax.ShapeDtypeStruct
     any_spec = pl.BlockSpec(memory_space=pl.ANY)
     across = [(0, 1), (1, 0)]
@@ -595,7 +587,7 @@
     gathered = shape((nodes * plan.rows, state), BF16)
 
     blocks = bucket(plan, na_route, na_weight, na_rows)
-    got = lax.all_to_all(blocks, (SPLIT[0], "blk", SPLIT[1]), split_axis=0, concat_axis=0, tiled=True)
+    got = lax.all_to_all(blocks, ORDER, split_axis=0, concat_axis=0, tiled=True)
 
     own_block = jnp.transpose(node_block, (1, 0, 2))
     leaf = dict(
@@ -655,11 +647,9 @@
     plain = jax.shard_map(
         shards_plain, mesh=mesh, in_specs=in_specs("leaf"), out_specs=out_specs("leaf"), check_vma=False
     )
-    if blk_count != 2 or leaf_count % INNER:
+    if blk_count != 2 or leaf_count != 2 ** len(SPLIT):
         return plain
-    split = jax.sharding.Mesh(
-        mesh.devices.reshape(leaf_count // INNER, INNER, blk_count), (*SPLIT, "blk")
-    )
+    split = jax.sharding.Mesh(mesh.devices.reshape((2,) * len(ORDER)), (*SPLIT, "blk"))
     folded = jax.shard_map(
         shards_folded, mesh=split, in_specs=in_specs(SPLIT), out_specs=out_specs(SPLIT), check_vma=False
     )

time: 44.2 us -> 42.5 us (0.962)
  the two profiles are of different devices: /device:TPU:0 before, /device:TPU:9 now
where the time goes in v6:
time: 42.5 us; the launch traced here: 42.2 us
  starting transfers between devices  16.3 us (38%)
  Pallas kernels  12.9 us (30%)
  waiting for transfers between devices  8.71 us (20%)
  local copies, waits for them, and re-layouts  3.6 us (8%)
  between operations  0.73 us (2%)
    all_to_all x1, waiting for transfers between devices, shards_folded(): got = lax.all_to_all(blocks, ORDER, split_axis=0, concat_axis=0, tiled=True)  7.67 us
    all_to_all x1, starting transfers between devices, shards_folded(): got = lax.all_to_all(blocks, ORDER, split_axis=0, concat_axis=0, tiled=True)  6.36 us
    unnamed x11, local copies, waits for them, and re-layouts  3.6 us
    ppermute x1, starting transfers between devices, shards_folded(): their_arrived = lax.ppermute(arrived, SPLIT, to_partner)  3.29 us
    pallas_call x1, Pallas kernels, shards_folded(): call(far_leaf_kernel, (rows, codes), [SMEM, any_spec, any_spec], **leaf)  2.93 us
    pallas_call x1, Pallas kernels, shards_folded(): call(near_leaf_kernel, (rows, rows, rows), [SMEM, any_spec, any_spec, VME...  2.88 us
    pallas_call x1, Pallas kernels, bucket(): call(functools.partial(bucket_kernel, plan), jax.ShapeDtypeStruct((plan.l...  2.73 us
    pallas_call x1, Pallas kernels, shards_folded(): call(merge_folded, (result, result), [VMEM] * 7, out_specs=(any_spec, any...  2.03 us
  transfers between devices with their start and end apart: 6, of which 3 were waited for; matrix products, arithmetic and copies ran while one was open for 0% of the time, Pallas kernels for 19%

profile of v6, /device:TPU:9, one launch (start us, length us, event | category | flops | bytes accessed | tf_op | source)
XLA Modules:
  0.0 42.2 jit_solution(4150548112395001201)
XLA Ops:
  0.6 0.0 copy-start.4
  0.6 2.7 %bucket.1 = bf16[32,104,128]{2,1,0:T(8,128)(2,1)} custom-call(s32[1,512]{1,0:T(1,128)} %bitcast.5, bf16[512]{0:T(512)(128)(2,1)} %weight_hbm.5, bf16[512,512]{1,0:T(8,128)(2,1)} %rows_hbm.5), custom_call_target="tpu_custom_call" | custom-call | flops 402653184 | bytes 1048576 | tf_op jit(solution)/shard_map/bucket/pallas_call | solution.py:521
  3.4 6.4 %all-to-all-start = ((bf16[32,104,128]{2,1,0:T(8,128)(2,1)}), bf16[32,104,128]{2,1,0:T(8,128)(2,1)S(1)}, u32[]{:S(2)}, u32[]{:S(2)}) async-start(bf16[32,104,128]{2,1,0:T(8,128)(2,1)} %bucket.1), calls=%async_computation | async-start | bytes 1703936 | tf_op jit(solution)/shard_map/all_to_all | solution.py:590
  9.7 0.0 copy-start
  9.8 2.2 %copy-done = bf16[2,8,256,512]{3,2,1,0:T(8,128)(2,1)S(1)} copy-done((bf16[2,8,256,512]{3,2,1,0:T(8,128)(2,1)S(1)}, bf16[2,8,256,512]{3,2,1,0:T(8,128)(2,1)}, u32[]{:S(2)}) %copy-start) | copy-done | bytes 4194328
  11.9 0.0 copy-start.1
  11.9 0.7 %copy-done.1 = bf16[2,8,256]{2,1,0:T(8,128)(2,1)S(1)} copy-done((bf16[2,8,256]{2,1,0:T(8,128)(2,1)S(1)}, bf16[2,8,256]{2,1,0:T(8,128)(2,1)}, u32[]{:S(2)}) %copy-start.1) | copy-done | bytes 8216
  12.6 0.0 copy-start.2
  12.6 0.7 %copy-done.2 = s32[2]{0:T(128)S(1)} copy-done((s32[2]{0:T(128)S(1)}, s32[2]{0:T(128)}, u32[]{:S(2)}) %copy-start.2) | copy-done | bytes 32
  13.3 2.9 %far_leaf_products.1 = (f32[256,512]{1,0:T(8,128)S(1)}, s16[784,128]{1,0:T(8,128)(2,1)S(1)}) custom-call(s32[2]{0:T(128)S(1)} %copy-done.2, bf16[2,8,256]{2,1,0:T(8,128)(2,1)S(1)} %copy-done.1, bf16[2,8,256,512]{3,2,1,0:T(8,128)(2,1)S(1)} %copy-done), custom_call_target="tpu_custom_call" | custom-call | flops 1 | bytes 1 | tf_op jit(solution)/shard_map/far_leaf_products/pallas_call | solution.py:605
  16.2 1.2 %collective-permute-start = (s16[784,128]{1,0:T(8,128)(2,1)S(1)}, s16[784,128]{1,0:T(8,128)(2,1)S(1)}, u32[]{:S(2)}, u32[]{:S(2)}) collective-permute-start(s16[784,128]{1,0:T(8,128)(2,1)S(1)} %get-tuple-element.17), channel_id=1, source_target_pairs={{0,1},{1,0},{2,3},{3,2},{4,5},{5,4},{6,7},{7,6},{8,9},{9,8},{10,11... | collective-permute-start | bytes 602120 | tf_op jit(solution)/shard_map/ppermute | solution.py:608
  17.5 0.0 copy-done.4
  17.5 0.1 copy.12
  17.5 2.9 %near_leaf_products.1 = (f32[256,512]{1,0:T(8,128)S(1)}, f32[256,512]{1,0:T(8,128)S(1)}, f32[256,512]{1,0:T(8,128)S(1)}) custom-call(s32[2]{0:T(128)S(1)} %copy-done.2, bf16[2,8,256]{2,1,0:T(8,128)(2,1)S(1)} %copy-done.1, bf16[2,8,256,512]{3,2,1,0:T(8,128)(2,1)S(1)} %copy-done, bf16[2,256,512]{2,1,0:T(8,128)(2,1)S(1)} %bitcast.4, ...), custom_call_target="tpu_custom_call" | custom-call | flops 1 | bytes 1 | tf_op jit(solution)/shard_map/near_leaf_products/pallas_call | solution.py:610
  20.4 2.0 %collective-permute-start.3 = (f32[256,512]{1,0:T(8,128)S(1)}, f32[256,512]{1,0:T(8,128)S(1)}, u32[]{:S(2)}, u32[]{:S(2)}) collective-permute-start(f32[256,512]{1,0:T(8,128)S(1)} %get-tuple-element.18.own_ref), channel_id=1, source_target_pairs={{0,2},{2,0},{4,6},{6,4},{8,10},{10,8},{12,14},{14,12},{16,18},{18,... | collective-permute-start | bytes 1572872 | tf_op jit(solution)/shard_map/ppermute | solution.py:613
  22.4 7.7 %all-to-all-done.got_ref = bf16[32,104,128]{2,1,0:T(8,128)(2,1)S(1)} async-done(((bf16[32,104,128]{2,1,0:T(8,128)(2,1)}), bf16[32,104,128]{2,1,0:T(8,128)(2,1)S(1)}, u32[]{:S(2)}, u32[]{:S(2)}) %all-to-all-start) | async-done | bytes 852000 | tf_op jit(solution)/shard_map/all_to_all | solution.py:590
  30.1 1.0 %routed_send.1 = (s16[784,128]{1,0:T(8,128)(2,1)S(1)}, bf16[768,512]{1,0:T(8,128)(2,1)S(1)}, bf16[768,512]{1,0:T(8,128)(2,1)S(1)}) custom-call(bf16[32,104,128]{2,1,0:T(8,128)(2,1)S(1)} %all-to-all-done.got_ref, f32[256,512]{1,0:T(8,128)S(1)} %get-tuple-element.14.part_ref), custom_call_target="tpu_custom_call" | custom-call | flops 201326592 | bytes 1048576 | tf_op jit(solution)/shard_map/routed_send/pallas_call | solution.py:615
  31.1 1.6 %collective-permute-start.1 = (s16[784,128]{1,0:T(8,128)(2,1)S(1)}, s16[784,128]{1,0:T(8,128)(2,1)S(1)}, u32[]{:S(2)}, u32[]{:S(2)}) collective-permute-start(s16[784,128]{1,0:T(8,128)(2,1)S(1)} %get-tuple-element.19), channel_id=1, source_target_pairs={{0,1},{1,0},{2,3},{3,2},{4,5},{5,4},{6,7},{7,6},{8,9},{9,8},{10,11... | collective-permute-start | bytes 602120 | tf_op jit(solution)/shard_map/ppermute | solution.py:621
  32.7 0.0 collective-permute-done.code_ref
  32.7 0.5 %near_node.1.near_ref = f32[256,512]{1,0:T(8,128)S(1)} custom-call(f32[256,512]{1,0:T(8,128)S(1)} %get-tuple-element.13.own_ref, bf16[768,512]{1,0:T(8,128)(2,1)S(1)} %get-tuple-element.15.plain_ref, bf16[768,512]{1,0:T(8,128)(2,1)S(1)} %get-tuple-element.16.scaled_ref, s16[784,128]{1,0:T(8,128)(2,1)S(1)} %collective-permute-done.code_ref), custom_call_target="tpu_custom_call" | custom-call | flops 20000000000 | bytes 1048576 | tf_op jit(solution)/shard_map/near_node/pallas_call | solution.py:623
  33.2 0.0 copy-start.3
  33.2 1.8 %collective-permute-start.2 = (f32[256,512]{1,0:T(8,128)S(1)}, f32[256,512]{1,0:T(8,128)S(1)}, u32[]{:S(2)}, u32[]{:S(2)}) collective-permute-start(f32[256,512]{1,0:T(8,128)S(1)} %near_node.1.near_ref), channel_id=1, source_target_pairs={{0,2},{2,0},{4,6},{6,4},{8,10},{10,8},{12,14},{14,12},{16,18},{18,... | collective-permute-start | bytes 1572872 | tf_op jit(solution)/shard_map/ppermute | solution.py:626
  35.0 0.8 %collective-permute-done.1.code_ref = s16[784,128]{1,0:T(8,128)(2,1)S(1)} collective-permute-done((s16[784,128]{1,0:T(8,128)(2,1)S(1)}, s16[784,128]{1,0:T(8,128)(2,1)S(1)}, u32[]{:S(2)}, u32[]{:S(2)}) %collective-permute-start.1) | collective-permute-done | bytes 200736 | tf_op jit(solution)/shard_map/ppermute | solution.py:621
  35.8 3.3 %collective-permute-start.4 = (s16[784,128]{1,0:T(8,128)(2,1)S(1)}, s16[784,128]{1,0:T(8,128)(2,1)S(1)}, u32[]{:S(2)}, u32[]{:S(2)}) collective-permute-start(s16[784,128]{1,0:T(8,128)(2,1)S(1)} %collective-permute-done.1.code_ref), channel_id=1, source_target_pairs={{0,2},{2,0},{4,6},{6,4},{8,10},{10,8},{12,14},{14,12},{16,18},{18,... | collective-permute-start | bytes 602120 | tf_op jit(solution)/shard_map/ppermute | solution.py:627
  39.1 0.8 %far_node.1 = (f32[256,512]{1,0:T(8,128)S(1)}, f32[256,2,512]{2,1,0:T(2,128)S(1)}) custom-call(f32[256,512]{1,0:T(8,128)S(1)} %near_node.1.near_ref, f32[256,512]{1,0:T(8,128)S(1)} %get-tuple-element.18.own_ref, s16[784,128]{1,0:T(8,128)(2,1)S(1)} %collective-permute-done.1.code_ref), custom_call_target="tpu_custom_call" | custom-call | flops 20000000000 | bytes 1048576 | tf_op jit(solution)/shard_map/far_node/pallas_call | solution.py:629
  39.9 0.0 collective-permute-done.3.their_own_ref
  40.0 0.2 collective-permute-done.4.code_ref
  40.2 0.0 collective-permute-done.2.their_near_ref
  40.2 0.0 copy-done.3
  40.2 2.0 %merge.1 = (f32[256,2,512]{2,1,0:T(2,128)}, f32[256,2,512]{2,1,0:T(2,128)}) custom-call(s32[1,2]{1,0:T(1,128)S(1)} %copy-done.3, f32[256,512]{1,0:T(8,128)S(1)} %near_node.1.near_ref, f32[256,512]{1,0:T(8,128)S(1)} %get-tuple-element.20.far_ref, f32[256,2,512]{2,1,0:T(2,128)S(1)} %get-tuple-element.21.node_ref, ...), custom_call_target="tpu_custom_call" | custom-call | bytes 1048576 | tf_op jit(solution)/shard_map/merge/pallas_call | solution.py:633
Async XLA Ops:
  0.6 16.9 %copy-start.4 = (bf16[256,2,512]{2,1,0:T(2,128)(2,1)S(1)}, bf16[256,2,512]{2,1,0:T(2,128)(2,1)}, u32[]{:S(2)}) copy-start(bf16[256,2,512]{2,1,0:T(2,128)(2,1)} %param.12) | copy-start | bytes 1572868
  3.4 26.7 %all-to-all-start = ((bf16[32,104,128]{2,1,0:T(8,128)(2,1)}), bf16[32,104,128]{2,1,0:T(8,128)(2,1)S(1)}, u32[]{:S(2)}, u32[]{:S(2)}) async-start(bf16[32,104,128]{2,1,0:T(8,128)(2,1)} %bucket.1), calls=%async_computation | async-start | bytes 1703936 | tf_op jit(solution)/shard_map/all_to_all | solution.py:590
  9.7 2.2 %copy-start = (bf16[2,8,256,512]{3,2,1,0:T(8,128)(2,1)S(1)}, bf16[2,8,256,512]{3,2,1,0:T(8,128)(2,1)}, u32[]{:S(2)}) copy-start(bf16[2,8,256,512]{3,2,1,0:T(8,128)(2,1)} %rows_hbm.4) | copy-start | bytes 12582916
  11.9 0.7 %copy-start.1 = (bf16[2,8,256]{2,1,0:T(8,128)(2,1)S(1)}, bf16[2,8,256]{2,1,0:T(8,128)(2,1)}, u32[]{:S(2)}) copy-start(bf16[2,8,256]{2,1,0:T(8,128)(2,1)} %weight_hbm.4) | copy-start | bytes 24580
  12.6 0.7 %copy-start.2 = (s32[2]{0:T(128)S(1)}, s32[2]{0:T(128)}, u32[]{:S(2)}) copy-start(s32[2]{0:T(128)} %branching_ref.3) | copy-start | bytes 28
  16.2 16.5 %collective-permute-start = (s16[784,128]{1,0:T(8,128)(2,1)S(1)}, s16[784,128]{1,0:T(8,128)(2,1)S(1)}, u32[]{:S(2)}, u32[]{:S(2)}) collective-permute-start(s16[784,128]{1,0:T(8,128)(2,1)S(1)} %get-tuple-element.17), channel_id=1, source_target_pairs={{0,1},{1,0},{2,3},{3,2},{4,5},{5,4},{6,7},{7,6},{8,9},{9,8},{10,11... | collective-permute-start | bytes 602120 | tf_op jit(solution)/shard_map/ppermute | solution.py:608
  20.4 19.5 %collective-permute-start.3 = (f32[256,512]{1,0:T(8,128)S(1)}, f32[256,512]{1,0:T(8,128)S(1)}, u32[]{:S(2)}, u32[]{:S(2)}) collective-permute-start(f32[256,512]{1,0:T(8,128)S(1)} %get-tuple-element.18.own_ref), channel_id=1, source_target_pairs={{0,2},{2,0},{4,6},{6,4},{8,10},{10,8},{12,14},{14,12},{16,18},{18,... | collective-permute-start | bytes 1572872 | tf_op jit(solution)/shard_map/ppermute | solution.py:613
  31.1 4.7 %collective-permute-start.1 = (s16[784,128]{1,0:T(8,128)(2,1)S(1)}, s16[784,128]{1,0:T(8,128)(2,1)S(1)}, u32[]{:S(2)}, u32[]{:S(2)}) collective-permute-start(s16[784,128]{1,0:T(8,128)(2,1)S(1)} %get-tuple-element.19), channel_id=1, source_target_pairs={{0,1},{1,0},{2,3},{3,2},{4,5},{5,4},{6,7},{7,6},{8,9},{9,8},{10,11... | collective-permute-start | bytes 602120 | tf_op jit(solution)/shard_map/ppermute | solution.py:621
  33.2 7.0 %copy-start.3 = (s32[1,2]{1,0:T(1,128)S(1)}, s32[1,2]{1,0:T(1,128)}, u32[]{:S(2)}) copy-start(s32[1,2]{1,0:T(1,128)} %sibling_ref.1) | copy-start | bytes 28
  33.2 7.0 %collective-permute-start.2 = (f32[256,512]{1,0:T(8,128)S(1)}, f32[256,512]{1,0:T(8,128)S(1)}, u32[]{:S(2)}, u32[]{:S(2)}) collective-permute-start(f32[256,512]{1,0:T(8,128)S(1)} %near_node.1.near_ref), channel_id=1, source_target_pairs={{0,2},{2,0},{4,6},{6,4},{8,10},{10,8},{12,14},{14,12},{16,18},{18,... | collective-permute-start | bytes 1572872 | tf_op jit(solution)/shard_map/ppermute | solution.py:626
  35.8 4.4 %collective-permute-start.4 = (s16[784,128]{1,0:T(8,128)(2,1)S(1)}, s16[784,128]{1,0:T(8,128)(2,1)S(1)}, u32[]{:S(2)}, u32[]{:S(2)}) collective-permute-start(s16[784,128]{1,0:T(8,128)(2,1)S(1)} %collective-permute-done.1.code_ref), channel_id=1, source_target_pairs={{0,2},{2,0},{4,6},{6,4},{8,10},{10,8},{12,14},{14,12},{16,18},{18,... | collective-permute-start | bytes 602120 | tf_op jit(solution)/shard_map/ppermute | solution.py:627

commit v7 on v6

--- a/solution.py
+++ b/solution.py
@@ -58,11 +58,10 @@
 
 def bucket_kernel(plan, route_hbm, weight_hbm, rows_hbm, out_hbm, route_ref, weight_ref, rows_ref, out_ref, sems):
     count = rows_hbm.shape[0]
-    state = plan.state
     copies = [
         pltpu.make_async_copy(route_hbm, route_ref, sems.at[0]),
         pltpu.make_async_copy(weight_hbm, weight_ref, sems.at[1]),
-        pltpu.make_async_copy(rows_hbm, rows_ref.at[:, pl.ds(0, state)], sems.at[2]),
+        pltpu.make_async_copy(rows_hbm, rows_ref, sems.at[2]),
     ]
     for copy in copies:
         copy.start()
@@ -84,8 +83,7 @@
         plan.node_dev * plan.full + q * plan.rest + position - plan.full,
     )
     copies[1].wait()
-    weight = weight_ref[...].reshape(1, count)
-    rows_ref[:, state:] = dot_t(weight, jnp.ones((1, LANES), BF16)).astype(BF16)
+    weight = weight_ref[...].reshape(1, count).astype(F32)
     lane = lax.broadcasted_iota(I32, (EXTRA, LANES), 1)
     sub = lax.broadcasted_iota(I32, (EXTRA, LANES), 0)
     want = []
@@ -102,9 +100,8 @@
     for p in range(PIECES):
         place = lax.broadcasted_iota(I32, (each * plan.rows, count), 0) + p * each * plan.rows
         hit = jnp.where(place == slot, 1.0, 0.0).astype(BF16)
-        filled = jnp.dot(hit, rows_ref[...], preferred_element_type=F32)
-        weights = filled[:, state:]
-        filled = filled[:, :state].astype(BF16)
+        weights = jnp.sum(jnp.where(place == slot, weight, 0.0), axis=1, keepdims=True) + jnp.zeros((1, LANES), F32)
+        filled = jnp.dot(hit, rows_ref[...], preferred_element_type=F32).astype(BF16)
         for i in range(each):
             at = i * plan.rows
             d = p * each + i
@@ -260,15 +257,17 @@
 def decode_node(code_ref):
     half = code_ref.shape[1]
     lines = from_code(code_ref[6 * half :, :])
-    step = jnp.transpose(jnp.exp2(0.125 * jnp.broadcast_to(lines[0:1, :], (8, half))) * (1.0 / CODE))[:, 0:1]
-    pieces = [from_code(code_ref[k * half : (k + 1) * half, :]) * step for k in range(6)]
+    line = jnp.exp2(0.125 * jnp.broadcast_to(lines[0:1, :], (half, half))) * (1.0 / CODE)
+    step = jnp.transpose(line)
+    raw = [from_code(code_ref[k * half : (k + 1) * half, :]) for k in range(6)]
+    turned, mirror = (jnp.transpose(r) * line for r in raw[:2])
+    pieces = [r * step for r in raw]
     both = pieces[0]
-    turned = jnp.transpose(both)
     row = lax.broadcasted_iota(I32, (half, half), 0)
     column = lax.broadcasted_iota(I32, (half, half), 1)
     upper = jnp.where(column >= row, both, turned)
-    lower = jnp.where(column < row, both, jnp.where(column == row, lines[1:2, :] * step, turned))
-    square = ((upper, pieces[1]), (jnp.transpose(pieces[1]), lower))
+    lower = jnp.where(column < row, both, jnp.where(column == row, lines[1:2, :] * line, turned))
+    square = ((upper, pieces[1]), (mirror, lower))
     beside = ((pieces[2], pieces[3]), (pieces[4], pieces[5]))
     return square, beside
 
@@ -334,26 +333,27 @@
     far_out[...] = far_ref[...] + block_ref[1 - node].astype(F32)
 
 
+def weighted(plan, got_ref, plain_ref, columns, scaled_ref):
+    cap = plan.rows
+    for d in range(0, plan.leaf_count, 2):
+        extras = [got_ref[d + i, plan.slabs * cap :, :].astype(F32) for i in range(2)]
+        weight = jnp.concatenate([e[:, g : g + 1] for e in extras for g in range(cap // EXTRA)], axis=0)
+        weight = jnp.broadcast_to(weight, (2 * cap, scaled_ref.shape[1])).astype(BF16)
+        rows = slice(d * cap, (d + 2) * cap)
+        scaled_ref[rows, :] = plain_ref[rows, columns] * weight
+
+
 def send_folded(plan, got_ref, part_ref, code_ref, plain_ref, scaled_ref):
     share = part_ref.shape[0]
     mine, theirs = halves(lax.axis_index("blk"), share)
     cap = plan.rows
     for d in range(0, plan.leaf_count, 2):
-        blocks = [got_ref[d + i].astype(F32) for i in range(2)]
-        weight = jnp.concatenate(
-            [
-                block[plan.slabs * cap :, g : g + 1]
-                for block in blocks
-                for g in range(cap // EXTRA)
-            ],
-            axis=0,
-        )
-        at = d * cap
         for c in range(plan.slabs):
-            rows = jnp.concatenate([block[c * cap : (c + 1) * cap, :] for block in blocks], axis=0)
-            plain_ref[at : at + 2 * cap, c * LANES : (c + 1) * LANES] = rows.astype(BF16)
-            scaled_ref[at : at + 2 * cap, c * LANES : (c + 1) * LANES] = (rows * weight).astype(BF16)
-    scaled = scaled_ref[:, theirs]
+            plain_ref[d * cap : (d + 2) * cap, c * LANES : (c + 1) * LANES] = jnp.concatenate(
+                [got_ref[d + i, c * cap : (c + 1) * cap, :] for i in range(2)], axis=0
+            )
+    weighted(plan, got_ref, plain_ref, theirs, scaled_ref)
+    scaled = scaled_ref[...]
     encode_node(
         code_ref,
         part_ref[:, theirs] + dot_t(scaled, plain_ref[:, theirs]),
@@ -376,10 +376,10 @@
             yield i, k, slice(i * half, (i + 1) * half), slice(k * half, (k + 1) * half)
 
 
-def near_node_kernel(own_ref, plain_ref, scaled_ref, code_ref, node_ref):
-    share = own_ref.shape[0]
-    mine, _ = halves(lax.axis_index("blk"), share)
-    node_ref[...] = own_ref[...] + dot_t(scaled_ref[:, mine], plain_ref[...])
+def near_node_kernel(plan, own_ref, got_ref, plain_ref, code_ref, node_ref, scaled_ref):
+    mine, _ = halves(lax.axis_index("blk"), own_ref.shape[0])
+    weighted(plan, got_ref, plain_ref, mine, scaled_ref)
+    node_ref[...] = own_ref[...] + dot_t(scaled_ref[...], plain_ref[...])
     terms = in_columns(lax.axis_index("blk"), *decode_node(code_ref))
     for i, k, rows, columns in tiles_of(node_ref):
         node_ref[rows, columns] += terms[i][k]
@@ -525,7 +525,7 @@
             scratch_shapes=[
                 pltpu.VMEM((1, count), I32),
                 pltpu.VMEM((count,), BF16),
-                pltpu.VMEM((count, state + LANES), BF16),
+                pltpu.VMEM((count, state), BF16),
                 pltpu.VMEM((plan.leaf_count, plan.block, LANES), BF16),
                 pltpu.SemaphoreType.DMA((3 + PIECES,)),
             ],
@@ -611,18 +611,24 @@
             near_leaf_kernel, (rows, rows, rows), [SMEM, any_spec, any_spec, VMEM, VMEM], **leaf
         )(branching, leaf_weight, leaf_rows, own_block, far_own)
     their_own = lax.ppermute(far_own, SPLIT, to_partner)
+    half_scaled = pltpu.VMEM((nodes * plan.rows, share), BF16)
     with jax.named_scope("routed_send"):
-        code, plain, scaled = call(
+        code, plain = call(
             functools.partial(send_folded, plan),
-            (codes, gathered, gathered),
+            (codes, gathered),
             [VMEM, VMEM],
+            scratch_shapes=[half_scaled],
             flops=2 * nodes * plan.rows * share * state,
         )(got, send_part)
     arrived = lax.ppermute(code, "blk", across)
     with jax.named_scope("near_node"):
-        near = call(near_node_kernel, rows, [VMEM, VMEM, VMEM, VMEM], flops=LONG)(
-            near_own, plain, scaled, near_code
-        )
+        near = call(
+            functools.partial(near_node_kernel, plan),
+            rows,
+            [VMEM] * 4,
+            scratch_shapes=[half_scaled],
+            flops=LONG,
+        )(near_own, got, plain, near_code)
     their_near = lax.ppermute(near, SPLIT, to_partner)
     their_arrived = lax.ppermute(arrived, SPLIT, to_partner)
     with jax.named_scope("far_node"):

time: 42.5 us -> 41.8 us (0.984)
  Pallas kernels: 12.9 us -> 9.67 us
  starting transfers between devices: 16.3 us -> 17.6 us
  waiting for transfers between devices: 8.71 us -> 9.83 us
    ppermute x1, starting transfers between devices: 2 us -> 3.36 us  [shards_folded(): their_own = lax.ppermute(far_own, SPLIT, to_partner)]
    pallas_call x1, Pallas kernels: 2.93 us -> 1.59 us  [shards_folded(): call(far_leaf_kernel, (rows, codes), [SMEM, any_spec, any_spec], **leaf)]
    pallas_call x1, Pallas kernels: 2.88 us -> 1.55 us  [shards_folded(): call(near_leaf_kernel, (rows, rows, rows), [SMEM, any_spec, any_spec, VME...]
    all_to_all x1, waiting for transfers between devices: 7.67 us -> 8.98 us  [shards_folded(): got = lax.all_to_all(blocks, ORDER, split_axis=0, concat_axis=0, tiled=True)]
  transfers between devices with their start and end apart: 6 -> 6, of which waited for: 3 -> 3; matrix products, arithmetic and copies ran while one was open for 0% -> 0% of each run, Pallas kernels for 19% -> 13%
where the time goes in v7:
time: 41.8 us; the launch traced here: 41.4 us
  starting transfers between devices  17.6 us (42%)
  waiting for transfers between devices  9.83 us (24%)
  Pallas kernels  9.67 us (23%)
  local copies, waits for them, and re-layouts  3.6 us (9%)
  between operations  0.73 us (2%)
    all_to_all x1, waiting for transfers between devices, shards_folded(): got = lax.all_to_all(blocks, ORDER, split_axis=0, concat_axis=0, tiled=True)  8.98 us
    all_to_all x1, starting transfers between devices, shards_folded(): got = lax.all_to_all(blocks, ORDER, split_axis=0, concat_axis=0, tiled=True)  6.36 us
    unnamed x11, local copies, waits for them, and re-layouts  3.6 us
    ppermute x1, starting transfers between devices, shards_folded(): their_own = lax.ppermute(far_own, SPLIT, to_partner)  3.36 us
    ppermute x1, starting transfers between devices, shards_folded(): their_arrived = lax.ppermute(arrived, SPLIT, to_partner)  3.29 us
    pallas_call x1, Pallas kernels, bucket(): call(functools.partial(bucket_kernel, plan), jax.ShapeDtypeStruct((plan.l...  2.47 us
    ppermute x1, starting transfers between devices, shards_folded(): their_near = lax.ppermute(near, SPLIT, to_partner)  1.79 us
    pallas_call x1, Pallas kernels, shards_folded(): call(merge_folded, (result, result), [VMEM] * 7, out_specs=(any_spec, any...  1.68 us
  transfers between devices with their start and end apart: 6, of which 3 were waited for; matrix products, arithmetic and copies ran while one was open for 0% of the time, Pallas kernels for 13%

profile of v7, /device:TPU:9, one launch (start us, length us, event | category | flops | bytes accessed | tf_op | source)
XLA Modules:
  0.0 41.4 jit_solution(10193989973976353715)
XLA Ops:
  0.6 0.0 copy-start.4
  0.6 2.5 %bucket.1 = bf16[32,104,128]{2,1,0:T(8,128)(2,1)} custom-call(s32[1,512]{1,0:T(1,128)} %bitcast.5, bf16[512]{0:T(512)(128)(2,1)} %weight_hbm.5, bf16[512,512]{1,0:T(8,128)(2,1)} %rows_hbm.5), custom_call_target="tpu_custom_call" | custom-call | flops 402653184 | bytes 1048576 | tf_op jit(solution)/shard_map/bucket/pallas_call | solution.py:521
  3.1 6.4 %all-to-all-start = ((bf16[32,104,128]{2,1,0:T(8,128)(2,1)}), bf16[32,104,128]{2,1,0:T(8,128)(2,1)S(1)}, u32[]{:S(2)}, u32[]{:S(2)}) async-start(bf16[32,104,128]{2,1,0:T(8,128)(2,1)} %bucket.1), calls=%async_computation | async-start | bytes 1703936 | tf_op jit(solution)/shard_map/all_to_all | solution.py:590
  9.5 0.0 copy-start
  9.5 2.2 %copy-done = bf16[2,8,256,512]{3,2,1,0:T(8,128)(2,1)S(1)} copy-done((bf16[2,8,256,512]{3,2,1,0:T(8,128)(2,1)S(1)}, bf16[2,8,256,512]{3,2,1,0:T(8,128)(2,1)}, u32[]{:S(2)}) %copy-start) | copy-done | bytes 4194328
  11.7 0.0 copy-start.1
  11.7 0.7 %copy-done.1 = bf16[2,8,256]{2,1,0:T(8,128)(2,1)S(1)} copy-done((bf16[2,8,256]{2,1,0:T(8,128)(2,1)S(1)}, bf16[2,8,256]{2,1,0:T(8,128)(2,1)}, u32[]{:S(2)}) %copy-start.1) | copy-done | bytes 8216
  12.4 0.0 copy-start.2
  12.4 0.7 %copy-done.2 = s32[2]{0:T(128)S(1)} copy-done((s32[2]{0:T(128)S(1)}, s32[2]{0:T(128)}, u32[]{:S(2)}) %copy-start.2) | copy-done | bytes 32
  13.0 1.6 %far_leaf_products.1 = (f32[256,512]{1,0:T(8,128)S(1)}, s16[784,128]{1,0:T(8,128)(2,1)S(1)}) custom-call(s32[2]{0:T(128)S(1)} %copy-done.2, bf16[2,8,256]{2,1,0:T(8,128)(2,1)S(1)} %copy-done.1, bf16[2,8,256,512]{3,2,1,0:T(8,128)(2,1)S(1)} %copy-done), custom_call_target="tpu_custom_call" | custom-call | flops 1 | bytes 1 | tf_op jit(solution)/shard_map/far_leaf_products/pallas_call | solution.py:605
  14.6 1.2 %collective-permute-start = (s16[784,128]{1,0:T(8,128)(2,1)S(1)}, s16[784,128]{1,0:T(8,128)(2,1)S(1)}, u32[]{:S(2)}, u32[]{:S(2)}) collective-permute-start(s16[784,128]{1,0:T(8,128)(2,1)S(1)} %get-tuple-element.15), channel_id=1, source_target_pairs={{0,1},{1,0},{2,3},{3,2},{4,5},{5,4},{6,7},{7,6},{8,9},{9,8},{10,11... | collective-permute-start | bytes 602120 | tf_op jit(solution)/shard_map/ppermute | solution.py:608
  15.9 0.0 copy-done.4
  15.9 0.1 copy.12
  15.9 1.5 %near_leaf_products.1 = (f32[256,512]{1,0:T(8,128)S(1)}, f32[256,512]{1,0:T(8,128)S(1)}, f32[256,512]{1,0:T(8,128)S(1)}) custom-call(s32[2]{0:T(128)S(1)} %copy-done.2, bf16[2,8,256]{2,1,0:T(8,128)(2,1)S(1)} %copy-done.1, bf16[2,8,256,512]{3,2,1,0:T(8,128)(2,1)S(1)} %copy-done, bf16[2,256,512]{2,1,0:T(8,128)(2,1)S(1)} %bitcast.4, ...), custom_call_target="tpu_custom_call" | custom-call | flops 1 | bytes 1 | tf_op jit(solution)/shard_map/near_leaf_products/pallas_call | solution.py:610
  17.5 3.4 %collective-permute-start.3 = (f32[256,512]{1,0:T(8,128)S(1)}, f32[256,512]{1,0:T(8,128)S(1)}, u32[]{:S(2)}, u32[]{:S(2)}) collective-permute-start(f32[256,512]{1,0:T(8,128)S(1)} %get-tuple-element.16.own_ref), channel_id=1, source_target_pairs={{0,2},{2,0},{4,6},{6,4},{8,10},{10,8},{12,14},{14,12},{16,18},{18,... | collective-permute-start | bytes 1572872 | tf_op jit(solution)/shard_map/ppermute | solution.py:613
  20.9 9.0 %all-to-all-done.got_ref = bf16[32,104,128]{2,1,0:T(8,128)(2,1)S(1)} async-done(((bf16[32,104,128]{2,1,0:T(8,128)(2,1)}), bf16[32,104,128]{2,1,0:T(8,128)(2,1)S(1)}, u32[]{:S(2)}, u32[]{:S(2)}) %all-to-all-start) | async-done | bytes 852000 | tf_op jit(solution)/shard_map/all_to_all | solution.py:590
  29.8 0.9 %routed_send.1 = (s16[784,128]{1,0:T(8,128)(2,1)S(1)}, bf16[768,512]{1,0:T(8,128)(2,1)S(1)}) custom-call(bf16[32,104,128]{2,1,0:T(8,128)(2,1)S(1)} %all-to-all-done.got_ref, f32[256,512]{1,0:T(8,128)S(1)} %get-tuple-element.13.part_ref), custom_call_target="tpu_custom_call" | custom-call | flops 201326592 | bytes 1048576 | tf_op jit(solution)/shard_map/routed_send/pallas_call | solution.py:616
  30.7 1.6 %collective-permute-start.1 = (s16[784,128]{1,0:T(8,128)(2,1)S(1)}, s16[784,128]{1,0:T(8,128)(2,1)S(1)}, u32[]{:S(2)}, u32[]{:S(2)}) collective-permute-start(s16[784,128]{1,0:T(8,128)(2,1)S(1)} %get-tuple-element.17), channel_id=1, source_target_pairs={{0,1},{1,0},{2,3},{3,2},{4,5},{5,4},{6,7},{7,6},{8,9},{9,8},{10,11... | collective-permute-start | bytes 602120 | tf_op jit(solution)/shard_map/ppermute | solution.py:623
  32.3 0.0 collective-permute-done.code_ref
  32.3 0.7 %near_node.1.near_ref = f32[256,512]{1,0:T(8,128)S(1)} custom-call(f32[256,512]{1,0:T(8,128)S(1)} %get-tuple-element.12.own_ref, bf16[32,104,128]{2,1,0:T(8,128)(2,1)S(1)} %all-to-all-done.got_ref, bf16[768,512]{1,0:T(8,128)(2,1)S(1)} %get-tuple-element.14.plain_ref, s16[784,128]{1,0:T(8,128)(2,1)S(1)} %collective-permute-done.code_ref), custom_call_target="tpu_custom_call" | custom-call | flops 20000000000 | bytes 1048576 | tf_op jit(solution)/shard_map/near_node/pallas_call | solution.py:625
  33.0 0.0 copy-start.3
  33.0 1.8 %collective-permute-start.2 = (f32[256,512]{1,0:T(8,128)S(1)}, f32[256,512]{1,0:T(8,128)S(1)}, u32[]{:S(2)}, u32[]{:S(2)}) collective-permute-start(f32[256,512]{1,0:T(8,128)S(1)} %near_node.1.near_ref), channel_id=1, source_target_pairs={{0,2},{2,0},{4,6},{6,4},{8,10},{10,8},{12,14},{14,12},{16,18},{18,... | collective-permute-start | bytes 1572872 | tf_op jit(solution)/shard_map/ppermute | solution.py:632
  34.8 0.6 %collective-permute-done.1.code_ref = s16[784,128]{1,0:T(8,128)(2,1)S(1)} collective-permute-done((s16[784,128]{1,0:T(8,128)(2,1)S(1)}, s16[784,128]{1,0:T(8,128)(2,1)S(1)}, u32[]{:S(2)}, u32[]{:S(2)}) %collective-permute-start.1) | collective-permute-done | bytes 200736 | tf_op jit(solution)/shard_map/ppermute | solution.py:623
  35.4 3.3 %collective-permute-start.4 = (s16[784,128]{1,0:T(8,128)(2,1)S(1)}, s16[784,128]{1,0:T(8,128)(2,1)S(1)}, u32[]{:S(2)}, u32[]{:S(2)}) collective-permute-start(s16[784,128]{1,0:T(8,128)(2,1)S(1)} %collective-permute-done.1.code_ref), channel_id=1, source_target_pairs={{0,2},{2,0},{4,6},{6,4},{8,10},{10,8},{12,14},{14,12},{16,18},{18,... | collective-permute-start | bytes 602120 | tf_op jit(solution)/shard_map/ppermute | solution.py:633
  38.7 0.8 %far_node.1 = (f32[256,512]{1,0:T(8,128)S(1)}, f32[256,2,512]{2,1,0:T(2,128)S(1)}) custom-call(f32[256,512]{1,0:T(8,128)S(1)} %near_node.1.near_ref, f32[256,512]{1,0:T(8,128)S(1)} %get-tuple-element.16.own_ref, s16[784,128]{1,0:T(8,128)(2,1)S(1)} %collective-permute-done.1.code_ref), custom_call_target="tpu_custom_call" | custom-call | flops 20000000000 | bytes 1048576 | tf_op jit(solution)/shard_map/far_node/pallas_call | solution.py:635
  39.5 0.0 collective-permute-done.3.their_own_ref
  39.5 0.3 collective-permute-done.4.code_ref
  39.8 0.0 collective-permute-done.2.their_near_ref
  39.8 0.0 copy-done.3
  39.8 1.7 %merge.1 = (f32[256,2,512]{2,1,0:T(2,128)}, f32[256,2,512]{2,1,0:T(2,128)}) custom-call(s32[1,2]{1,0:T(1,128)S(1)} %copy-done.3, f32[256,512]{1,0:T(8,128)S(1)} %near_node.1.near_ref, f32[256,512]{1,0:T(8,128)S(1)} %get-tuple-element.18.far_ref, f32[256,2,512]{2,1,0:T(2,128)S(1)} %get-tuple-element.19.node_ref, ...), custom_call_target="tpu_custom_call" | custom-call | bytes 1048576 | tf_op jit(solution)/shard_map/merge/pallas_call | solution.py:639
Async XLA Ops:
  0.6 15.3 %copy-start.4 = (bf16[256,2,512]{2,1,0:T(2,128)(2,1)S(1)}, bf16[256,2,512]{2,1,0:T(2,128)(2,1)}, u32[]{:S(2)}) copy-start(bf16[256,2,512]{2,1,0:T(2,128)(2,1)} %param.12) | copy-start | bytes 1572868
  3.1 26.7 %all-to-all-start = ((bf16[32,104,128]{2,1,0:T(8,128)(2,1)}), bf16[32,104,128]{2,1,0:T(8,128)(2,1)S(1)}, u32[]{:S(2)}, u32[]{:S(2)}) async-start(bf16[32,104,128]{2,1,0:T(8,128)(2,1)} %bucket.1), calls=%async_computation | async-start | bytes 1703936 | tf_op jit(solution)/shard_map/all_to_all | solution.py:590
  9.5 2.2 %copy-start = (bf16[2,8,256,512]{3,2,1,0:T(8,128)(2,1)S(1)}, bf16[2,8,256,512]{3,2,1,0:T(8,128)(2,1)}, u32[]{:S(2)}) copy-start(bf16[2,8,256,512]{3,2,1,0:T(8,128)(2,1)} %rows_hbm.4) | copy-start | bytes 12582916
  11.7 0.7 %copy-start.1 = (bf16[2,8,256]{2,1,0:T(8,128)(2,1)S(1)}, bf16[2,8,256]{2,1,0:T(8,128)(2,1)}, u32[]{:S(2)}) copy-start(bf16[2,8,256]{2,1,0:T(8,128)(2,1)} %weight_hbm.4) | copy-start | bytes 24580
  12.4 0.7 %copy-start.2 = (s32[2]{0:T(128)S(1)}, s32[2]{0:T(128)}, u32[]{:S(2)}) copy-start(s32[2]{0:T(128)} %branching_ref.3) | copy-start | bytes 28
  14.6 17.6 %collective-permute-start = (s16[784,128]{1,0:T(8,128)(2,1)S(1)}, s16[784,128]{1,0:T(8,128)(2,1)S(1)}, u32[]{:S(2)}, u32[]{:S(2)}) collective-permute-start(s16[784,128]{1,0:T(8,128)(2,1)S(1)} %get-tuple-element.15), channel_id=1, source_target_pairs={{0,1},{1,0},{2,3},{3,2},{4,5},{5,4},{6,7},{7,6},{8,9},{9,8},{10,11... | collective-permute-start | bytes 602120 | tf_op jit(solution)/shard_map/ppermute | solution.py:608
  17.5 22.0 %collective-permute-start.3 = (f32[256,512]{1,0:T(8,128)S(1)}, f32[256,512]{1,0:T(8,128)S(1)}, u32[]{:S(2)}, u32[]{:S(2)}) collective-permute-start(f32[256,512]{1,0:T(8,128)S(1)} %get-tuple-element.16.own_ref), channel_id=1, source_target_pairs={{0,2},{2,0},{4,6},{6,4},{8,10},{10,8},{12,14},{14,12},{16,18},{18,... | collective-permute-start | bytes 1572872 | tf_op jit(solution)/shard_map/ppermute | solution.py:613
  30.7 4.7 %collective-permute-start.1 = (s16[784,128]{1,0:T(8,128)(2,1)S(1)}, s16[784,128]{1,0:T(8,128)(2,1)S(1)}, u32[]{:S(2)}, u32[]{:S(2)}) collective-permute-start(s16[784,128]{1,0:T(8,128)(2,1)S(1)} %get-tuple-element.17), channel_id=1, source_target_pairs={{0,1},{1,0},{2,3},{3,2},{4,5},{5,4},{6,7},{7,6},{8,9},{9,8},{10,11... | collective-permute-start | bytes 602120 | tf_op jit(solution)/shard_map/ppermute | solution.py:623
  33.0 6.8 %copy-start.3 = (s32[1,2]{1,0:T(1,128)S(1)}, s32[1,2]{1,0:T(1,128)}, u32[]{:S(2)}) copy-start(s32[1,2]{1,0:T(1,128)} %sibling_ref.1) | copy-start | bytes 28
  33.0 6.8 %collective-permute-start.2 = (f32[256,512]{1,0:T(8,128)S(1)}, f32[256,512]{1,0:T(8,128)S(1)}, u32[]{:S(2)}, u32[]{:S(2)}) collective-permute-start(f32[256,512]{1,0:T(8,128)S(1)} %near_node.1.near_ref), channel_id=1, source_target_pairs={{0,2},{2,0},{4,6},{6,4},{8,10},{10,8},{12,14},{14,12},{16,18},{18,... | collective-permute-start | bytes 1572872 | tf_op jit(solution)/shard_map/ppermute | solution.py:632
  35.4 4.4 %collective-permute-start.4 = (s16[784,128]{1,0:T(8,128)(2,1)S(1)}, s16[784,128]{1,0:T(8,128)(2,1)S(1)}, u32[]{:S(2)}, u32[]{:S(2)}) collective-permute-start(s16[784,128]{1,0:T(8,128)(2,1)S(1)} %collective-permute-done.1.code_ref), channel_id=1, source_target_pairs={{0,2},{2,0},{4,6},{6,4},{8,10},{10,8},{12,14},{14,12},{16,18},{18,... | collective-permute-start | bytes 602120 | tf_op jit(solution)/shard_map/ppermute | solution.py:633

commit v8 on v7

--- a/solution.py
+++ b/solution.py
@@ -206,7 +206,8 @@
     peers, nodes, share, state = part_ref.shape
     gather_rows(plan, got_ref, plain_ref, scaled_ref)
     for q in range(nodes):
-        product = Product(scaled_ref.at[q], plain_ref.at[q], total)
+        filled = pl.ds(0, plan.depth[q])
+        product = Product(scaled_ref.at[q, filled], plain_ref.at[q, filled], total)
         for e in range(1, peers + 1):
             at = pl.multiple_of((blk ^ e) * share, share)
             value = part_ref[e - 1, q] + product.rows(at, share)
@@ -426,11 +427,13 @@
         copy.wait()
 
 
-def own_kernel(place_ref, part_ref, plain_ref, scaled_ref, own_ref, total=None):
+def own_kernel(plan, place_ref, part_ref, plain_ref, scaled_ref, own_ref, total=None):
     nodes, share, _ = part_ref.shape
     at = pl.multiple_of(place_ref[0] * share, share)
     for q in range(nodes):
-        own_ref[q] = part_ref[q] + Product(scaled_ref.at[q], plain_ref.at[q], total).rows(at, share)
+        filled = pl.ds(0, plan.depth[q])
+        product = Product(scaled_ref.at[q, filled], plain_ref.at[q, filled], total)
+        own_ref[q] = part_ref[q] + product.rows(at, share)
 
 
 def node_kernel(own_ref, code_ref, out_ref, node_ref):
@@ -490,7 +493,7 @@
     )
     with jax.named_scope("routed_own"):
         own = call(
-            own_kernel,
+            functools.partial(own_kernel, plan),
             shape((node_dev, share, state), F32),
             [SMEM, VMEM, VMEM, VMEM],
             scratch_shapes=whole,

time: 41.8 us -> 41.8 us (level)
  starting transfers between devices: 17.6 us -> 15 us
  waiting for transfers between devices: 9.83 us -> 11.8 us
  Pallas kernels: 9.67 us -> 10.3 us
    ppermute x1, starting transfers between devices: 3.36 us -> 0.07 us  [shards_folded(): their_own = lax.ppermute(far_own, SPLIT, to_partner)]
    all_to_all x1, waiting for transfers between devices: 8.98 us -> 10.9 us  [shards_folded(): got = lax.all_to_all(blocks, ORDER, split_axis=0, concat_axis=0, tiled=True)]
    pallas_call x1, Pallas kernels: 1.55 us -> 2.21 us  [shards_folded(): call(near_leaf_kernel, (rows, rows, rows), [SMEM, any_spec, any_spec, VME...]
    ppermute x1, starting transfers between devices: 1.25 us -> 1.92 us  [shards_folded(): near_code = lax.ppermute(far_code, 'blk', across)]
  transfers between devices with their start and end apart: 6 -> 6, of which waited for: 3 -> 3; matrix products, arithmetic and copies ran while one was open for 0% -> 0% of each run, Pallas kernels for 13% -> 15%
where the time goes in v8:
time: 41.8 us; the launch traced here: 41.4 us
  starting transfers between devices  15 us (36%)
  waiting for transfers between devices  11.8 us (28%)
  Pallas kernels  10.3 us (25%)
  local copies, waits for them, and re-layouts  3.6 us (9%)
  between operations  0.73 us (2%)
    all_to_all x1, waiting for transfers between devices, shards_folded(): got = lax.all_to_all(blocks, ORDER, split_axis=0, concat_axis=0, tiled=True)  10.9 us
    all_to_all x1, starting transfers between devices, shards_folded(): got = lax.all_to_all(blocks, ORDER, split_axis=0, concat_axis=0, tiled=True)  6.36 us
    unnamed x11, local copies, waits for them, and re-layouts  3.6 us
    ppermute x1, starting transfers between devices, shards_folded(): their_arrived = lax.ppermute(arrived, SPLIT, to_partner)  3.29 us
    pallas_call x1, Pallas kernels, bucket(): call(functools.partial(bucket_kernel, plan), jax.ShapeDtypeStruct((plan.l...  2.47 us
    pallas_call x1, Pallas kernels, shards_folded(): call(near_leaf_kernel, (rows, rows, rows), [SMEM, any_spec, any_spec, VME...  2.21 us
    ppermute x1, starting transfers between devices, shards_folded(): near_code = lax.ppermute(far_code, 'blk', across)  1.92 us
    ppermute x1, starting transfers between devices, shards_folded(): their_near = lax.ppermute(near, SPLIT, to_partner)  1.79 us
  transfers between devices with their start and end apart: 6, of which 3 were waited for; matrix products, arithmetic and copies ran while one was open for 0% of the time, Pallas kernels for 15%

profile of v8, /device:TPU:9, one launch (start us, length us, event | category | flops | bytes accessed | tf_op | source)
XLA Modules:
  0.0 41.4 jit_solution(10193989973976353715)
XLA Ops:
  0.6 0.0 copy-start.4
  0.6 2.5 %bucket.1 = bf16[32,104,128]{2,1,0:T(8,128)(2,1)} custom-call(s32[1,512]{1,0:T(1,128)} %bitcast.5, bf16[512]{0:T(512)(128)(2,1)} %weight_hbm.5, bf16[512,512]{1,0:T(8,128)(2,1)} %rows_hbm.5), custom_call_target="tpu_custom_call" | custom-call | flops 402653184 | bytes 1048576 | tf_op jit(solution)/shard_map/bucket/pallas_call | solution.py:524
  3.1 6.4 %all-to-all-start = ((bf16[32,104,128]{2,1,0:T(8,128)(2,1)}), bf16[32,104,128]{2,1,0:T(8,128)(2,1)S(1)}, u32[]{:S(2)}, u32[]{:S(2)}) async-start(bf16[32,104,128]{2,1,0:T(8,128)(2,1)} %bucket.1), calls=%async_computation | async-start | bytes 1703936 | tf_op jit(solution)/shard_map/all_to_all | solution.py:593
  9.5 0.0 copy-start
  9.5 2.2 %copy-done = bf16[2,8,256,512]{3,2,1,0:T(8,128)(2,1)S(1)} copy-done((bf16[2,8,256,512]{3,2,1,0:T(8,128)(2,1)S(1)}, bf16[2,8,256,512]{3,2,1,0:T(8,128)(2,1)}, u32[]{:S(2)}) %copy-start) | copy-done | bytes 4194328
  11.7 0.0 copy-start.1
  11.7 0.7 %copy-done.1 = bf16[2,8,256]{2,1,0:T(8,128)(2,1)S(1)} copy-done((bf16[2,8,256]{2,1,0:T(8,128)(2,1)S(1)}, bf16[2,8,256]{2,1,0:T(8,128)(2,1)}, u32[]{:S(2)}) %copy-start.1) | copy-done | bytes 8216
  12.4 0.0 copy-start.2
  12.4 0.7 %copy-done.2 = s32[2]{0:T(128)S(1)} copy-done((s32[2]{0:T(128)S(1)}, s32[2]{0:T(128)}, u32[]{:S(2)}) %copy-start.2) | copy-done | bytes 32
  13.0 1.6 %far_leaf_products.1 = (f32[256,512]{1,0:T(8,128)S(1)}, s16[784,128]{1,0:T(8,128)(2,1)S(1)}) custom-call(s32[2]{0:T(128)S(1)} %copy-done.2, bf16[2,8,256]{2,1,0:T(8,128)(2,1)S(1)} %copy-done.1, bf16[2,8,256,512]{3,2,1,0:T(8,128)(2,1)S(1)} %copy-done), custom_call_target="tpu_custom_call" | custom-call | flops 1 | bytes 1 | tf_op jit(solution)/shard_map/far_leaf_products/pallas_call | solution.py:608
  14.6 1.9 %collective-permute-start = (s16[784,128]{1,0:T(8,128)(2,1)S(1)}, s16[784,128]{1,0:T(8,128)(2,1)S(1)}, u32[]{:S(2)}, u32[]{:S(2)}) collective-permute-start(s16[784,128]{1,0:T(8,128)(2,1)S(1)} %get-tuple-element.15), channel_id=1, source_target_pairs={{0,1},{1,0},{2,3},{3,2},{4,5},{5,4},{6,7},{7,6},{8,9},{9,8},{10,11... | collective-permute-start | bytes 602120 | tf_op jit(solution)/shard_map/ppermute | solution.py:611
  16.6 0.0 copy-done.4
  16.6 0.1 copy.12
  16.6 2.2 %near_leaf_products.1 = (f32[256,512]{1,0:T(8,128)S(1)}, f32[256,512]{1,0:T(8,128)S(1)}, f32[256,512]{1,0:T(8,128)S(1)}) custom-call(s32[2]{0:T(128)S(1)} %copy-done.2, bf16[2,8,256]{2,1,0:T(8,128)(2,1)S(1)} %copy-done.1, bf16[2,8,256,512]{3,2,1,0:T(8,128)(2,1)S(1)} %copy-done, bf16[2,256,512]{2,1,0:T(8,128)(2,1)S(1)} %bitcast.4, ...), custom_call_target="tpu_custom_call" | custom-call | flops 1 | bytes 1 | tf_op jit(solution)/shard_map/near_leaf_products/pallas_call | solution.py:613
  18.8 0.1 collective-permute-start.3
  18.9 10.9 %all-to-all-done.got_ref = bf16[32,104,128]{2,1,0:T(8,128)(2,1)S(1)} async-done(((bf16[32,104,128]{2,1,0:T(8,128)(2,1)}), bf16[32,104,128]{2,1,0:T(8,128)(2,1)S(1)}, u32[]{:S(2)}, u32[]{:S(2)}) %all-to-all-start) | async-done | bytes 852000 | tf_op jit(solution)/shard_map/all_to_all | solution.py:593
  29.8 0.9 %routed_send.1 = (s16[784,128]{1,0:T(8,128)(2,1)S(1)}, bf16[768,512]{1,0:T(8,128)(2,1)S(1)}) custom-call(bf16[32,104,128]{2,1,0:T(8,128)(2,1)S(1)} %all-to-all-done.got_ref, f32[256,512]{1,0:T(8,128)S(1)} %get-tuple-element.13.part_ref), custom_call_target="tpu_custom_call" | custom-call | flops 201326592 | bytes 1048576 | tf_op jit(solution)/shard_map/routed_send/pallas_call | solution.py:619
  30.7 1.6 %collective-permute-start.1 = (s16[784,128]{1,0:T(8,128)(2,1)S(1)}, s16[784,128]{1,0:T(8,128)(2,1)S(1)}, u32[]{:S(2)}, u32[]{:S(2)}) collective-permute-start(s16[784,128]{1,0:T(8,128)(2,1)S(1)} %get-tuple-element.17), channel_id=1, source_target_pairs={{0,1},{1,0},{2,3},{3,2},{4,5},{5,4},{6,7},{7,6},{8,9},{9,8},{10,11... | collective-permute-start | bytes 602120 | tf_op jit(solution)/shard_map/ppermute | solution.py:626
  32.3 0.0 collective-permute-done.code_ref
  32.3 0.7 %near_node.1.near_ref = f32[256,512]{1,0:T(8,128)S(1)} custom-call(f32[256,512]{1,0:T(8,128)S(1)} %get-tuple-element.12.own_ref, bf16[32,104,128]{2,1,0:T(8,128)(2,1)S(1)} %all-to-all-done.got_ref, bf16[768,512]{1,0:T(8,128)(2,1)S(1)} %get-tuple-element.14.plain_ref, s16[784,128]{1,0:T(8,128)(2,1)S(1)} %collective-permute-done.code_ref), custom_call_target="tpu_custom_call" | custom-call | flops 20000000000 | bytes 1048576 | tf_op jit(solution)/shard_map/near_node/pallas_call | solution.py:628
  33.0 0.0 copy-start.3
  33.0 1.8 %collective-permute-start.2 = (f32[256,512]{1,0:T(8,128)S(1)}, f32[256,512]{1,0:T(8,128)S(1)}, u32[]{:S(2)}, u32[]{:S(2)}) collective-permute-start(f32[256,512]{1,0:T(8,128)S(1)} %near_node.1.near_ref), channel_id=1, source_target_pairs={{0,2},{2,0},{4,6},{6,4},{8,10},{10,8},{12,14},{14,12},{16,18},{18,... | collective-permute-start | bytes 1572872 | tf_op jit(solution)/shard_map/ppermute | solution.py:635
  34.8 0.6 %collective-permute-done.1.code_ref = s16[784,128]{1,0:T(8,128)(2,1)S(1)} collective-permute-done((s16[784,128]{1,0:T(8,128)(2,1)S(1)}, s16[784,128]{1,0:T(8,128)(2,1)S(1)}, u32[]{:S(2)}, u32[]{:S(2)}) %collective-permute-start.1) | collective-permute-done | bytes 200736 | tf_op jit(solution)/shard_map/ppermute | solution.py:626
  35.4 3.3 %collective-permute-start.4 = (s16[784,128]{1,0:T(8,128)(2,1)S(1)}, s16[784,128]{1,0:T(8,128)(2,1)S(1)}, u32[]{:S(2)}, u32[]{:S(2)}) collective-permute-start(s16[784,128]{1,0:T(8,128)(2,1)S(1)} %collective-permute-done.1.code_ref), channel_id=1, source_target_pairs={{0,2},{2,0},{4,6},{6,4},{8,10},{10,8},{12,14},{14,12},{16,18},{18,... | collective-permute-start | bytes 602120 | tf_op jit(solution)/shard_map/ppermute | solution.py:636
  38.7 0.8 %far_node.1 = (f32[256,512]{1,0:T(8,128)S(1)}, f32[256,2,512]{2,1,0:T(2,128)S(1)}) custom-call(f32[256,512]{1,0:T(8,128)S(1)} %near_node.1.near_ref, f32[256,512]{1,0:T(8,128)S(1)} %get-tuple-element.16.own_ref, s16[784,128]{1,0:T(8,128)(2,1)S(1)} %collective-permute-done.1.code_ref), custom_call_target="tpu_custom_call" | custom-call | flops 20000000000 | bytes 1048576 | tf_op jit(solution)/shard_map/far_node/pallas_call | solution.py:638
  39.5 0.0 collective-permute-done.3.their_own_ref
  39.5 0.3 collective-permute-done.4.code_ref
  39.8 0.0 collective-permute-done.2.their_near_ref
  39.8 0.0 copy-done.3
  39.8 1.7 %merge.1 = (f32[256,2,512]{2,1,0:T(2,128)}, f32[256,2,512]{2,1,0:T(2,128)}) custom-call(s32[1,2]{1,0:T(1,128)S(1)} %copy-done.3, f32[256,512]{1,0:T(8,128)S(1)} %near_node.1.near_ref, f32[256,512]{1,0:T(8,128)S(1)} %get-tuple-element.18.far_ref, f32[256,2,512]{2,1,0:T(2,128)S(1)} %get-tuple-element.19.node_ref, ...), custom_call_target="tpu_custom_call" | custom-call | bytes 1048576 | tf_op jit(solution)/shard_map/merge/pallas_call | solution.py:642
Async XLA Ops:
  0.6 15.9 %copy-start.4 = (bf16[256,2,512]{2,1,0:T(2,128)(2,1)S(1)}, bf16[256,2,512]{2,1,0:T(2,128)(2,1)}, u32[]{:S(2)}) copy-start(bf16[256,2,512]{2,1,0:T(2,128)(2,1)} %param.12) | copy-start | bytes 1572868
  3.1 26.7 %all-to-all-start = ((bf16[32,104,128]{2,1,0:T(8,128)(2,1)}), bf16[32,104,128]{2,1,0:T(8,128)(2,1)S(1)}, u32[]{:S(2)}, u32[]{:S(2)}) async-start(bf16[32,104,128]{2,1,0:T(8,128)(2,1)} %bucket.1), calls=%async_computation | async-start | bytes 1703936 | tf_op jit(solution)/shard_map/all_to_all | solution.py:593
  9.5 2.2 %copy-start = (bf16[2,8,256,512]{3,2,1,0:T(8,128)(2,1)S(1)}, bf16[2,8,256,512]{3,2,1,0:T(8,128)(2,1)}, u32[]{:S(2)}) copy-start(bf16[2,8,256,512]{3,2,1,0:T(8,128)(2,1)} %rows_hbm.4) | copy-start | bytes 12582916
  11.7 0.7 %copy-start.1 = (bf16[2,8,256]{2,1,0:T(8,128)(2,1)S(1)}, bf16[2,8,256]{2,1,0:T(8,128)(2,1)}, u32[]{:S(2)}) copy-start(bf16[2,8,256]{2,1,0:T(8,128)(2,1)} %weight_hbm.4) | copy-start | bytes 24580
  12.4 0.7 %copy-start.2 = (s32[2]{0:T(128)S(1)}, s32[2]{0:T(128)}, u32[]{:S(2)}) copy-start(s32[2]{0:T(128)} %branching_ref.3) | copy-start | bytes 28
  14.6 17.6 %collective-permute-start = (s16[784,128]{1,0:T(8,128)(2,1)S(1)}, s16[784,128]{1,0:T(8,128)(2,1)S(1)}, u32[]{:S(2)}, u32[]{:S(2)}) collective-permute-start(s16[784,128]{1,0:T(8,128)(2,1)S(1)} %get-tuple-element.15), channel_id=1, source_target_pairs={{0,1},{1,0},{2,3},{3,2},{4,5},{5,4},{6,7},{7,6},{8,9},{9,8},{10,11... | collective-permute-start | bytes 602120 | tf_op jit(solution)/shard_map/ppermute | solution.py:611
  18.8 20.7 %collective-permute-start.3 = (f32[256,512]{1,0:T(8,128)S(1)}, f32[256,512]{1,0:T(8,128)S(1)}, u32[]{:S(2)}, u32[]{:S(2)}) collective-permute-start(f32[256,512]{1,0:T(8,128)S(1)} %get-tuple-element.16.own_ref), channel_id=1, source_target_pairs={{0,2},{2,0},{4,6},{6,4},{8,10},{10,8},{12,14},{14,12},{16,18},{18,... | collective-permute-start | bytes 1572872 | tf_op jit(solution)/shard_map/ppermute | solution.py:616
  30.7 4.7 %collective-permute-start.1 = (s16[784,128]{1,0:T(8,128)(2,1)S(1)}, s16[784,128]{1,0:T(8,128)(2,1)S(1)}, u32[]{:S(2)}, u32[]{:S(2)}) collective-permute-start(s16[784,128]{1,0:T(8,128)(2,1)S(1)} %get-tuple-element.17), channel_id=1, source_target_pairs={{0,1},{1,0},{2,3},{3,2},{4,5},{5,4},{6,7},{7,6},{8,9},{9,8},{10,11... | collective-permute-start | bytes 602120 | tf_op jit(solution)/shard_map/ppermute | solution.py:626
  33.0 6.8 %copy-start.3 = (s32[1,2]{1,0:T(1,128)S(1)}, s32[1,2]{1,0:T(1,128)}, u32[]{:S(2)}) copy-start(s32[1,2]{1,0:T(1,128)} %sibling_ref.1) | copy-start | bytes 28
  33.0 6.8 %collective-permute-start.2 = (f32[256,512]{1,0:T(8,128)S(1)}, f32[256,512]{1,0:T(8,128)S(1)}, u32[]{:S(2)}, u32[]{:S(2)}) collective-permute-start(f32[256,512]{1,0:T(8,128)S(1)} %near_node.1.near_ref), channel_id=1, source_target_pairs={{0,2},{2,0},{4,6},{6,4},{8,10},{10,8},{12,14},{14,12},{16,18},{18,... | collective-permute-start | bytes 1572872 | tf_op jit(solution)/shard_map/ppermute | solution.py:635
  35.4 4.4 %collective-permute-start.4 = (s16[784,128]{1,0:T(8,128)(2,1)S(1)}, s16[784,128]{1,0:T(8,128)(2,1)S(1)}, u32[]{:S(2)}, u32[]{:S(2)}) collective-permute-start(s16[784,128]{1,0:T(8,128)(2,1)S(1)} %collective-permute-done.1.code_ref), channel_id=1, source_target_pairs={{0,2},{2,0},{4,6},{6,4},{8,10},{10,8},{12,14},{14,12},{16,18},{18,... | collective-permute-start | bytes 602120 | tf_op jit(solution)/shard_map/ppermute | solution.py:636

commit v9 on v8

--- a/solution.py
+++ b/solution.py
@@ -386,40 +386,48 @@
         node_ref[rows, columns] += terms[i][k]
 
 
-def far_node_kernel(near_ref, own_ref, code_ref, node_ref, out_ref):
+def far_node_kernel(near_ref, own_ref, code_ref, far_ref, out_ref):
     first = lax.axis_index("blk") == 0
     terms = in_columns(lax.axis_index("blk"), *decode_node(code_ref))
-    for i, k, rows, columns in tiles_of(node_ref):
+    for i, k, rows, columns in tiles_of(own_ref):
         far = own_ref[rows, columns] + terms[i][k]
         near = near_ref[rows, columns]
-        node_ref[rows, columns] = far
+        far_ref[rows, columns] = far
         out_ref[rows, 0, columns] = jnp.where(first, near, far)
         out_ref[rows, 1, columns] = jnp.where(first, far, near)
 
 
-def merge_folded(
-    sibling_ref, near_ref, far_ref, node_ref, their_near_ref, their_own_ref, code_ref,
-    node_hbm, out_hbm, out_ref, sems,
-):
-    share = far_ref.shape[0]
+def first_awaits(sibling_ref, count):
+    straight = jnp.broadcast_to(sibling_ref[0:1, 0:1], (count, LANES)) == 0
+    return straight != (lax.axis_index("blk") == 0)
+
+
+def base_kernel(sibling_ref, near_ref, far_ref, their_near_ref, their_own_ref, base_ref):
+    first = lax.axis_index("blk") == 0
+    zero = first_awaits(sibling_ref, LANES)
+    for _, _, rows, columns in tiles_of(their_own_ref):
+        near, far = near_ref[rows, columns], far_ref[rows, columns]
+        their_near, their_far = their_near_ref[rows, columns], their_own_ref[rows, columns]
+        base_ref[0, rows, columns] = jnp.where(first, near, far) + jnp.where(zero, their_far, their_near)
+        base_ref[1, rows, columns] = jnp.where(first, far, near) + jnp.where(zero, their_near, their_far)
+
+
+def merge_folded(sibling_ref, node_ref, base_ref, code_ref, node_hbm, out_hbm, out_ref, sems):
+    _, share, state = base_ref.shape
     half = share // 2
     each = share // PIECES
     copies = [pltpu.make_async_copy(node_ref, node_hbm, sems.at[PIECES])]
     copies[0].start()
-    first = lax.axis_index("blk") == 0
-    straight = jnp.broadcast_to(sibling_ref[0:1, 0:1], (each, LANES)) == 0
+    zero = first_awaits(sibling_ref, each)
     terms = in_columns(lax.axis_index("blk"), *decode_node(code_ref))
     for p in range(PIECES):
         rows = slice(p * each, (p + 1) * each)
         inner = slice(p * each % half, p * each % half + each)
-        for k in range(far_ref.shape[1] // half):
+        for k in range(state // half):
             columns = slice(k * half, (k + 1) * half)
-            their_near = their_near_ref[rows, columns]
-            their_far = their_own_ref[rows, columns] + terms[p * each // half][k][inner]
-            near = near_ref[rows, columns] + jnp.where(straight, their_near, their_far)
-            far = far_ref[rows, columns] + jnp.where(straight, their_far, their_near)
-            out_ref[rows, 0, columns] = jnp.where(first, near, far)
-            out_ref[rows, 1, columns] = jnp.where(first, far, near)
+            term = terms[p * each // half][k][inner]
+            out_ref[rows, 0, columns] = base_ref[0, rows, columns] + jnp.where(zero, term, 0.0)
+            out_ref[rows, 1, columns] = base_ref[1, rows, columns] + jnp.where(zero, 0.0, term)
         span = pl.ds(p * each, each)
         copies.append(pltpu.make_async_copy(out_ref.at[span], out_hbm.at[span], sems.at[p]))
         copies[-1].start()
@@ -635,20 +643,22 @@
     their_near = lax.ppermute(near, SPLIT, to_partner)
     their_arrived = lax.ppermute(arrived, SPLIT, to_partner)
     with jax.named_scope("far_node"):
-        far, node = call(far_node_kernel, (rows, result), [VMEM, VMEM, VMEM], flops=LONG)(
-            near, far_own, arrived
+        far, node = call(far_node_kernel, (rows, result), [VMEM] * 3, flops=LONG)(near, far_own, arrived)
+    with jax.named_scope("merge_base"):
+        base = call(base_kernel, shape((node_dev, share, state), F32), [VMEM] * 5, flops=LONG)(
+            sibling, near, far, their_near, their_own
         )
     with jax.named_scope("merge"):
         return call(
             merge_folded,
             (result, result),
-            [VMEM] * 7,
+            [VMEM] * 4,
             out_specs=(any_spec, any_spec),
             scratch_shapes=[
                 pltpu.VMEM((share, node_dev, state), F32),
                 pltpu.SemaphoreType.DMA((PIECES + 1,)),
             ],
-        )(sibling, near, far, node, their_near, their_own, their_arrived)
+        )(sibling, node, base, their_arrived)
 
 
 def solution(mesh):

time: 41.8 us -> 41.7 us (level)
  waiting for transfers between devices: 11.8 us -> 8.27 us
  starting transfers between devices: 15 us -> 17.6 us
  Pallas kernels: 10.3 us -> 11.2 us
    ppermute x1, starting transfers between devices: 0.07 us -> 3.34 us  [shards_folded(): their_own = lax.ppermute(far_own, SPLIT, to_partner)]
    all_to_all x1, waiting for transfers between devices: 10.9 us -> 7.67 us  [shards_folded(): got = lax.all_to_all(blocks, ORDER, split_axis=0, concat_axis=0, tiled=True)]
    pallas_call x1, Pallas kernels: 1.59 us -> 2.26 us  [shards_folded(): call(far_leaf_kernel, (rows, codes), [SMEM, any_spec, any_spec], **leaf)]
    ppermute x1, starting transfers between devices: 1.92 us -> 1.25 us  [shards_folded(): near_code = lax.ppermute(far_code, 'blk', across)]
    pallas_call x2 -> x3, Pallas kernels: 2.49 us -> 2.67 us  [the longest x1 1.52 us: shards_folded(): call(merge_folded, (result, result), [VMEM] * 4, out_specs=(any_spec, any...]
  transfers between devices with their start and end apart: 6 -> 6, of which waited for: 3 -> 2; matrix products, arithmetic and copies ran while one was open for 0% -> 0% of each run, Pallas kernels for 15% -> 17%
where the time goes in v9:
time: 41.7 us; the launch traced here: 41.4 us
  starting transfers between devices  17.6 us (42%)
  Pallas kernels  11.2 us (27%)
  waiting for transfers between devices  8.27 us (20%)
  local copies, waits for them, and re-layouts  3.6 us (9%)
  between operations  0.76 us (2%)
    all_to_all x1, waiting for transfers between devices, shards_folded(): got = lax.all_to_all(blocks, ORDER, split_axis=0, concat_axis=0, tiled=True)  7.67 us
    all_to_all x1, starting transfers between devices, shards_folded(): got = lax.all_to_all(blocks, ORDER, split_axis=0, concat_axis=0, tiled=True)  6.36 us
    unnamed x11, local copies, waits for them, and re-layouts  3.6 us
    ppermute x1, starting transfers between devices, shards_folded(): their_own = lax.ppermute(far_own, SPLIT, to_partner)  3.34 us
    ppermute x1, starting transfers between devices, shards_folded(): their_arrived = lax.ppermute(arrived, SPLIT, to_partner)  3.29 us
    pallas_call x1, Pallas kernels, bucket(): call(functools.partial(bucket_kernel, plan), jax.ShapeDtypeStruct((plan.l...  2.47 us
    pallas_call x1, Pallas kernels, shards_folded(): call(far_leaf_kernel, (rows, codes), [SMEM, any_spec, any_spec], **leaf)  2.26 us
    pallas_call x1, Pallas kernels, shards_folded(): call(near_leaf_kernel, (rows, rows, rows), [SMEM, any_spec, any_spec, VME...  2.21 us
  transfers between devices with their start and end apart: 6, of which 2 were waited for; matrix products, arithmetic and copies ran while one was open for 0% of the time, Pallas kernels for 17%

profile of v9, /device:TPU:9, one launch (start us, length us, event | category | flops | bytes accessed | tf_op | source)
XLA Modules:
  0.0 41.4 jit_solution(2278937747405283367)
XLA Ops:
  0.6 0.0 copy-start.4
  0.6 2.5 %bucket.1 = bf16[32,104,128]{2,1,0:T(8,128)(2,1)} custom-call(s32[1,512]{1,0:T(1,128)} %bitcast.5, bf16[512]{0:T(512)(128)(2,1)} %weight_hbm.5, bf16[512,512]{1,0:T(8,128)(2,1)} %rows_hbm.5), custom_call_target="tpu_custom_call" | custom-call | flops 402653184 | bytes 1048576 | tf_op jit(solution)/shard_map/bucket/pallas_call | solution.py:532
  3.1 6.4 %all-to-all-start = ((bf16[32,104,128]{2,1,0:T(8,128)(2,1)}), bf16[32,104,128]{2,1,0:T(8,128)(2,1)S(1)}, u32[]{:S(2)}, u32[]{:S(2)}) async-start(bf16[32,104,128]{2,1,0:T(8,128)(2,1)} %bucket.1), calls=%async_computation | async-start | bytes 1703936 | tf_op jit(solution)/shard_map/all_to_all | solution.py:601
  9.5 0.0 copy-start
  9.5 2.2 %copy-done = bf16[2,8,256,512]{3,2,1,0:T(8,128)(2,1)S(1)} copy-done((bf16[2,8,256,512]{3,2,1,0:T(8,128)(2,1)S(1)}, bf16[2,8,256,512]{3,2,1,0:T(8,128)(2,1)}, u32[]{:S(2)}) %copy-start) | copy-done | bytes 4194328
  11.7 0.0 copy-start.1
  11.7 0.7 %copy-done.1 = bf16[2,8,256]{2,1,0:T(8,128)(2,1)S(1)} copy-done((bf16[2,8,256]{2,1,0:T(8,128)(2,1)S(1)}, bf16[2,8,256]{2,1,0:T(8,128)(2,1)}, u32[]{:S(2)}) %copy-start.1) | copy-done | bytes 8216
  12.4 0.0 copy-start.2
  12.4 0.7 %copy-done.2 = s32[2]{0:T(128)S(1)} copy-done((s32[2]{0:T(128)S(1)}, s32[2]{0:T(128)}, u32[]{:S(2)}) %copy-start.2) | copy-done | bytes 32
  13.0 2.3 %far_leaf_products.1 = (f32[256,512]{1,0:T(8,128)S(1)}, s16[784,128]{1,0:T(8,128)(2,1)S(1)}) custom-call(s32[2]{0:T(128)S(1)} %copy-done.2, bf16[2,8,256]{2,1,0:T(8,128)(2,1)S(1)} %copy-done.1, bf16[2,8,256,512]{3,2,1,0:T(8,128)(2,1)S(1)} %copy-done), custom_call_target="tpu_custom_call" | custom-call | flops 1 | bytes 1 | tf_op jit(solution)/shard_map/far_leaf_products/pallas_call | solution.py:616
  15.3 1.2 %collective-permute-start = (s16[784,128]{1,0:T(8,128)(2,1)S(1)}, s16[784,128]{1,0:T(8,128)(2,1)S(1)}, u32[]{:S(2)}, u32[]{:S(2)}) collective-permute-start(s16[784,128]{1,0:T(8,128)(2,1)S(1)} %get-tuple-element.15), channel_id=1, source_target_pairs={{0,1},{1,0},{2,3},{3,2},{4,5},{5,4},{6,7},{7,6},{8,9},{9,8},{10,11... | collective-permute-start | bytes 602120 | tf_op jit(solution)/shard_map/ppermute | solution.py:619
  16.6 0.0 copy-done.4
  16.6 0.1 copy.12
  16.6 2.2 %near_leaf_products.1 = (f32[256,512]{1,0:T(8,128)S(1)}, f32[256,512]{1,0:T(8,128)S(1)}, f32[256,512]{1,0:T(8,128)S(1)}) custom-call(s32[2]{0:T(128)S(1)} %copy-done.2, bf16[2,8,256]{2,1,0:T(8,128)(2,1)S(1)} %copy-done.1, bf16[2,8,256,512]{3,2,1,0:T(8,128)(2,1)S(1)} %copy-done, bf16[2,256,512]{2,1,0:T(8,128)(2,1)S(1)} %bitcast.4, ...), custom_call_target="tpu_custom_call" | custom-call | flops 1 | bytes 1 | tf_op jit(solution)/shard_map/near_leaf_products/pallas_call | solution.py:621
  18.8 3.3 %collective-permute-start.3 = (f32[256,512]{1,0:T(8,128)S(1)}, f32[256,512]{1,0:T(8,128)S(1)}, u32[]{:S(2)}, u32[]{:S(2)}) collective-permute-start(f32[256,512]{1,0:T(8,128)S(1)} %get-tuple-element.16.own_ref), channel_id=1, source_target_pairs={{0,2},{2,0},{4,6},{6,4},{8,10},{10,8},{12,14},{14,12},{16,18},{18,... | collective-permute-start | bytes 1572872 | tf_op jit(solution)/shard_map/ppermute | solution.py:624
  22.2 7.7 %all-to-all-done.got_ref = bf16[32,104,128]{2,1,0:T(8,128)(2,1)S(1)} async-done(((bf16[32,104,128]{2,1,0:T(8,128)(2,1)}), bf16[32,104,128]{2,1,0:T(8,128)(2,1)S(1)}, u32[]{:S(2)}, u32[]{:S(2)}) %all-to-all-start) | async-done | bytes 852000 | tf_op jit(solution)/shard_map/all_to_all | solution.py:601
  29.8 0.9 %routed_send.1 = (s16[784,128]{1,0:T(8,128)(2,1)S(1)}, bf16[768,512]{1,0:T(8,128)(2,1)S(1)}) custom-call(bf16[32,104,128]{2,1,0:T(8,128)(2,1)S(1)} %all-to-all-done.got_ref, f32[256,512]{1,0:T(8,128)S(1)} %get-tuple-element.13.part_ref), custom_call_target="tpu_custom_call" | custom-call | flops 201326592 | bytes 1048576 | tf_op jit(solution)/shard_map/routed_send/pallas_call | solution.py:627
  30.7 1.6 %collective-permute-start.1 = (s16[784,128]{1,0:T(8,128)(2,1)S(1)}, s16[784,128]{1,0:T(8,128)(2,1)S(1)}, u32[]{:S(2)}, u32[]{:S(2)}) collective-permute-start(s16[784,128]{1,0:T(8,128)(2,1)S(1)} %get-tuple-element.17), channel_id=1, source_target_pairs={{0,1},{1,0},{2,3},{3,2},{4,5},{5,4},{6,7},{7,6},{8,9},{9,8},{10,11... | collective-permute-start | bytes 602120 | tf_op jit(solution)/shard_map/ppermute | solution.py:634
  32.3 0.0 collective-permute-done.code_ref
  32.3 0.7 %near_node.1.near_ref = f32[256,512]{1,0:T(8,128)S(1)} custom-call(f32[256,512]{1,0:T(8,128)S(1)} %get-tuple-element.12.own_ref, bf16[32,104,128]{2,1,0:T(8,128)(2,1)S(1)} %all-to-all-done.got_ref, bf16[768,512]{1,0:T(8,128)(2,1)S(1)} %get-tuple-element.14.plain_ref, s16[784,128]{1,0:T(8,128)(2,1)S(1)} %collective-permute-done.code_ref), custom_call_target="tpu_custom_call" | custom-call | flops 20000000000 | bytes 1048576 | tf_op jit(solution)/shard_map/near_node/pallas_call | solution.py:636
  33.0 0.0 copy-start.3
  33.0 1.8 %collective-permute-start.2 = (f32[256,512]{1,0:T(8,128)S(1)}, f32[256,512]{1,0:T(8,128)S(1)}, u32[]{:S(2)}, u32[]{:S(2)}) collective-permute-start(f32[256,512]{1,0:T(8,128)S(1)} %near_node.1.near_ref), channel_id=1, source_target_pairs={{0,2},{2,0},{4,6},{6,4},{8,10},{10,8},{12,14},{14,12},{16,18},{18,... | collective-permute-start | bytes 1572872 | tf_op jit(solution)/shard_map/ppermute | solution.py:643
  34.8 0.6 %collective-permute-done.1.code_ref = s16[784,128]{1,0:T(8,128)(2,1)S(1)} collective-permute-done((s16[784,128]{1,0:T(8,128)(2,1)S(1)}, s16[784,128]{1,0:T(8,128)(2,1)S(1)}, u32[]{:S(2)}, u32[]{:S(2)}) %collective-permute-start.1) | collective-permute-done | bytes 200736 | tf_op jit(solution)/shard_map/ppermute | solution.py:634
  35.4 3.3 %collective-permute-start.4 = (s16[784,128]{1,0:T(8,128)(2,1)S(1)}, s16[784,128]{1,0:T(8,128)(2,1)S(1)}, u32[]{:S(2)}, u32[]{:S(2)}) collective-permute-start(s16[784,128]{1,0:T(8,128)(2,1)S(1)} %collective-permute-done.1.code_ref), channel_id=1, source_target_pairs={{0,2},{2,0},{4,6},{6,4},{8,10},{10,8},{12,14},{14,12},{16,18},{18,... | collective-permute-start | bytes 602120 | tf_op jit(solution)/shard_map/ppermute | solution.py:644
  38.7 0.8 %far_node.1 = (f32[256,512]{1,0:T(8,128)S(1)}, f32[256,2,512]{2,1,0:T(2,128)S(1)}) custom-call(f32[256,512]{1,0:T(8,128)S(1)} %near_node.1.near_ref, f32[256,512]{1,0:T(8,128)S(1)} %get-tuple-element.16.own_ref, s16[784,128]{1,0:T(8,128)(2,1)S(1)} %collective-permute-done.1.code_ref), custom_call_target="tpu_custom_call" | custom-call | flops 20000000000 | bytes 1048576 | tf_op jit(solution)/shard_map/far_node/pallas_call | solution.py:646
  39.5 0.0 collective-permute-done.3.their_own_ref
  39.5 0.0 collective-permute-done.2.their_near_ref
  39.5 0.0 copy-done.3
  39.5 0.3 merge_base.1.base_ref
  39.9 0.0 collective-permute-done.4.code_ref
  39.9 1.5 %merge.1 = (f32[256,2,512]{2,1,0:T(2,128)}, f32[256,2,512]{2,1,0:T(2,128)}) custom-call(s32[1,2]{1,0:T(1,128)S(1)} %copy-done.3, f32[256,2,512]{2,1,0:T(2,128)S(1)} %get-tuple-element.18.node_ref, f32[2,256,512]{2,1,0:T(8,128)S(1)} %merge_base.1.base_ref, s16[784,128]{1,0:T(8,128)(2,1)S(1)} %collective-permute-done.4.code_ref), custom_call_target="tpu_custom_call" | custom-call | bytes 1048576 | tf_op jit(solution)/shard_map/merge/pallas_call | solution.py:652
Async XLA Ops:
  0.6 15.9 %copy-start.4 = (bf16[256,2,512]{2,1,0:T(2,128)(2,1)S(1)}, bf16[256,2,512]{2,1,0:T(2,128)(2,1)}, u32[]{:S(2)}) copy-start(bf16[256,2,512]{2,1,0:T(2,128)(2,1)} %param.12) | copy-start | bytes 1572868
  3.1 26.7 %all-to-all-start = ((bf16[32,104,128]{2,1,0:T(8,128)(2,1)}), bf16[32,104,128]{2,1,0:T(8,128)(2,1)S(1)}, u32[]{:S(2)}, u32[]{:S(2)}) async-start(bf16[32,104,128]{2,1,0:T(8,128)(2,1)} %bucket.1), calls=%async_computation | async-start | bytes 1703936 | tf_op jit(solution)/shard_map/all_to_all | solution.py:601
  9.5 2.2 %copy-start = (bf16[2,8,256,512]{3,2,1,0:T(8,128)(2,1)S(1)}, bf16[2,8,256,512]{3,2,1,0:T(8,128)(2,1)}, u32[]{:S(2)}) copy-start(bf16[2,8,256,512]{3,2,1,0:T(8,128)(2,1)} %rows_hbm.4) | copy-start | bytes 12582916
  11.7 0.7 %copy-start.1 = (bf16[2,8,256]{2,1,0:T(8,128)(2,1)S(1)}, bf16[2,8,256]{2,1,0:T(8,128)(2,1)}, u32[]{:S(2)}) copy-start(bf16[2,8,256]{2,1,0:T(8,128)(2,1)} %weight_hbm.4) | copy-start | bytes 24580
  12.4 0.7 %copy-start.2 = (s32[2]{0:T(128)S(1)}, s32[2]{0:T(128)}, u32[]{:S(2)}) copy-start(s32[2]{0:T(128)} %branching_ref.3) | copy-start | bytes 28
  15.3 17.0 %collective-permute-start = (s16[784,128]{1,0:T(8,128)(2,1)S(1)}, s16[784,128]{1,0:T(8,128)(2,1)S(1)}, u32[]{:S(2)}, u32[]{:S(2)}) collective-permute-start(s16[784,128]{1,0:T(8,128)(2,1)S(1)} %get-tuple-element.15), channel_id=1, source_target_pairs={{0,1},{1,0},{2,3},{3,2},{4,5},{5,4},{6,7},{7,6},{8,9},{9,8},{10,11... | collective-permute-start | bytes 602120 | tf_op jit(solution)/shard_map/ppermute | solution.py:619
  18.8 20.7 %collective-permute-start.3 = (f32[256,512]{1,0:T(8,128)S(1)}, f32[256,512]{1,0:T(8,128)S(1)}, u32[]{:S(2)}, u32[]{:S(2)}) collective-permute-start(f32[256,512]{1,0:T(8,128)S(1)} %get-tuple-element.16.own_ref), channel_id=1, source_target_pairs={{0,2},{2,0},{4,6},{6,4},{8,10},{10,8},{12,14},{14,12},{16,18},{18,... | collective-permute-start | bytes 1572872 | tf_op jit(solution)/shard_map/ppermute | solution.py:624
  30.7 4.7 %collective-permute-start.1 = (s16[784,128]{1,0:T(8,128)(2,1)S(1)}, s16[784,128]{1,0:T(8,128)(2,1)S(1)}, u32[]{:S(2)}, u32[]{:S(2)}) collective-permute-start(s16[784,128]{1,0:T(8,128)(2,1)S(1)} %get-tuple-element.17), channel_id=1, source_target_pairs={{0,1},{1,0},{2,3},{3,2},{4,5},{5,4},{6,7},{7,6},{8,9},{9,8},{10,11... | collective-permute-start | bytes 602120 | tf_op jit(solution)/shard_map/ppermute | solution.py:634
  33.0 6.5 %copy-start.3 = (s32[1,2]{1,0:T(1,128)S(1)}, s32[1,2]{1,0:T(1,128)}, u32[]{:S(2)}) copy-start(s32[1,2]{1,0:T(1,128)} %sibling_ref.3) | copy-start | bytes 28
  33.0 6.5 %collective-permute-start.2 = (f32[256,512]{1,0:T(8,128)S(1)}, f32[256,512]{1,0:T(8,128)S(1)}, u32[]{:S(2)}, u32[]{:S(2)}) collective-permute-start(f32[256,512]{1,0:T(8,128)S(1)} %near_node.1.near_ref), channel_id=1, source_target_pairs={{0,2},{2,0},{4,6},{6,4},{8,10},{10,8},{12,14},{14,12},{16,18},{18,... | collective-permute-start | bytes 1572872 | tf_op jit(solution)/shard_map/ppermute | solution.py:643
  35.4 4.5 %collective-permute-start.4 = (s16[784,128]{1,0:T(8,128)(2,1)S(1)}, s16[784,128]{1,0:T(8,128)(2,1)S(1)}, u32[]{:S(2)}, u32[]{:S(2)}) collective-permute-start(s16[784,128]{1,0:T(8,128)(2,1)S(1)} %collective-permute-done.1.code_ref), channel_id=1, source_target_pairs={{0,2},{2,0},{4,6},{6,4},{8,10},{10,8},{12,14},{14,12},{16,18},{18,... | collective-permute-start | bytes 602120 | tf_op jit(solution)/shard_map/ppermute | solution.py:644

commit v10 on v9

--- a/solution.py
+++ b/solution.py
@@ -14,6 +14,7 @@
 GROUP = 16
 EXTRA = 8
 PIECES = 4
+LEAVES = 8
 VMEM = pl.BlockSpec(memory_space=pltpu.VMEM)
 SMEM = pl.BlockSpec(memory_space=pltpu.SMEM)
 CODE = 32000.0
@@ -249,7 +250,7 @@
     for k, piece in enumerate(pieces):
         code_ref[(k + 1) * half : (k + 2) * half, :] = to_code(piece * factor)
     corner = jnp.sum(jnp.where(column == row, jnp.round(lower), 0.0), axis=0, keepdims=True)
-    line = lax.broadcasted_iota(I32, (GROUP, half), 0)
+    line = lax.broadcasted_iota(I32, (EXTRA, half), 0)
     code_ref[6 * half :, :] = to_code(
         jnp.where(line == 0, as_line(power), jnp.where(line == 1, corner, 0.0))
     )
@@ -415,12 +416,12 @@
 def merge_folded(sibling_ref, node_ref, base_ref, code_ref, node_hbm, out_hbm, out_ref, sems):
     _, share, state = base_ref.shape
     half = share // 2
-    each = share // PIECES
-    copies = [pltpu.make_async_copy(node_ref, node_hbm, sems.at[PIECES])]
+    each = share // LEAVES
+    copies = [pltpu.make_async_copy(node_ref, node_hbm, sems.at[LEAVES])]
     copies[0].start()
     zero = first_awaits(sibling_ref, each)
     terms = in_columns(lax.axis_index("blk"), *decode_node(code_ref))
-    for p in range(PIECES):
+    for p in range(LEAVES):
         rows = slice(p * each, (p + 1) * each)
         inner = slice(p * each % half, p * each % half + each)
         for k in range(state // half):
@@ -594,7 +595,7 @@
     to_partner = [(i, i ^ 1) for i in range(leaf_count)]
     result = shape((share, node_dev, state), F32)
     rows = shape((share, state), F32)
-    codes = shape((6 * half + GROUP, half), jnp.int16)
+    codes = shape((6 * half + EXTRA, half), jnp.int16)
     gathered = shape((nodes * plan.rows, state), BF16)
 
     blocks = bucket(plan, na_route, na_weight, na_rows)
@@ -656,7 +657,7 @@
             out_specs=(any_spec, any_spec),
             scratch_shapes=[
                 pltpu.VMEM((share, node_dev, state), F32),
-                pltpu.SemaphoreType.DMA((PIECES + 1,)),
+                pltpu.SemaphoreType.DMA((LEAVES + 1,)),
             ],
         )(sibling, node, base, their_arrived)
 

time: 41.7 us -> 41.7 us (level)
  waiting for transfers between devices: 8.27 us -> 10.9 us
  Pallas kernels: 11.2 us -> 9.83 us
  starting transfers between devices: 17.6 us -> 16.3 us
    all_to_all x1, waiting for transfers between devices: 7.67 us -> 10.3 us  [shards_folded(): got = lax.all_to_all(blocks, ORDER, split_axis=0, concat_axis=0, tiled=True)]
    ppermute x1, starting transfers between devices: 3.34 us -> 2.04 us  [shards_folded(): their_own = lax.ppermute(far_own, SPLIT, to_partner)]
    pallas_call x1, Pallas kernels: 2.21 us -> 1.54 us  [shards_folded(): call(near_leaf_kernel, (rows, rows, rows), [SMEM, any_spec, any_spec, VME...]
    pallas_call x1, Pallas kernels: 2.26 us -> 1.59 us  [shards_folded(): call(far_leaf_kernel, (rows, codes), [SMEM, any_spec, any_spec], **leaf)]
  transfers between devices with their start and end apart: 6 -> 6, of which waited for: 2 -> 2; matrix products, arithmetic and copies ran while one was open for 0% -> 0% of each run, Pallas kernels for 17% -> 14%
where the time goes in v10:
time: 41.7 us; the launch traced here: 41.4 us
  starting transfers between devices  16.3 us (39%)
  waiting for transfers between devices  10.9 us (26%)
  Pallas kernels  9.83 us (24%)
  local copies, waits for them, and re-layouts  3.6 us (9%)
  between operations  0.76 us (2%)
    all_to_all x1, waiting for transfers between devices, shards_folded(): got = lax.all_to_all(blocks, ORDER, split_axis=0, concat_axis=0, tiled=True)  10.3 us
    all_to_all x1, starting transfers between devices, shards_folded(): got = lax.all_to_all(blocks, ORDER, split_axis=0, concat_axis=0, tiled=True)  6.36 us
    unnamed x11, local copies, waits for them, and re-layouts  3.6 us
    ppermute x1, starting transfers between devices, shards_folded(): their_arrived = lax.ppermute(arrived, SPLIT, to_partner)  3.29 us
    pallas_call x1, Pallas kernels, bucket(): call(functools.partial(bucket_kernel, plan), jax.ShapeDtypeStruct((plan.l...  2.47 us
    ppermute x1, starting transfers between devices, shards_folded(): their_own = lax.ppermute(far_own, SPLIT, to_partner)  2.04 us
    ppermute x1, starting transfers between devices, shards_folded(): their_near = lax.ppermute(near, SPLIT, to_partner)  1.79 us
    pallas_call x1, Pallas kernels, shards_folded(): call(far_leaf_kernel, (rows, codes), [SMEM, any_spec, any_spec], **leaf)  1.59 us
  transfers between devices with their start and end apart: 6, of which 2 were waited for; matrix products, arithmetic and copies ran while one was open for 0% of the time, Pallas kernels for 14%

profile of v10, /device:TPU:9, one launch (start us, length us, event | category | flops | bytes accessed | tf_op | source)
XLA Modules:
  0.0 41.4 jit_solution(11717492579173507274)
XLA Ops:
  0.6 0.0 copy-start.4
  0.6 2.5 %bucket.1 = bf16[32,104,128]{2,1,0:T(8,128)(2,1)} custom-call(s32[1,512]{1,0:T(1,128)} %bitcast.5, bf16[512]{0:T(512)(128)(2,1)} %weight_hbm.5, bf16[512,512]{1,0:T(8,128)(2,1)} %rows_hbm.5), custom_call_target="tpu_custom_call" | custom-call | flops 402653184 | bytes 1048576 | tf_op jit(solution)/shard_map/bucket/pallas_call | solution.py:533
  3.1 6.4 %all-to-all-start = ((bf16[32,104,128]{2,1,0:T(8,128)(2,1)}), bf16[32,104,128]{2,1,0:T(8,128)(2,1)S(1)}, u32[]{:S(2)}, u32[]{:S(2)}) async-start(bf16[32,104,128]{2,1,0:T(8,128)(2,1)} %bucket.1), calls=%async_computation | async-start | bytes 1703936 | tf_op jit(solution)/shard_map/all_to_all | solution.py:602
  9.5 0.0 copy-start
  9.5 2.2 %copy-done = bf16[2,8,256,512]{3,2,1,0:T(8,128)(2,1)S(1)} copy-done((bf16[2,8,256,512]{3,2,1,0:T(8,128)(2,1)S(1)}, bf16[2,8,256,512]{3,2,1,0:T(8,128)(2,1)}, u32[]{:S(2)}) %copy-start) | copy-done | bytes 4194328
  11.7 0.0 copy-start.1
  11.7 0.7 %copy-done.1 = bf16[2,8,256]{2,1,0:T(8,128)(2,1)S(1)} copy-done((bf16[2,8,256]{2,1,0:T(8,128)(2,1)S(1)}, bf16[2,8,256]{2,1,0:T(8,128)(2,1)}, u32[]{:S(2)}) %copy-start.1) | copy-done | bytes 8216
  12.4 0.0 copy-start.2
  12.4 0.7 %copy-done.2 = s32[2]{0:T(128)S(1)} copy-done((s32[2]{0:T(128)S(1)}, s32[2]{0:T(128)}, u32[]{:S(2)}) %copy-start.2) | copy-done | bytes 32
  13.0 1.6 %far_leaf_products.1 = (f32[256,512]{1,0:T(8,128)S(1)}, s16[776,128]{1,0:T(8,128)(2,1)S(1)}) custom-call(s32[2]{0:T(128)S(1)} %copy-done.2, bf16[2,8,256]{2,1,0:T(8,128)(2,1)S(1)} %copy-done.1, bf16[2,8,256,512]{3,2,1,0:T(8,128)(2,1)S(1)} %copy-done), custom_call_target="tpu_custom_call" | custom-call | flops 1 | bytes 1 | tf_op jit(solution)/shard_map/far_leaf_products/pallas_call | solution.py:617
  14.6 1.2 %collective-permute-start = (s16[776,128]{1,0:T(8,128)(2,1)S(1)}, s16[776,128]{1,0:T(8,128)(2,1)S(1)}, u32[]{:S(2)}, u32[]{:S(2)}) collective-permute-start(s16[776,128]{1,0:T(8,128)(2,1)S(1)} %get-tuple-element.15), channel_id=1, source_target_pairs={{0,1},{1,0},{2,3},{3,2},{4,5},{5,4},{6,7},{7,6},{8,9},{9,8},{10,11... | collective-permute-start | bytes 595976 | tf_op jit(solution)/shard_map/ppermute | solution.py:620
  15.9 0.0 copy-done.4
  15.9 0.1 copy.12
  15.9 1.5 %near_leaf_products.1 = (f32[256,512]{1,0:T(8,128)S(1)}, f32[256,512]{1,0:T(8,128)S(1)}, f32[256,512]{1,0:T(8,128)S(1)}) custom-call(s32[2]{0:T(128)S(1)} %copy-done.2, bf16[2,8,256]{2,1,0:T(8,128)(2,1)S(1)} %copy-done.1, bf16[2,8,256,512]{3,2,1,0:T(8,128)(2,1)S(1)} %copy-done, bf16[2,256,512]{2,1,0:T(8,128)(2,1)S(1)} %bitcast.4, ...), custom_call_target="tpu_custom_call" | custom-call | flops 1 | bytes 1 | tf_op jit(solution)/shard_map/near_leaf_products/pallas_call | solution.py:622
  17.5 2.0 %collective-permute-start.3 = (f32[256,512]{1,0:T(8,128)S(1)}, f32[256,512]{1,0:T(8,128)S(1)}, u32[]{:S(2)}, u32[]{:S(2)}) collective-permute-start(f32[256,512]{1,0:T(8,128)S(1)} %get-tuple-element.16.own_ref), channel_id=1, source_target_pairs={{0,2},{2,0},{4,6},{6,4},{8,10},{10,8},{12,14},{14,12},{16,18},{18,... | collective-permute-start | bytes 1572872 | tf_op jit(solution)/shard_map/ppermute | solution.py:625
  19.5 10.3 %all-to-all-done.got_ref = bf16[32,104,128]{2,1,0:T(8,128)(2,1)S(1)} async-done(((bf16[32,104,128]{2,1,0:T(8,128)(2,1)}), bf16[32,104,128]{2,1,0:T(8,128)(2,1)S(1)}, u32[]{:S(2)}, u32[]{:S(2)}) %all-to-all-start) | async-done | bytes 852000 | tf_op jit(solution)/shard_map/all_to_all | solution.py:602
  29.8 0.9 %routed_send.1 = (s16[776,128]{1,0:T(8,128)(2,1)S(1)}, bf16[768,512]{1,0:T(8,128)(2,1)S(1)}) custom-call(bf16[32,104,128]{2,1,0:T(8,128)(2,1)S(1)} %all-to-all-done.got_ref, f32[256,512]{1,0:T(8,128)S(1)} %get-tuple-element.13.part_ref), custom_call_target="tpu_custom_call" | custom-call | flops 201326592 | bytes 1048576 | tf_op jit(solution)/shard_map/routed_send/pallas_call | solution.py:628
  30.7 1.6 %collective-permute-start.1 = (s16[776,128]{1,0:T(8,128)(2,1)S(1)}, s16[776,128]{1,0:T(8,128)(2,1)S(1)}, u32[]{:S(2)}, u32[]{:S(2)}) collective-permute-start(s16[776,128]{1,0:T(8,128)(2,1)S(1)} %get-tuple-element.17), channel_id=1, source_target_pairs={{0,1},{1,0},{2,3},{3,2},{4,5},{5,4},{6,7},{7,6},{8,9},{9,8},{10,11... | collective-permute-start | bytes 595976 | tf_op jit(solution)/shard_map/ppermute | solution.py:635
  32.3 0.0 collective-permute-done.code_ref
  32.3 0.7 %near_node.1.near_ref = f32[256,512]{1,0:T(8,128)S(1)} custom-call(f32[256,512]{1,0:T(8,128)S(1)} %get-tuple-element.12.own_ref, bf16[32,104,128]{2,1,0:T(8,128)(2,1)S(1)} %all-to-all-done.got_ref, bf16[768,512]{1,0:T(8,128)(2,1)S(1)} %get-tuple-element.14.plain_ref, s16[776,128]{1,0:T(8,128)(2,1)S(1)} %collective-permute-done.code_ref), custom_call_target="tpu_custom_call" | custom-call | flops 20000000000 | bytes 1048576 | tf_op jit(solution)/shard_map/near_node/pallas_call | solution.py:637
  33.0 0.0 copy-start.3
  33.0 1.8 %collective-permute-start.2 = (f32[256,512]{1,0:T(8,128)S(1)}, f32[256,512]{1,0:T(8,128)S(1)}, u32[]{:S(2)}, u32[]{:S(2)}) collective-permute-start(f32[256,512]{1,0:T(8,128)S(1)} %near_node.1.near_ref), channel_id=1, source_target_pairs={{0,2},{2,0},{4,6},{6,4},{8,10},{10,8},{12,14},{14,12},{16,18},{18,... | collective-permute-start | bytes 1572872 | tf_op jit(solution)/shard_map/ppermute | solution.py:644
  34.8 0.6 %collective-permute-done.1.code_ref = s16[776,128]{1,0:T(8,128)(2,1)S(1)} collective-permute-done((s16[776,128]{1,0:T(8,128)(2,1)S(1)}, s16[776,128]{1,0:T(8,128)(2,1)S(1)}, u32[]{:S(2)}, u32[]{:S(2)}) %collective-permute-start.1) | collective-permute-done | bytes 198688 | tf_op jit(solution)/shard_map/ppermute | solution.py:635
  35.4 3.3 %collective-permute-start.4 = (s16[776,128]{1,0:T(8,128)(2,1)S(1)}, s16[776,128]{1,0:T(8,128)(2,1)S(1)}, u32[]{:S(2)}, u32[]{:S(2)}) collective-permute-start(s16[776,128]{1,0:T(8,128)(2,1)S(1)} %collective-permute-done.1.code_ref), channel_id=1, source_target_pairs={{0,2},{2,0},{4,6},{6,4},{8,10},{10,8},{12,14},{14,12},{16,18},{18,... | collective-permute-start | bytes 595976 | tf_op jit(solution)/shard_map/ppermute | solution.py:645
  38.7 0.8 %far_node.1 = (f32[256,512]{1,0:T(8,128)S(1)}, f32[256,2,512]{2,1,0:T(2,128)S(1)}) custom-call(f32[256,512]{1,0:T(8,128)S(1)} %near_node.1.near_ref, f32[256,512]{1,0:T(8,128)S(1)} %get-tuple-element.16.own_ref, s16[776,128]{1,0:T(8,128)(2,1)S(1)} %collective-permute-done.1.code_ref), custom_call_target="tpu_custom_call" | custom-call | flops 20000000000 | bytes 1048576 | tf_op jit(solution)/shard_map/far_node/pallas_call | solution.py:647
  39.5 0.0 collective-permute-done.3.their_own_ref
  39.5 0.0 collective-permute-done.2.their_near_ref
  39.5 0.0 copy-done.3
  39.5 0.3 merge_base.1.base_ref
  39.8 0.0 collective-permute-done.4.code_ref
  39.9 1.5 %merge.1 = (f32[256,2,512]{2,1,0:T(2,128)}, f32[256,2,512]{2,1,0:T(2,128)}) custom-call(s32[1,2]{1,0:T(1,128)S(1)} %copy-done.3, f32[256,2,512]{2,1,0:T(2,128)S(1)} %get-tuple-element.18.node_ref, f32[2,256,512]{2,1,0:T(8,128)S(1)} %merge_base.1.base_ref, s16[776,128]{1,0:T(8,128)(2,1)S(1)} %collective-permute-done.4.code_ref), custom_call_target="tpu_custom_call" | custom-call | bytes 1048576 | tf_op jit(solution)/shard_map/merge/pallas_call | solution.py:653
Async XLA Ops:
  0.6 15.3 %copy-start.4 = (bf16[256,2,512]{2,1,0:T(2,128)(2,1)S(1)}, bf16[256,2,512]{2,1,0:T(2,128)(2,1)}, u32[]{:S(2)}) copy-start(bf16[256,2,512]{2,1,0:T(2,128)(2,1)} %param.12) | copy-start | bytes 1572868
  3.1 26.7 %all-to-all-start = ((bf16[32,104,128]{2,1,0:T(8,128)(2,1)}), bf16[32,104,128]{2,1,0:T(8,128)(2,1)S(1)}, u32[]{:S(2)}, u32[]{:S(2)}) async-start(bf16[32,104,128]{2,1,0:T(8,128)(2,1)} %bucket.1), calls=%async_computation | async-start | bytes 1703936 | tf_op jit(solution)/shard_map/all_to_all | solution.py:602
  9.5 2.2 %copy-start = (bf16[2,8,256,512]{3,2,1,0:T(8,128)(2,1)S(1)}, bf16[2,8,256,512]{3,2,1,0:T(8,128)(2,1)}, u32[]{:S(2)}) copy-start(bf16[2,8,256,512]{3,2,1,0:T(8,128)(2,1)} %rows_hbm.4) | copy-start | bytes 12582916
  11.7 0.7 %copy-start.1 = (bf16[2,8,256]{2,1,0:T(8,128)(2,1)S(1)}, bf16[2,8,256]{2,1,0:T(8,128)(2,1)}, u32[]{:S(2)}) copy-start(bf16[2,8,256]{2,1,0:T(8,128)(2,1)} %weight_hbm.4) | copy-start | bytes 24580
  12.4 0.7 %copy-start.2 = (s32[2]{0:T(128)S(1)}, s32[2]{0:T(128)}, u32[]{:S(2)}) copy-start(s32[2]{0:T(128)} %branching_ref.3) | copy-start | bytes 28
  14.6 17.6 %collective-permute-start = (s16[776,128]{1,0:T(8,128)(2,1)S(1)}, s16[776,128]{1,0:T(8,128)(2,1)S(1)}, u32[]{:S(2)}, u32[]{:S(2)}) collective-permute-start(s16[776,128]{1,0:T(8,128)(2,1)S(1)} %get-tuple-element.15), channel_id=1, source_target_pairs={{0,1},{1,0},{2,3},{3,2},{4,5},{5,4},{6,7},{7,6},{8,9},{9,8},{10,11... | collective-permute-start | bytes 595976 | tf_op jit(solution)/shard_map/ppermute | solution.py:620
  17.5 22.0 %collective-permute-start.3 = (f32[256,512]{1,0:T(8,128)S(1)}, f32[256,512]{1,0:T(8,128)S(1)}, u32[]{:S(2)}, u32[]{:S(2)}) collective-permute-start(f32[256,512]{1,0:T(8,128)S(1)} %get-tuple-element.16.own_ref), channel_id=1, source_target_pairs={{0,2},{2,0},{4,6},{6,4},{8,10},{10,8},{12,14},{14,12},{16,18},{18,... | collective-permute-start | bytes 1572872 | tf_op jit(solution)/shard_map/ppermute | solution.py:625
  30.7 4.6 %collective-permute-start.1 = (s16[776,128]{1,0:T(8,128)(2,1)S(1)}, s16[776,128]{1,0:T(8,128)(2,1)S(1)}, u32[]{:S(2)}, u32[]{:S(2)}) collective-permute-start(s16[776,128]{1,0:T(8,128)(2,1)S(1)} %get-tuple-element.17), channel_id=1, source_target_pairs={{0,1},{1,0},{2,3},{3,2},{4,5},{5,4},{6,7},{7,6},{8,9},{9,8},{10,11... | collective-permute-start | bytes 595976 | tf_op jit(solution)/shard_map/ppermute | solution.py:635
  33.0 6.5 %copy-start.3 = (s32[1,2]{1,0:T(1,128)S(1)}, s32[1,2]{1,0:T(1,128)}, u32[]{:S(2)}) copy-start(s32[1,2]{1,0:T(1,128)} %sibling_ref.3) | copy-start | bytes 28
  33.0 6.5 %collective-permute-start.2 = (f32[256,512]{1,0:T(8,128)S(1)}, f32[256,512]{1,0:T(8,128)S(1)}, u32[]{:S(2)}, u32[]{:S(2)}) collective-permute-start(f32[256,512]{1,0:T(8,128)S(1)} %near_node.1.near_ref), channel_id=1, source_target_pairs={{0,2},{2,0},{4,6},{6,4},{8,10},{10,8},{12,14},{14,12},{16,18},{18,... | collective-permute-start | bytes 1572872 | tf_op jit(solution)/shard_map/ppermute | solution.py:644
  35.4 4.5 %collective-permute-start.4 = (s16[776,128]{1,0:T(8,128)(2,1)S(1)}, s16[776,128]{1,0:T(8,128)(2,1)S(1)}, u32[]{:S(2)}, u32[]{:S(2)}) collective-permute-start(s16[776,128]{1,0:T(8,128)(2,1)S(1)} %collective-permute-done.1.code_ref), channel_id=1, source_target_pairs={{0,2},{2,0},{4,6},{6,4},{8,10},{10,8},{12,14},{14,12},{16,18},{18,... | collective-permute-start | bytes 595976 | tf_op jit(solution)/shard_map/ppermute | solution.py:645
